TPU v7x, 32 devices: a whole 2x2x4 slice. The times are simulated.
32 devices in a mesh: lat: 4 (over x, core), lon: 8 (over z, y).
Axes of the slice: x: 2, y: 2, z: 4, core: 2. Of those that a mesh axis runs over, the one named last changes fastest.
Arguments:
- queries: bfloat16 [64, 128, 1280], P('lat', 'lon'), may hold values from -8 to 8
- key_field: bfloat16 [64, 128, 1280], P('lat', 'lon'), may hold values from -8 to 8
- value_field: bfloat16 [64, 128, 1280], P('lat', 'lon'), may hold values from -6 to 6
- out_grad: bfloat16 [64, 128, 1280], P('lat', 'lon'), may hold values from -6 to 6
Outputs:
- grad_query: bfloat16 [64, 128, 1280], P('lat', 'lon')
- grad_key: bfloat16 [64, 128, 1280], P('lat', 'lon')
- grad_value: bfloat16 [64, 128, 1280], P('lat', 'lon')
All inputs are finite; a program needn't handle non-finite values.
Results may differ from a plain program's by a relative error of at most 0.012.
Values may be sent and summed in bfloat16 or wider, within the bound.
No kernel may reach another device: no remote copies, remote signals or barrier semaphores. Data moves between devices by JAX's collectives and lax.ppermute only.
A program may use at most 128 MiB of HBM per device.

v0:
```python
import math

import jax
import jax.numpy as jnp
from jax import lax
from jax.sharding import PartitionSpec as P

HEADS = 10
HEAD_DIM = 128
WINDOW = 13


def padded(shard, sides, width, wrap):
    for axis, dim in sides:
        count, length = (lax.axis_size(axis), shard.shape[dim])
        up = [(i, (i + 1) % count) for i in range(count if wrap else count - 1)]
        down = [(j, i) for i, j in up]
        last = lax.slice_in_dim(shard, length - width, length, axis=dim)
        first = lax.slice_in_dim(shard, 0, width, axis=dim)
        before = lax.ppermute(last, axis, up)
        after = lax.ppermute(first, axis, down)
        shard = jnp.concatenate([before, shard, after], axis=dim)
    return shard


def window_test(query_row, query_col, key_row, key_col, total_rows, radius):
    first_row = jnp.clip(query_row - radius, 0, total_rows - WINDOW)
    inside = (key_row >= first_row) & (key_row < first_row + WINDOW)
    inside = inside & (jnp.abs(key_col - query_col) <= radius)
    return inside & (query_row >= 0) & (query_row < total_rows)


def head_slice(tensor, offset):
    return lax.dynamic_slice_in_dim(tensor, offset, HEAD_DIM, tensor.ndim - 1)


def band_starts(global_rows, row_first, total_rows, radius, ext_rows):
    window_first = jnp.clip(global_rows - radius, 0, total_rows - WINDOW)
    return jnp.clip(window_first - row_first + radius, 0, ext_rows - WINDOW)


def placement(starts, ext_rows, dtype):
    targets = starts[:, None, None] + jnp.arange(WINDOW, dtype=jnp.int32)[None, :, None]
    return (targets == jnp.arange(ext_rows, dtype=jnp.int32)[None, None, :]).astype(dtype)


def band_of(pick_rows, grid):
    gathered = jnp.einsum(
        "rwe,ecd->rwcd", pick_rows, grid, preferred_element_type=jnp.float32
    ).astype(jnp.bfloat16)
    return gathered.reshape(gathered.shape[0], WINDOW * grid.shape[1], grid.shape[2])


def fold_of(pick_rows, partial_value, width):
    partial_value = partial_value.reshape(
        partial_value.shape[0], WINDOW, width, partial_value.shape[-1]
    )
    return jnp.einsum(
        "rwe,rwcd->ecd",
        pick_rows,
        partial_value,
        precision=lax.Precision.HIGHEST,
        preferred_element_type=jnp.float32,
    )


def attend_rows(query_head, key_head, value_head, grad_head, in_window, score_scale):
    scores = (
        jnp.einsum("rqd,rkd->rqk", query_head, key_head, preferred_element_type=jnp.float32)
        * score_scale
    )
    masked = jnp.where(in_window, scores, -jnp.inf)
    row_peak = jnp.max(masked, axis=-1, keepdims=True)
    log_total = row_peak + jnp.log(jnp.sum(jnp.exp(masked - row_peak), axis=-1, keepdims=True))
    weights = jnp.exp(masked - log_total)
    low_weights = weights.astype(jnp.bfloat16)
    attended = jnp.einsum(
        "rqk,rkd->rqd", low_weights, value_head, preferred_element_type=jnp.float32
    )
    row_delta = jnp.sum(grad_head.astype(jnp.float32) * attended, axis=-1, keepdims=True)
    weight_grad = jnp.einsum(
        "rqd,rkd->rqk", grad_head, value_head, preferred_element_type=jnp.float32
    )
    low_grad = (weights * (weight_grad - row_delta)).astype(jnp.bfloat16)
    return (low_weights, low_grad, log_total, row_delta)


def shards(queries, key_field, value_field, out_grad):
    lat_rows, lon_cols, feat_width = queries.shape
    radius = WINDOW // 2
    score_scale = 1.0 / math.sqrt(HEAD_DIM)
    total_rows = lat_rows * lax.axis_size("lat")
    row_first = lax.axis_index("lat") * lat_rows
    ext_rows = lat_rows + 2 * radius
    ext_cols = lon_cols + 2 * radius
    own_count = lat_rows * lon_cols
    ext_count = ext_rows * ext_cols
    paired = jnp.concatenate([key_field, value_field], axis=-1)
    border = padded(paired, (("lat", 0), ("lon", 1)), radius, True)
    key_ext = border[:, :, :feat_width]
    value_ext = border[:, :, feat_width:]
    own_global = row_first + jnp.arange(lat_rows, dtype=jnp.int32)
    fwd_starts = band_starts(own_global, row_first, total_rows, radius, ext_rows)
    pick_fwd = placement(fwd_starts, ext_rows, jnp.bfloat16)
    fold_fwd = placement(fwd_starts, ext_rows, jnp.float32)
    key_index = jnp.arange(WINDOW * ext_cols, dtype=jnp.int32)
    key_rows = (row_first - radius + fwd_starts[:, None] + key_index[None, :] // ext_cols)[
        :, None, :
    ]
    key_cols = (key_index % ext_cols)[None, None, :]
    query_rows = own_global[:, None, None]
    query_cols = (jnp.arange(lon_cols, dtype=jnp.int32) + radius)[None, :, None]
    fwd_window = window_test(query_rows, query_cols, key_rows, key_cols, total_rows, radius)
    query_init = jnp.zeros((own_count, feat_width), jnp.bfloat16)

    def forward_head(offset):
        query_head = head_slice(queries, offset)
        grad_head = head_slice(out_grad, offset)
        key_band = band_of(pick_fwd, head_slice(key_ext, offset))
        value_band = band_of(pick_fwd, head_slice(value_ext, offset))
        low_weights, low_grad, log_total, row_delta = attend_rows(
            query_head, key_band, value_band, grad_head, fwd_window, score_scale
        )
        query_new = (
            jnp.einsum("rqk,rkd->rqd", low_grad, key_band, preferred_element_type=jnp.float32)
            * score_scale
        )
        query_new = query_new.astype(jnp.bfloat16).reshape(own_count, HEAD_DIM)
        return (query_head, grad_head, low_weights, low_grad, log_total, row_delta, query_new)

    def head_pass(head_index, running):
        query_grad, pair_part = running
        offset = head_index * HEAD_DIM
        query_head, grad_head, low_weights, low_grad, log_total, row_delta, query_new = (
            forward_head(offset)
        )
        query_grad = lax.dynamic_update_slice_in_dim(query_grad, query_new, offset, 1)
        key_part = (
            jnp.einsum("rqk,rqd->rkd", low_grad, query_head, preferred_element_type=jnp.float32)
            * score_scale
        )
        value_part = jnp.einsum(
            "rqk,rqd->rkd", low_weights, grad_head, preferred_element_type=jnp.float32
        )
        key_fold = fold_of(fold_fwd, key_part, ext_cols).reshape(ext_count, HEAD_DIM)
        value_fold = fold_of(fold_fwd, value_part, ext_cols).reshape(ext_count, HEAD_DIM)
        pair_part = lax.dynamic_update_slice_in_dim(pair_part, key_fold, offset, 1)
        pair_part = lax.dynamic_update_slice_in_dim(pair_part, value_fold, feat_width + offset, 1)
        return (query_grad, pair_part)

    part_init = jnp.zeros((ext_count, 2 * feat_width), jnp.float32)
    query_grad, pair_part = lax.fori_loop(0, HEADS, head_pass, (query_init, part_init))
    partial_value = pair_part.reshape(ext_rows, ext_cols, 2 * feat_width)
    left_rim = partial_value[:, :radius]
    right_rim = partial_value[:, radius + lon_cols :]
    middle = partial_value[:, radius : radius + lon_cols]
    arrived = padded(
        jnp.concatenate([left_rim, right_rim], axis=1).astype(jnp.bfloat16),
        (("lon", 1),),
        radius,
        True,
    ).astype(jnp.float32)
    middle = middle + jnp.pad(arrived[:, :radius], ((0, 0), (0, lon_cols - radius), (0, 0)))
    middle = middle + jnp.pad(arrived[:, 3 * radius :], ((0, 0), (lon_cols - radius, 0), (0, 0)))
    top_rim = middle[:radius]
    bottom = middle[radius + lat_rows :]
    inner_rows = middle[radius : radius + lat_rows]
    landed = padded(
        jnp.concatenate([top_rim, bottom], axis=0).astype(jnp.bfloat16),
        (("lat", 0),),
        radius,
        False,
    ).astype(jnp.float32)
    inner_rows = inner_rows + jnp.pad(landed[:radius], ((0, lat_rows - radius), (0, 0), (0, 0)))
    inner_rows = inner_rows + jnp.pad(
        landed[3 * radius :], ((lat_rows - radius, 0), (0, 0), (0, 0))
    )
    grad_key = inner_rows[:, :, :feat_width].astype(jnp.bfloat16)
    grad_value = inner_rows[:, :, feat_width:].astype(jnp.bfloat16)
    grad_query = query_grad.reshape(lat_rows, lon_cols, feat_width)
    return (grad_query, grad_key, grad_value)


def solution(mesh):
    return jax.shard_map(
        shards,
        mesh=mesh,
        in_specs=(
            P("lat", "lon", None),
            P("lat", "lon", None),
            P("lat", "lon", None),
            P("lat", "lon", None),
        ),
        out_specs=(P("lat", "lon", None), P("lat", "lon", None), P("lat", "lon", None)),
        check_vma=False,
    )
```

profile of v0, /device:TPU:1, one launch (start us, length us, event | category | flops | bytes accessed | tf_op | source)
XLA Modules:
  0.0 362.6 jit_solution(16717948868645211439)
XLA Ops:
  3.0 2.7 collective-permute-start
  5.7 10.9 %collective-permute-done = bf16[6,16,2560]{2,1,0:T(8,128)(2,1)S(1)} collective-permute-done((bf16[6,16,2560]{2,1,0:T(8,128)(2,1)S(1)}, bf16[6,16,2560]{2,1,0:T(8,128)(2,1)S(1)}, u32[]{:S(2)}, u32[]{:S(2)}) %collective-permute-start) | collective-permute-done | bytes 491552 | tf_op jit(solution)/shard_map/ppermute | solution.py:20
  17.7 5.1 %collective-permute-start.3 = (bf16[28,6,2560]{2,0,1:T(8,128)(2,1)S(1)}, bf16[28,6,2560]{2,0,1:T(8,128)(2,1)S(1)}, u32[]{:S(2)}, u32[]{:S(2)}) collective-permute-start(bf16[28,6,2560]{2,0,1:T(8,128)(2,1)S(1)} %copy.66), channel_id=1, source_target_pairs={{1,0},{2,1},{3,2},{4,3},{5,4},{6,5},{7,6},{0,7},{9,8},{10,9},{11,1... | collective-permute-start | bytes 2580488 | tf_op jit(solution)/shard_map/ppermute | solution.py:21
  23.0 39.9 %collective-permute-done.3 = bf16[28,6,2560]{2,0,1:T(8,128)(2,1)S(1)} collective-permute-done((bf16[28,6,2560]{2,0,1:T(8,128)(2,1)S(1)}, bf16[28,6,2560]{2,0,1:T(8,128)(2,1)S(1)}, u32[]{:S(2)}, u32[]{:S(2)}) %collective-permute-start.3) | collective-permute-done | bytes 860192 | tf_op jit(solution)/shard_map/ppermute | solution.py:21
  63.8 2.4 pad_maximum_fusion
  66.2 2.7 fusion.86
  69.0 4.1 %broadcast_in_dim.39 = f32[784,2560]{1,0:T(8,128)} broadcast(f32[]{:T(128)} %constant.126.clone.1), dimensions={} | broadcast | bytes 8028164 | tf_op jit(solution)/shard_map/broadcast_in_dim | solution.py:151
  73.1 199.1 %while.19 = (s32[]{:T(128)}, bf16[256,1280]{1,0:T(8,128)(2,1)S(1)}, f32[784,2560]{1,0:T(8,128)}, bf16[16,16,1280]{2,1,0:T(8,128)(2,1)}, bf16[28,28,1280]{2,1,0:T...) while((s32[]{:T(128)}, bf16[256,1280]{1,0:T(8,128)(2,1)S(1)}, ...), condition=%wide.region_4.5_spmd.clone.clone, body=%wide.region_0.4_spmd.clone.clone.sunk | while | flops 731517952 | bytes 48562128 | solution.py:152
  76.2 1.6 fusion.136
  78.0 1.5 fusion.137
  81.5 1.7 fusion.140
  84.2 2.1 convolution_bitcast_fusion.5
  89.0 2.1 convolution_bitcast_fusion.4
  96.1 1.6 fusion.136
  101.5 1.7 fusion.140
  104.2 2.1 convolution_bitcast_fusion.5
  109.0 2.1 convolution_bitcast_fusion.4
  116.0 1.6 fusion.136
  117.8 1.5 fusion.137
  121.3 1.7 fusion.140
  124.0 2.1 convolution_bitcast_fusion.5
  128.8 2.1 convolution_bitcast_fusion.4
  135.9 1.6 fusion.136
  141.3 1.7 fusion.140
  144.0 2.1 convolution_bitcast_fusion.5
  148.8 2.1 convolution_bitcast_fusion.4
  155.8 1.6 fusion.136
  161.2 1.7 fusion.140
  163.9 2.1 convolution_bitcast_fusion.5
  168.7 2.1 convolution_bitcast_fusion.4
  175.7 1.6 fusion.136
  181.0 1.7 fusion.140
  183.7 2.1 convolution_bitcast_fusion.5
  188.6 2.1 convolution_bitcast_fusion.4
  195.6 1.6 fusion.136
  200.9 1.7 fusion.140
  203.6 2.1 convolution_bitcast_fusion.5
  208.5 2.1 convolution_bitcast_fusion.4
  215.5 1.6 fusion.136
  217.3 1.5 fusion.137
  220.9 1.7 fusion.140
  223.6 2.1 convolution_bitcast_fusion.5
  228.4 2.1 convolution_bitcast_fusion.4
  235.4 1.6 fusion.136
  237.2 1.5 fusion.137
  240.8 1.7 fusion.140
  243.5 2.1 convolution_bitcast_fusion.5
  248.3 2.1 convolution_bitcast_fusion.4
  255.3 1.6 fusion.136
  257.1 1.5 fusion.137
  260.7 1.7 fusion.140
  263.4 2.1 convolution_bitcast_fusion.5
  268.2 2.1 convolution_bitcast_fusion.4
  272.2 9.6 %reshape.288 = f32[28,28,2560]{2,1,0:T(8,128)} reshape(f32[784,2560]{1,0:T(8,128)} %get-tuple-element.247) | data formatting | bytes 16056320 | tf_op jit(solution)/shard_map/reshape | solution.py:153
  281.8 4.3 %convert.16 = bf16[28,28,2560]{2,1,0:T(8,128)(2,1)S(1)} convert(f32[28,28,2560]{2,1,0:T(8,128)} %reshape.288) | non-fusion elementwise | flops 2007040 | bytes 12042240 | tf_op jit(solution)/shard_map/convert.8
  286.7 4.2 %collective-permute-start.5 = (bf16[28,6,2560]{2,0,1:T(8,128)(2,1)S(1)}, bf16[28,6,2560]{2,0,1:T(8,128)(2,1)S(1)}, u32[]{:S(2)}, u32[]{:S(2)}) collective-permute-start(bf16[28,6,2560]{2,0,1:T(8,128)(2,1)S(1)} %copy.72), channel_id=1, source_target_pairs={{1,0},{2,1},{3,2},{4,3},{5,4},{6,5},{7,6},{0,7},{9,8},{10,9},{11,1... | collective-permute-start | bytes 2580488 | tf_op jit(solution)/shard_map/ppermute | solution.py:21
  291.2 40.5 %collective-permute-done.5 = bf16[28,6,2560]{2,0,1:T(8,128)(2,1)S(1)} collective-permute-done((bf16[28,6,2560]{2,0,1:T(8,128)(2,1)S(1)}, bf16[28,6,2560]{2,0,1:T(8,128)(2,1)S(1)}, u32[]{:S(2)}, u32[]{:S(2)}) %collective-permute-start.5) | collective-permute-done | bytes 860192 | tf_op jit(solution)/shard_map/ppermute | solution.py:21
  332.9 1.9 maximum_convert_fusion.2
  334.8 4.0 %maximum_convert_fusion = f32[28,24,2560]{2,1,0:T(8,128)} fusion(bf16[28,6,2560]{2,1,0:T(8,128)(2,1)S(1)} %copy.74, bf16[28,6,2560]{2,1,0:T(8,128)(2,1)S(1)} %get-tuple-element.383, bf16[28,6,2560]{2,1,0:T(8,128)(2,1)S(1)} %get-tuple-element.384, bf16[28,6,2560]{2,1,0:T(8,128)(2,1)S(1)} %copy.73), kind=kLoop, calls=%fused_computation.62 | loop fusion | flops 13762560 | bytes 10321920 | tf_op jit(solution)/shard_map/convert_element_type | solution.py:162
  339.0 6.1 %fusion.82 = (bf16[28,16,2560]{2,1,0:T(8,128)(2,1)}, f32[28,16,2560]{2,1,0:T(8,128)S(1)}) fusion(f32[28,6,2560]{2,1,0:T(8,128)} %maximum_convert_fusion.2, f32[28,24,2560]{2,1,0:T(8,128)} %maximum_convert_fusion, pred[16]{0:T(512)(128)(4,1)S(1)} %copy-done.1, f32[28,28,2560]{2,1,0:T(8,128)S(1)} %bitcast.88), kind=kLoop, calls=%fused_computation.97 | loop fusion | flops 4587520 | bytes 17776656 | tf_op jit(solution)/shard_map/convert.4
  346.4 3.8 %collective-permute-start.6 = (bf16[6,16,2560]{2,1,0:T(8,128)(2,1)S(1)}, bf16[6,16,2560]{2,1,0:T(8,128)(2,1)S(1)}, u32[]{:S(2)}, u32[]{:S(2)}) collective-permute-start(bf16[6,16,2560]{2,1,0:T(8,128)(2,1)S(1)} %get-tuple-element.387), channel_id=1, source_target_pairs={{0,8},{8,16},{16,24},{1,9},{9,17},{17,25},{2,10},{10,18},{18,26},{... | collective-permute-start | bytes 1474568 | tf_op jit(solution)/shard_map/ppermute | solution.py:20
  350.2 1.9 collective-permute-start.7
  352.1 3.8 %collective-permute-done.6 = bf16[6,16,2560]{2,1,0:T(8,128)(2,1)S(1)} collective-permute-done((bf16[6,16,2560]{2,1,0:T(8,128)(2,1)S(1)}, bf16[6,16,2560]{2,1,0:T(8,128)(2,1)S(1)}, u32[]{:S(2)}, u32[]{:S(2)}) %collective-permute-start.6) | collective-permute-done | bytes 491552 | tf_op jit(solution)/shard_map/ppermute | solution.py:20
  355.9 4.4 %collective-permute-done.7 = bf16[6,16,2560]{2,1,0:T(8,128)(2,1)S(1)} collective-permute-done((bf16[6,16,2560]{2,1,0:T(8,128)(2,1)S(1)}, bf16[6,16,2560]{2,1,0:T(8,128)(2,1)S(1)}, u32[]{:S(2)}, u32[]{:S(2)}) %collective-permute-start.7) | collective-permute-done | bytes 491552 | tf_op jit(solution)/shard_map/ppermute | solution.py:21
  (241 shorter events, 126.5 us)
Async XLA Ops:
  3.0 13.6 %collective-permute-start = (bf16[6,16,2560]{2,1,0:T(8,128)(2,1)S(1)}, bf16[6,16,2560]{2,1,0:T(8,128)(2,1)S(1)}, u32[]{:S(2)}, u32[]{:S(2)}) collective-permute-start(bf16[6,16,2560]{2,1,0:T(8,128)(2,1)S(1)} %get-tuple-element.393), channel_id=1, source_target_pairs={{0,8},{8,16},{16,24},{24,0},{1,9},{9,17},{17,25},{25,1},{2,10},{10... | collective-permute-start | bytes 1474568 | tf_op jit(solution)/shard_map/ppermute | solution.py:20
  5.7 11.0 %collective-permute-start.1 = (bf16[6,16,2560]{2,1,0:T(8,128)(2,1)S(1)}, bf16[6,16,2560]{2,1,0:T(8,128)(2,1)S(1)}, u32[]{:S(2)}, u32[]{:S(2)}) collective-permute-start(bf16[6,16,2560]{2,1,0:T(8,128)(2,1)S(1)} %get-tuple-element.394), channel_id=1, source_target_pairs={{8,0},{16,8},{24,16},{0,24},{9,1},{17,9},{25,17},{1,25},{10,2},{18... | collective-permute-start | bytes 1474568 | tf_op jit(solution)/shard_map/ppermute | solution.py:21
  17.7 45.2 %collective-permute-start.3 = (bf16[28,6,2560]{2,0,1:T(8,128)(2,1)S(1)}, bf16[28,6,2560]{2,0,1:T(8,128)(2,1)S(1)}, u32[]{:S(2)}, u32[]{:S(2)}) collective-permute-start(bf16[28,6,2560]{2,0,1:T(8,128)(2,1)S(1)} %copy.66), channel_id=1, source_target_pairs={{1,0},{2,1},{3,2},{4,3},{5,4},{6,5},{7,6},{0,7},{9,8},{10,9},{11,1... | collective-permute-start | bytes 2580488 | tf_op jit(solution)/shard_map/ppermute | solution.py:21
  22.8 40.5 %collective-permute-start.2 = (bf16[28,6,2560]{2,0,1:T(8,128)(2,1)S(1)}, bf16[28,6,2560]{2,0,1:T(8,128)(2,1)S(1)}, u32[]{:S(2)}, u32[]{:S(2)}) collective-permute-start(bf16[28,6,2560]{2,0,1:T(8,128)(2,1)S(1)} %copy.65), channel_id=1, source_target_pairs={{0,1},{1,2},{2,3},{3,4},{4,5},{5,6},{6,7},{7,0},{8,9},{9,10},{10,1... | collective-permute-start | bytes 2580488 | tf_op jit(solution)/shard_map/ppermute | solution.py:20
  272.2 9.6 %copy-start = (bf16[256,1280]{1,0:T(8,128)(2,1)}, bf16[256,1280]{1,0:T(8,128)(2,1)S(1)}, u32[]{:S(2)}) copy-start(bf16[256,1280]{1,0:T(8,128)(2,1)S(1)} %get-tuple-element.246) | copy-start | bytes 1966084
  286.7 45.0 %collective-permute-start.5 = (bf16[28,6,2560]{2,0,1:T(8,128)(2,1)S(1)}, bf16[28,6,2560]{2,0,1:T(8,128)(2,1)S(1)}, u32[]{:S(2)}, u32[]{:S(2)}) collective-permute-start(bf16[28,6,2560]{2,0,1:T(8,128)(2,1)S(1)} %copy.72), channel_id=1, source_target_pairs={{1,0},{2,1},{3,2},{4,3},{5,4},{6,5},{7,6},{0,7},{9,8},{10,9},{11,1... | collective-permute-start | bytes 2580488 | tf_op jit(solution)/shard_map/ppermute | solution.py:21
  291.2 41.2 %collective-permute-start.4 = (bf16[28,6,2560]{2,0,1:T(8,128)(2,1)S(1)}, bf16[28,6,2560]{2,0,1:T(8,128)(2,1)S(1)}, u32[]{:S(2)}, u32[]{:S(2)}) collective-permute-start(bf16[28,6,2560]{2,0,1:T(8,128)(2,1)S(1)} %copy.71), channel_id=1, source_target_pairs={{0,1},{1,2},{2,3},{3,4},{4,5},{5,6},{6,7},{7,0},{8,9},{9,10},{10,1... | collective-permute-start | bytes 2580488 | tf_op jit(solution)/shard_map/ppermute | solution.py:20
  332.8 5.9 %slice-start = ((s8[9175040]{0:T(1024)(128)(4,1)}), s8[4194304]{0:T(1024)(128)(4,1)S(1)}, s32[]{:S(2)}) async-start(s8[9175040]{0:T(1024)(128)(4,1)} %bitcast.87), calls=%async_computation | async-start | bytes 8388608
  332.8 5.9 %slice-start.1 = ((s8[9175040]{0:T(1024)(128)(4,1)}), s8[4194304]{0:T(1024)(128)(4,1)S(1)}, s32[]{:S(2)}) async-start(s8[9175040]{0:T(1024)(128)(4,1)} %bitcast.87), calls=%async_computation.1 | async-start | bytes 8388608
  334.8 4.2 %slice-start.2 = ((s8[9175040]{0:T(1024)(128)(4,1)}), s8[786432]{0:T(1024)(128)(4,1)S(1)}, s32[]{:S(2)}) async-start(s8[9175040]{0:T(1024)(128)(4,1)} %bitcast.87), calls=%async_computation.2 | async-start | bytes 1572864
  334.8 4.2 %copy-start.1 = (pred[16]{0:T(512)(128)(4,1)S(1)}, pred[16]{0:T(512)(128)(4,1)}, u32[]{:S(2)}) copy-start(pred[16]{0:T(512)(128)(4,1)} %constant.138.clone.1) | copy-start | bytes 52
  346.4 9.6 %collective-permute-start.6 = (bf16[6,16,2560]{2,1,0:T(8,128)(2,1)S(1)}, bf16[6,16,2560]{2,1,0:T(8,128)(2,1)S(1)}, u32[]{:S(2)}, u32[]{:S(2)}) collective-permute-start(bf16[6,16,2560]{2,1,0:T(8,128)(2,1)S(1)} %get-tuple-element.387), channel_id=1, source_target_pairs={{0,8},{8,16},{16,24},{1,9},{9,17},{17,25},{2,10},{10,18},{18,26},{... | collective-permute-start | bytes 1474568 | tf_op jit(solution)/shard_map/ppermute | solution.py:20
  350.2 10.1 %collective-permute-start.7 = (bf16[6,16,2560]{2,1,0:T(8,128)(2,1)S(1)}, bf16[6,16,2560]{2,1,0:T(8,128)(2,1)S(1)}, u32[]{:S(2)}, u32[]{:S(2)}) collective-permute-start(bf16[6,16,2560]{2,1,0:T(8,128)(2,1)S(1)} %get-tuple-element.388), channel_id=1, source_target_pairs={{8,0},{16,8},{24,16},{9,1},{17,9},{25,17},{10,2},{18,10},{26,18},{... | collective-permute-start | bytes 1474568 | tf_op jit(solution)/shard_map/ppermute | solution.py:21
where the time goes:
time: 366 us; the launch traced here: 363 us
  matrix products  136 us (37%)
  waiting for transfers between devices  99.6 us (27%)
  local copies, waits for them, and re-layouts  84.6 us (23%)
  other arithmetic  22.5 us (6%)
  starting transfers between devices  17.8 us (5%)
    ppermute x4, waiting for transfers between devices, padded(): after = lax.ppermute(first, axis, down)  84.8 us
    dot_general x20, matrix products, fold_of(): jnp.einsum('rwe,rwcd->ecd', pick_rows, partial_value, precision=lax.Preci...  41.2 us
    dot_general x10, matrix products, head_pass(): jnp.einsum('rqk,rqd->rkd', low_weights, grad_head, preferred_element_type...  17.1 us
    dot_general x10, matrix products, attend_rows(): jnp.einsum('rqd,rkd->rqk', query_head, key_head, preferred_element_type=j...  15.6 us
    dot_general x10, matrix products, attend_rows(): jnp.einsum('rqk,rkd->rqd', low_weights, value_head, preferred_element_typ...  15 us
    dot_general x10, matrix products, attend_rows(): jnp.einsum('rqd,rkd->rqk', grad_head, value_head, preferred_element_type=...  15 us
    dot_general x10, matrix products, head_pass(): jnp.einsum('rqk,rqd->rkd', low_grad, query_head, preferred_element_type=j...  14.8 us
    ppermute x4, waiting for transfers between devices, padded(): before = lax.ppermute(last, axis, up)  14.8 us
  transfers between devices with their start and end apart: 8, of which 6 were waited for; matrix products, arithmetic and copies ran while one was open for 0% of the time, Pallas kernels for 0%

commit v1 on v0

v1 whole, which is shorter than its diff:
```python
import functools
import math

import jax
import jax.numpy as jnp
from jax import lax
from jax.experimental import pallas as pl
from jax.experimental.pallas import tpu as pltpu
from jax.sharding import PartitionSpec as P

HEAD_DIM = 128
WINDOW = 13
RADIUS = WINDOW // 2
CHUNKS = (10,)
LANES = 128
MASKED = -1e30
LOG2E = math.log2(math.e)
VMEM_BYTES = 40 * 1024 * 1024


def split(index, width):
    if width & (width - 1) == 0:
        whole = index >> (width.bit_length() - 1)
    else:
        whole = (index * ((1 << 12) // width + 1)) >> 12
    return whole, index - whole * width


def odd(axis):
    return lax.axis_index(axis) & 1


def slot_side(axis, slot):
    parity = odd(axis)
    return 1 - parity if slot == 0 else parity


def own_query_cell(position, rows, cols):
    edge = rows * RADIUS
    group = position >> 7
    place = position & (LANES - 1)
    side = jnp.where(group == 0, slot_side("lon", 0), slot_side("lon", 1))
    row_a, col_a = split(place, RADIUS)
    inner = cols - 2 * RADIUS
    row_b, col_b = split(place - edge + (LANES - edge) * group, inner)
    at_edge = place < edge
    row = jnp.where(at_edge, row_a, row_b)
    col = jnp.where(at_edge, side * (cols - RADIUS) + col_a, RADIUS + col_b)
    return row, col


def halo_query_cell(position, rows, cols):
    edge = rows * RADIUS
    group = position >> 7
    place = position & (LANES - 1)
    side = jnp.where(group == 0, slot_side("lon", 0), slot_side("lon", 1))
    row, col = split(place, RADIUS)
    col = jnp.where(side == 1, cols, -RADIUS) + col
    col = jnp.where(place < edge, col, 1 << 12)
    return row, col


def key_cell(position, rows, cols):
    own = rows * cols
    edge = RADIUS * cols
    row, col = split(position, cols)
    row_0 = row - rows + jnp.where(slot_side("lat", 0) == 1, rows, -RADIUS)
    row_1 = row - rows - RADIUS + jnp.where(slot_side("lat", 1) == 1, rows, -RADIUS)
    row = jnp.where(position < own, row, jnp.where(position < own + edge, row_0, row_1))
    return row, col


def bias_of(kind, rows, cols):
    total_rows = rows * lax.axis_size("lat")
    first = rows * lax.axis_index("lat")
    keys = rows * cols + 2 * RADIUS * cols
    key_row, key_col = key_cell(lax.broadcasted_iota(jnp.int32, (keys, 1), 0), rows, cols)
    query_row, query_col = kind(lax.broadcasted_iota(jnp.int32, (1, 2 * LANES), 1), rows, cols)
    start = jnp.clip(first + query_row - RADIUS, 0, total_rows - WINDOW)
    from_start = first + key_row - start
    inside = (from_start >= 0) & (from_start < WINDOW)
    inside = inside & (jnp.abs(key_col - query_col) <= RADIUS)
    return jnp.where(inside, 0.0, MASKED)


def dot(a, b, contract):
    return lax.dot_general(a, b, ((contract[:1], contract[1:]), ((), ())), preferred_element_type=jnp.float32)


def call(kernel, name, grid, ins, outs, out_shapes, scratch=(), flops=0, aliases=None):
    return pl.pallas_call(
        kernel,
        name=name,
        grid=(grid,),
        in_specs=ins,
        out_specs=outs,
        out_shape=out_shapes,
        scratch_shapes=scratch,
        input_output_aliases=aliases or {},
        compiler_params=pltpu.CompilerParams(
            dimension_semantics=("arbitrary",), vmem_limit_bytes=VMEM_BYTES
        ),
        cost_estimate=pl.CostEstimate(flops=flops, bytes_accessed=1 << 20, transcendentals=0),
    )


def heads_of(rows, first=0):
    return pl.BlockSpec((rows, HEAD_DIM), lambda i: (0, first + i))


def whole(shape):
    return pl.BlockSpec(shape, lambda i: (0,) * len(shape))


def pack_queries(queries, out_grad, rows, cols, first, count):
    own, edge = rows * cols, rows * RADIUS

    def kernel(q_ref, g_ref, qp_ref, gp_ref, send_0, send_1, order):
        @pl.when(pl.program_id(0) == 0)
        def _():
            row, col = own_query_cell(lax.broadcasted_iota(jnp.int32, (own, 1), 0), rows, cols)
            source = lax.broadcasted_iota(jnp.int32, (own, own), 1)
            order[...] = jnp.where(source == row * cols + col, 1.0, 0.0).astype(jnp.bfloat16)

        for place, (src, dst) in enumerate(((q_ref, qp_ref), (g_ref, gp_ref))):
            moved = dot(order[...], src[...], (1, 0)).astype(jnp.bfloat16)
            dst[...] = moved
            for group, send in enumerate((send_0, send_1)):
                send[place * edge : (place + 1) * edge, :] = moved[group * LANES : group * LANES + edge]

    width = count * HEAD_DIM
    shape = lambda n: jax.ShapeDtypeStruct((n, width), jnp.bfloat16)
    return call(
        kernel, "pack_queries", count,
        [heads_of(own, first)] * 2,
        [heads_of(own)] * 2 + [heads_of(2 * edge)] * 2,
        [shape(own)] * 2 + [shape(2 * edge)] * 2,
        [pltpu.VMEM((own, own), jnp.bfloat16)],
        flops=1 << 28,
    )(queries, out_grad)


def pack_keys(key_field, value_field, rows, cols):
    own, edge = rows * cols, RADIUS * cols

    def kernel(k_ref, v_ref, send_0, send_1):
        for slot, send in enumerate((send_0, send_1)):
            start = pl.multiple_of(slot_side("lat", slot) * (own - edge), 16)
            send[:edge, :] = k_ref[pl.ds(start, edge), :]
            send[edge:, :] = v_ref[pl.ds(start, edge), :]

    width = key_field.shape[1]
    block = 2 * HEAD_DIM
    spec = lambda n: pl.BlockSpec((n, block), lambda i: (0, i))
    return call(
        kernel, "pack_keys", width // block,
        [spec(own)] * 2, [spec(2 * edge)] * 2,
        [jax.ShapeDtypeStruct((2 * edge, width), jnp.bfloat16)] * 2,
        flops=1 << 28,
    )(key_field, value_field)


def padded(first, second, edge):
    gap = jnp.zeros((LANES - edge, HEAD_DIM), jnp.bfloat16)
    return jnp.concatenate([first, gap, second, gap], axis=0)


def halo_heads(ref_0, ref_1, edge, part):
    piece = slice(part * edge, (part + 1) * edge)
    return padded(ref_0[piece, :], ref_1[piece, :], edge)


def key_heads(own_ref, ref_0, ref_1, edge, part):
    piece = slice(part * edge, (part + 1) * edge)
    return jnp.concatenate([own_ref[...], ref_0[piece, :], ref_1[piece, :]], axis=0)


SCORE_SCALE = 1.0 / math.sqrt(HEAD_DIM)


def part_stats(keys, values, queries, grads, bias):
    scores = dot(keys, queries, (1, 1)) * (SCORE_SCALE * LOG2E) + bias
    peak = jnp.max(scores, axis=0, keepdims=True)
    weights = jnp.exp2(scores - peak)
    total = jnp.sum(weights, axis=0, keepdims=True)
    weight_grad = dot(values, grads, (1, 1))
    dotted = jnp.sum(weights * weight_grad, axis=0, keepdims=True)
    return peak + jnp.log(total) * LOG2E, dotted / total


def put_row(ref, lanes, row, value):
    here = lax.broadcasted_iota(jnp.int32, (ref.shape[0], 1), 0) == row
    ref[:, lanes] = jnp.where(here, value, ref[:, lanes])


def stat_rows(count):
    return -(-2 * count // 8) * 8


def own_stats(qp, gp, keys, values, lat_0, lat_1, rows, cols, first, count):
    own, edge = rows * cols, RADIUS * cols

    def kernel(q_ref, g_ref, k_ref, v_ref, lat_0, lat_1, out, bias):
        head = pl.program_id(0)

        @pl.when(head == 0)
        def _():
            bias[...] = bias_of(own_query_cell, rows, cols)
            out[...] = jnp.zeros_like(out)

        log_total, delta = part_stats(
            key_heads(k_ref, lat_0, lat_1, edge, 0), key_heads(v_ref, lat_0, lat_1, edge, 1),
            q_ref[...], g_ref[...], bias[...],
        )
        put_row(out, slice(None), head, log_total)
        put_row(out, slice(None), count + head, delta)

    shape = (stat_rows(count), own)
    return call(
        kernel, "own_stats", count,
        [heads_of(own)] * 2 + [heads_of(own, first)] * 2 + [heads_of(2 * edge, first)] * 2,
        whole(shape), jax.ShapeDtypeStruct(shape, jnp.float32),
        [pltpu.VMEM((own + 2 * edge, own), jnp.float32)],
        flops=1 << 30,
    )(qp, gp, keys, values, lat_0, lat_1)


def halo_stats(halo_0, halo_1, own_stat, keys, values, lat_0, lat_1, rows, cols, first, count):
    own, edge = rows * cols, RADIUS * cols
    lon_edge = RADIUS * rows

    def kernel(h_0, h_1, stat, k_ref, v_ref, lat_0, lat_1, out_0, out_1, bias):
        head = pl.program_id(0)

        @pl.when(head == 0)
        def _():
            bias[...] = bias_of(halo_query_cell, rows, cols)
            for group, out in enumerate((out_0, out_1)):
                out[:, :LANES] = stat[:, group * LANES : (group + 1) * LANES]
                out[:, LANES:] = jnp.zeros((out.shape[0], LANES), jnp.float32)

        log_total, delta = part_stats(
            key_heads(k_ref, lat_0, lat_1, edge, 0), key_heads(v_ref, lat_0, lat_1, edge, 1),
            halo_heads(h_0, h_1, lon_edge, 0), halo_heads(h_0, h_1, lon_edge, 1), bias[...],
        )
        for group, out in enumerate((out_0, out_1)):
            lanes = slice(group * LANES, (group + 1) * LANES)
            put_row(out, slice(LANES, None), head, log_total[:, lanes])
            put_row(out, slice(LANES, None), count + head, delta[:, lanes])

    shape = (stat_rows(count), 2 * LANES)
    return call(
        kernel, "halo_stats", count,
        [heads_of(2 * lon_edge)] * 2 + [whole(own_stat.shape)] + [heads_of(own, first)] * 2
        + [heads_of(2 * edge, first)] * 2,
        [whole(shape)] * 2, [jax.ShapeDtypeStruct(shape, jnp.float32)] * 2,
        [pltpu.VMEM((own + 2 * edge, 2 * LANES), jnp.float32)],
        flops=1 << 30,
    )(halo_0, halo_1, own_stat, keys, values, lat_0, lat_1)


def combined(mine, theirs, count):
    a, b = mine[:count], theirs[:count]
    peak = jnp.maximum(a, b)
    part_a, part_b = jnp.exp2(a - peak), jnp.exp2(b - peak)
    total = part_a + part_b
    delta = (part_a * mine[count : 2 * count] + part_b * theirs[count : 2 * count]) / total
    return peak + jnp.log(total) * LOG2E, delta


def fill_combined(mine, theirs, mine_half, log_ref, delta_ref, at, count):
    for group, (a, b) in enumerate(zip(mine, theirs)):
        low, high = slice(0, LANES), slice(LANES, 2 * LANES)
        own_half, other_half = (low, high) if mine_half == 0 else (high, low)
        log_total, delta = combined(a[:, own_half], b[:, other_half], count)
        lanes = slice(at + group * LANES, at + (group + 1) * LANES)
        log_ref[:count, lanes] = log_total
        delta_ref[:count, lanes] = delta


def gradients(keys, values, queries, grads, bias, log_total, delta):
    scores = dot(keys, queries, (1, 1)) * (SCORE_SCALE * LOG2E) + bias
    weights = jnp.exp2(scores - log_total)
    weight_grad = dot(values, grads, (1, 1))
    low_grad = (weights * (weight_grad - delta)).astype(jnp.bfloat16)
    return weights.astype(jnp.bfloat16), low_grad


def halo_query_grad(halo_0, halo_1, mine, theirs, keys, values, lat_0, lat_1, rows, cols, first, count):
    own, edge = rows * cols, RADIUS * cols
    lon_edge = RADIUS * rows

    def kernel(h_0, h_1, m_0, m_1, t_0, t_1, k_ref, v_ref, lat_0, lat_1, out_0, out_1, bias, logs, deltas):
        head = pl.program_id(0)

        @pl.when(head == 0)
        def _():
            bias[...] = bias_of(halo_query_cell, rows, cols)
            fill_combined((m_0, m_1), (t_0, t_1), 1, logs, deltas, 0, count)

        key_all = key_heads(k_ref, lat_0, lat_1, edge, 0)
        _, low_grad = gradients(
            key_all, key_heads(v_ref, lat_0, lat_1, edge, 1),
            halo_heads(h_0, h_1, lon_edge, 0), halo_heads(h_0, h_1, lon_edge, 1),
            bias[...], logs[pl.ds(head, 1), :], deltas[pl.ds(head, 1), :],
        )
        grad = (dot(low_grad, key_all, (0, 0)) * SCORE_SCALE).astype(jnp.bfloat16)
        out_0[...] = grad[:lon_edge]
        out_1[...] = grad[LANES : LANES + lon_edge]

    return call(
        kernel, "halo_query_grad", count,
        [heads_of(2 * lon_edge)] * 2 + [whole(mine[0].shape)] * 4 + [heads_of(own, first)] * 2
        + [heads_of(2 * edge, first)] * 2,
        [heads_of(lon_edge)] * 2,
        [jax.ShapeDtypeStruct((lon_edge, count * HEAD_DIM), jnp.bfloat16)] * 2,
        [pltpu.VMEM((own + 2 * edge, 2 * LANES), jnp.float32)]
        + [pltpu.VMEM((-(-count // 8) * 8, 2 * LANES), jnp.float32)] * 2,
        flops=1 << 30,
    )(halo_0, halo_1, *mine, *theirs, keys, values, lat_0, lat_1)


def own_grads(qp, gp, halo_0, halo_1, mine, theirs, keys, values, lat_0, lat_1, rows, cols, first, count):
    own, edge = rows * cols, RADIUS * cols
    lon_edge = RADIUS * rows
    every = own + 2 * LANES

    def kernel(
        q_ref, g_ref, h_0, h_1, m_0, m_1, t_0, t_1, k_ref, v_ref, lat_0, lat_1,
        dq_ref, dk_ref, dv_ref, out_0, out_1, bias, logs, deltas,
    ):
        head = pl.program_id(0)

        @pl.when(head == 0)
        def _():
            bias[:, :own] = bias_of(own_query_cell, rows, cols)
            bias[:, own:] = bias_of(halo_query_cell, rows, cols)
            fill_combined((m_0, m_1), (t_0, t_1), 0, logs, deltas, 0, count)
            fill_combined((m_0, m_1), (t_0, t_1), 1, logs, deltas, own, count)

        key_all = key_heads(k_ref, lat_0, lat_1, edge, 0)
        queries = jnp.concatenate([q_ref[...], halo_heads(h_0, h_1, lon_edge, 0)], axis=0)
        grads = jnp.concatenate([g_ref[...], halo_heads(h_0, h_1, lon_edge, 1)], axis=0)
        low_weights, low_grad = gradients(
            key_all, key_heads(v_ref, lat_0, lat_1, edge, 1), queries, grads,
            bias[...], logs[pl.ds(head, 1), :], deltas[pl.ds(head, 1), :],
        )
        dq_ref[...] = dot(low_grad[:, :own], key_all, (0, 0)) * SCORE_SCALE
        key_grad = dot(low_grad, queries, (1, 0)) * SCORE_SCALE
        value_grad = dot(low_weights, grads, (1, 0))
        dk_ref[...] = key_grad[:own]
        dv_ref[...] = value_grad[:own]
        for slot, out in enumerate((out_0, out_1)):
            piece = slice(own + slot * edge, own + (slot + 1) * edge)
            out[:edge, :] = key_grad[piece].astype(jnp.bfloat16)
            out[edge:, :] = value_grad[piece].astype(jnp.bfloat16)

    width = count * HEAD_DIM
    return call(
        kernel, "own_grads", count,
        [heads_of(own)] * 2 + [heads_of(2 * lon_edge)] * 2 + [whole(mine[0].shape)] * 4
        + [heads_of(own, first)] * 2 + [heads_of(2 * edge, first)] * 2,
        [heads_of(own)] * 3 + [heads_of(2 * edge)] * 2,
        [jax.ShapeDtypeStruct((own, width), jnp.float32)] * 3
        + [jax.ShapeDtypeStruct((2 * edge, width), jnp.bfloat16)] * 2,
        [pltpu.VMEM((own + 2 * edge, every), jnp.float32)]
        + [pltpu.VMEM((-(-count // 8) * 8, every), jnp.float32)] * 2,
        flops=1 << 31,
    )(qp, gp, halo_0, halo_1, *mine, *theirs, keys, values, lat_0, lat_1)


def finish_queries(grad, back_0, back_1, result, rows, cols, first, count, width):
    own, edge = rows * cols, rows * RADIUS

    def kernel(g_ref, b_0, b_1, *rest):
        out, order, total = rest[-3:]

        @pl.when(pl.program_id(0) == 0)
        def _():
            row, col = own_query_cell(lax.broadcasted_iota(jnp.int32, (1, own), 1), rows, cols)
            target = lax.broadcasted_iota(jnp.int32, (own, own), 0)
            order[...] = jnp.where(target == row * cols + col, 1.0, 0.0).astype(jnp.bfloat16)

        total[...] = g_ref[...].astype(jnp.bfloat16)
        for group, back in enumerate((b_0, b_1)):
            piece = slice(group * LANES, group * LANES + edge)
            total[piece, :] = (g_ref[piece, :] + back[...].astype(jnp.float32)).astype(jnp.bfloat16)
        out[...] = dot(order[...], total[...], (1, 0)).astype(jnp.bfloat16)

    extra = [] if result is None else [result]
    return call(
        kernel, "finish_queries", count,
        [heads_of(own)] + [heads_of(edge)] * 2 + [pl.BlockSpec(memory_space=pl.ANY)] * len(extra),
        heads_of(own, first),
        jax.ShapeDtypeStruct((own, width), jnp.bfloat16),
        [pltpu.VMEM((own, own), jnp.bfloat16), pltpu.VMEM((own, HEAD_DIM), jnp.bfloat16)],
        flops=1 << 28, aliases={3: 0} if extra else None,
    )(grad, back_0, back_1, *extra)


def finish_keys(key_grad, value_grad, back_0, back_1, results, rows, cols, first, count, width):
    own, edge = rows * cols, RADIUS * cols

    def kernel(dk_ref, dv_ref, b_0, b_1, *rest):
        outs = rest[-2:]
        for part, (grad, out) in enumerate(zip((dk_ref, dv_ref), outs)):
            middle = slice(edge, own - edge)
            out[middle, :] = grad[middle, :].astype(jnp.bfloat16)
            for slot, back in enumerate((b_0, b_1)):
                start = pl.multiple_of(slot_side("lat", slot) * (own - edge), 16)
                arrived = back[part * edge : (part + 1) * edge, :].astype(jnp.float32)
                out[pl.ds(start, edge), :] = (grad[pl.ds(start, edge), :] + arrived).astype(jnp.bfloat16)

    extra = [] if results is None else list(results)
    return call(
        kernel, "finish_keys", count,
        [heads_of(own)] * 2 + [heads_of(2 * edge)] * 2 + [pl.BlockSpec(memory_space=pl.ANY)] * len(extra),
        [heads_of(own, first)] * 2,
        [jax.ShapeDtypeStruct((own, width), jnp.bfloat16)] * 2,
        flops=1 << 28, aliases={4: 0, 5: 1} if extra else None,
    )(key_grad, value_grad, back_0, back_1, *extra)


def swap(axis, slot, wrap, array):
    count = lax.axis_size(axis)
    pairs = []
    for low in range(slot, count if wrap else count - 1, 2):
        high = (low + 1) % count
        pairs += [(low, high), (high, low)]
    return lax.ppermute(array, axis, pairs)


def swap_lon(arrays):
    return [swap("lon", slot, True, array) for slot, array in enumerate(arrays)]


def swap_lat(arrays):
    return [swap("lat", slot, False, array) for slot, array in enumerate(arrays)]


def shards(queries, key_field, value_field, out_grad):
    rows, cols, width = queries.shape
    own = rows * cols
    heads = width // HEAD_DIM
    flat = lambda x: x.reshape(own, width)
    queries, key_field, value_field, out_grad = map(flat, (queries, key_field, value_field, out_grad))
    starts = [sum(CHUNKS[:i]) for i in range(len(CHUNKS))]
    assert sum(CHUNKS) == heads
    size = (rows, cols)

    packs = [pack_queries(queries, out_grad, *size, f, n) for f, n in zip(starts, CHUNKS)]
    halos = [swap_lon(pack[2:]) for pack in packs]
    lat = swap_lat(pack_keys(key_field, value_field, *size))
    keyed = (key_field, value_field, *lat)
    grad_query, key_value = None, None
    for (f, n), pack, halo in zip(zip(starts, CHUNKS), packs, halos):
        qp, gp = pack[:2]
        own_stat = own_stats(qp, gp, *keyed, *size, f, n)
        mine = halo_stats(*halo, own_stat, *keyed, *size, f, n)
        theirs = swap_lon(mine)
        back = swap_lon(halo_query_grad(*halo, mine, theirs, *keyed, *size, f, n))
        dq, dk, dv, *lat_back = own_grads(qp, gp, *halo, mine, theirs, *keyed, *size, f, n)
        lat_back = swap_lat(lat_back)
        grad_query = finish_queries(dq, *back, grad_query, *size, f, n, width)
        key_value = finish_keys(dk, dv, *lat_back, key_value, *size, f, n, width)
    shape = (rows, cols, width)
    return tuple(x.reshape(shape) for x in (grad_query, *key_value))


def solution(mesh):
    spec = P("lat", "lon", None)
    return jax.shard_map(
        shards, mesh=mesh, in_specs=(spec,) * 4, out_specs=(spec,) * 3, check_vma=False
    )
```

time: 366 us -> 86 us (0.23)
  matrix products: 136 us -> 0 us
  local copies, waits for them, and re-layouts: 84.6 us -> 2.28 us
  waiting for transfers between devices: 99.6 us -> 21.1 us
  Pallas kernels: 0 us -> 39.6 us
  other arithmetic: 22.5 us -> 0 us
  starting transfers between devices: 17.8 us -> 22 us
    dot_general x100 -> x0, matrix products: 136 us -> none  [the longest x20 41.2 us: fold_of(): jnp.einsum('rwe,rwcd->ecd', pick_rows, partial_value, precision=lax.Preci...]
    ppermute x8 -> x10, waiting for transfers between devices: 99.6 us -> 21.1 us  [swap(): return lax.ppermute(array, axis, pairs)]
    pallas_call x0 -> x8, Pallas kernels: none -> 39.6 us  [the longest x1 11 us: own_grads(): call(kernel, 'own_grads', count, [heads_of(own)] * 2 + [heads_of(2 * lon_...]
    dynamic_update_slice x30 -> x0, local copies, waits for them, and re-layouts: 16.8 us -> none  [the longest x10 8.39 us: head_pass(): pair_part = lax.dynamic_update_slice_in_dim(pair_part, key_fold, offset, 1)]
    dot_general x30 -> x0, local copies, waits for them, and re-layouts: 14.4 us -> none  [the longest x10 9.61 us: head_pass(): jnp.einsum('rqk,rqd->rkd', low_weights, grad_head, preferred_element_type...]
    another operation x3 -> x0, other arithmetic: 11 us -> none
    dynamic_slice x10 -> x0, local copies, waits for them, and re-layouts: 10.9 us -> none  [head_slice(): return lax.dynamic_slice_in_dim(tensor, offset, HEAD_DIM, tensor.ndim - 1)]
    reshape x21 -> x0, local copies, waits for them, and re-layouts: 10.2 us -> none  [the longest x1 9.6 us: shards(): partial_value = pair_part.reshape(ext_rows, ext_cols, 2 * feat_width)]
  transfers between devices with their start and end apart: 8 -> 10, of which waited for: 6 -> 3; matrix products, arithmetic and copies ran while one was open for 0% -> 0% of each run, Pallas kernels for 0% -> 23%
where the time goes in v1:
time: 86 us; the launch traced here: 85.8 us
  Pallas kernels  39.6 us (46%)
  starting transfers between devices  22 us (26%)
  waiting for transfers between devices  21.1 us (25%)
  local copies, waits for them, and re-layouts  2.28 us (3%)
    ppermute x10, starting transfers between devices, swap(): return lax.ppermute(array, axis, pairs)  22 us
    ppermute x10, waiting for transfers between devices, swap(): return lax.ppermute(array, axis, pairs)  21.1 us
    pallas_call x1, Pallas kernels, own_grads(): call(kernel, 'own_grads', count, [heads_of(own)] * 2 + [heads_of(2 * lon_...  11 us
    pallas_call x1, Pallas kernels, halo_query_grad(): call(kernel, 'halo_query_grad', count, [heads_of(2 * lon_edge)] * 2 + [wh...  6.76 us
    pallas_call x1, Pallas kernels, halo_stats(): call(kernel, 'halo_stats', count, [heads_of(2 * lon_edge)] * 2 + [whole(o...  5.22 us
    pallas_call x1, Pallas kernels, own_stats(): call(kernel, 'own_stats', count, [heads_of(own)] * 2 + [heads_of(own, fir...  5.04 us
    pallas_call x1, Pallas kernels, finish_queries(): call(kernel, 'finish_queries', count, [heads_of(own)] + [heads_of(edge)]...  4.48 us
    pallas_call x1, Pallas kernels, finish_keys(): call(kernel, 'finish_keys', count, [heads_of(own)] * 2 + [heads_of(2 * ed...  3.67 us
  transfers between devices with their start and end apart: 10, of which 3 were waited for; matrix products, arithmetic and copies ran while one was open for 0% of the time, Pallas kernels for 23%

profile of v1, /device:TPU:1, one launch (start us, length us, event | category | flops | bytes accessed | tf_op | source)
XLA Modules:
  0.0 85.8 jit_solution(13002792029544723681)
XLA Ops:
  0.6 0.0 copy-start
  0.6 0.0 copy-start.1
  0.7 0.0 copy-start.2
  0.7 1.2 %copy-done.2 = bf16[16,16,1280]{2,1,0:T(8,128)(2,1)S(1)} copy-done((bf16[16,16,1280]{2,1,0:T(8,128)(2,1)S(1)}, bf16[16,16,1280]{2,1,0:T(8,128)(2,1)}, u32[]{:S(2)}) %copy-start.2) | copy-done | bytes 655384
  1.8 0.0 copy-start.4
  1.8 1.1 %copy-done.4 = bf16[16,16,1280]{2,1,0:T(8,128)(2,1)S(1)} copy-done((bf16[16,16,1280]{2,1,0:T(8,128)(2,1)S(1)}, bf16[16,16,1280]{2,1,0:T(8,128)(2,1)}, u32[]{:S(2)}) %copy-start.4) | copy-done | bytes 655384
  2.9 0.0 copy-start.3
  2.9 0.0 copy-start.5
  2.9 0.4 pack_keys.1
  3.3 0.1 collective-permute-start.2
  3.5 4.5 %collective-permute-start.3 = (bf16[192,1280]{1,0:T(8,128)(2,1)S(1)}, bf16[192,1280]{1,0:T(8,128)(2,1)S(1)}, u32[]{:S(2)}, u32[]{:S(2)}) collective-permute-start(bf16[192,1280]{1,0:T(8,128)(2,1)S(1)} %get-tuple-element.25), channel_id=1, source_target_pairs={{8,16},{16,8},{9,17},{17,9},{10,18},{18,10},{11,19},{19,11},{12,20... | collective-permute-start | bytes 1474568 | tf_op jit(solution)/shard_map/ppermute | solution.py:430
  7.9 0.0 copy-done
  7.9 0.0 copy-done.1
  7.9 3.1 %pack_queries.1 = (bf16[256,1280]{1,0:T(8,128)(2,1)S(1)}, bf16[256,1280]{1,0:T(8,128)(2,1)S(1)}, bf16[192,1280]{1,0:T(8,128)(2,1)S(1)}, bf16[192,1280]{1,0:T(8,128)(2,1)S(1)}) custom-call(bf16[256,1280]{1,0:T(8,128)(2,1)S(1)} %bitcast.7, bf16[256,1280]{1,0:T(8,128)(2,1)S(1)} %bitcast.8), custom_call_target="tpu_custom_call" | custom-call | flops 268435456 | bytes 1048576 | tf_op jit(solution)/shard_map/pack_queries/pallas_call | solution.py:133
  11.0 1.3 %collective-permute-start = (bf16[192,1280]{1,0:T(8,128)(2,1)S(1)}, bf16[192,1280]{1,0:T(8,128)(2,1)S(1)}, u32[]{:S(2)}, u32[]{:S(2)}) collective-permute-start(bf16[192,1280]{1,0:T(8,128)(2,1)S(1)} %get-tuple-element.22), channel_id=1, source_target_pairs={{0,1},{1,0},{2,3},{3,2},{4,5},{5,4},{6,7},{7,6},{8,9},{9,8},{10,11... | collective-permute-start | bytes 1474568 | tf_op jit(solution)/shard_map/ppermute | solution.py:430
  12.3 3.3 %collective-permute-start.1 = (bf16[192,1280]{1,0:T(8,128)(2,1)S(1)}, bf16[192,1280]{1,0:T(8,128)(2,1)S(1)}, u32[]{:S(2)}, u32[]{:S(2)}) collective-permute-start(bf16[192,1280]{1,0:T(8,128)(2,1)S(1)} %get-tuple-element.23), channel_id=1, source_target_pairs={{1,2},{2,1},{3,4},{4,3},{5,6},{6,5},{7,0},{0,7},{9,10},{10,9},{11,... | collective-permute-start | bytes 1474568 | tf_op jit(solution)/shard_map/ppermute | solution.py:430
  15.6 0.0 collective-permute-done.2.lat_0
  15.6 0.0 collective-permute-done.3.lat_1
  15.6 0.0 copy-done.3
  15.6 0.0 copy-done.5
  15.6 5.0 %own_stats.1.stat = f32[24,256]{1,0:T(8,128)S(1)} custom-call(bf16[256,1280]{1,0:T(8,128)(2,1)S(1)} %get-tuple-element.20.q_ref, bf16[256,1280]{1,0:T(8,128)(2,1)S(1)} %get-tuple-element.21.g_ref, bf16[256,1280]{1,0:T(8,128)(2,1)S(1)} %bitcast.10, bf16[256,1280]{1,0:T(8,128)(2,1)S(1)} %bitcast.15, bf16[192,1280]{1,0:T(8,128)(2,1)S(1)} %collective-permute-done.2.lat_0, ...), custom_call_target="tpu_custom_call" | custom-call | flops 1073741824 | bytes 1048576 | tf_op jit(solution)/shard_map/own_stats/pallas_call | solution.py:219
  20.7 11.6 %collective-permute-done.h_0 = bf16[192,1280]{1,0:T(8,128)(2,1)S(1)} collective-permute-done((bf16[192,1280]{1,0:T(8,128)(2,1)S(1)}, bf16[192,1280]{1,0:T(8,128)(2,1)S(1)}, u32[]{:S(2)}, u32[]{:S(2)}) %collective-permute-start) | collective-permute-done | bytes 491552 | tf_op jit(solution)/shard_map/ppermute | solution.py:430
  32.2 0.0 collective-permute-done.1.h_1
  32.2 5.2 %halo_stats.1 = (f32[24,256]{1,0:T(8,128)S(1)}, f32[24,256]{1,0:T(8,128)S(1)}) custom-call(bf16[192,1280]{1,0:T(8,128)(2,1)S(1)} %collective-permute-done.h_0, bf16[192,1280]{1,0:T(8,128)(2,1)S(1)} %collective-permute-done.1.h_1, f32[24,256]{1,0:T(8,128)S(1)} %own_stats.1.stat, bf16[256,1280]{1,0:T(8,128)(2,1)S(1)} %bitcast.11, ...), custom_call_target="tpu_custom_call" | custom-call | flops 1073741824 | bytes 1048576 | tf_op jit(solution)/shard_map/halo_stats/pallas_call | solution.py:252
  37.4 1.8 %collective-permute-start.4 = (f32[24,256]{1,0:T(8,128)S(1)}, f32[24,256]{1,0:T(8,128)S(1)}, u32[]{:S(2)}, u32[]{:S(2)}) collective-permute-start(f32[24,256]{1,0:T(8,128)S(1)} %get-tuple-element.26.m_0), channel_id=1, source_target_pairs={{0,1},{1,0},{2,3},{3,2},{4,5},{5,4},{6,7},{7,6},{8,9},{9,8},{10,11... | collective-permute-start | bytes 73736 | tf_op jit(solution)/shard_map/ppermute | solution.py:430
  39.2 3.3 %collective-permute-start.5 = (f32[24,256]{1,0:T(8,128)S(1)}, f32[24,256]{1,0:T(8,128)S(1)}, u32[]{:S(2)}, u32[]{:S(2)}) collective-permute-start(f32[24,256]{1,0:T(8,128)S(1)} %get-tuple-element.27.m_1), channel_id=1, source_target_pairs={{1,2},{2,1},{3,4},{4,3},{5,6},{6,5},{7,0},{0,7},{9,10},{10,9},{11,... | collective-permute-start | bytes 73736 | tf_op jit(solution)/shard_map/ppermute | solution.py:430
  42.5 0.0 collective-permute-done.4.t_0
  42.5 2.4 %collective-permute-done.5.t_1 = f32[24,256]{1,0:T(8,128)S(1)} collective-permute-done((f32[24,256]{1,0:T(8,128)S(1)}, f32[24,256]{1,0:T(8,128)S(1)}, u32[]{:S(2)}, u32[]{:S(2)}) %collective-permute-start.5) | collective-permute-done | bytes 24608 | tf_op jit(solution)/shard_map/ppermute | solution.py:430
  44.9 11.0 %own_grads.1 = (f32[256,1280]{1,0:T(8,128)S(1)}, f32[256,1280]{1,0:T(8,128)S(1)}, f32[256,1280]{1,0:T(8,128)S(1)}, bf16[192,1280]{1,0:T(8,128)(2,1)S(1)}, bf16[192,1280]{1,0:T(8,128)(2,1)S(1)}) custom-call(bf16[256,1280]{1,0:T(8,128)(2,1)S(1)} %get-tuple-element.20.q_ref, bf16[256,1280]{1,0:T(8,128)(2,1)S(1)} %get-tuple-element.21.g_ref, ...), custom_call_target="tpu_custom_call" | custom-call | flops 2147483648 | bytes 1048576 | tf_op jit(solution)/shard_map/own_grads/pallas_call | solution.py:359
  56.0 0.7 collective-permute-start.8
  56.7 3.7 %collective-permute-start.9 = (bf16[192,1280]{1,0:T(8,128)(2,1)S(1)}, bf16[192,1280]{1,0:T(8,128)(2,1)S(1)}, u32[]{:S(2)}, u32[]{:S(2)}) collective-permute-start(bf16[192,1280]{1,0:T(8,128)(2,1)S(1)} %get-tuple-element.34), channel_id=1, source_target_pairs={{8,16},{16,8},{9,17},{17,9},{10,18},{18,10},{11,19},{19,11},{12,20... | collective-permute-start | bytes 1474568 | tf_op jit(solution)/shard_map/ppermute | solution.py:430
  60.4 6.8 %halo_query_grad.1 = (bf16[96,1280]{1,0:T(8,128)(2,1)S(1)}, bf16[96,1280]{1,0:T(8,128)(2,1)S(1)}) custom-call(bf16[192,1280]{1,0:T(8,128)(2,1)S(1)} %collective-permute-done.h_0, bf16[192,1280]{1,0:T(8,128)(2,1)S(1)} %collective-permute-done.1.h_1, f32[24,256]{1,0:T(8,128)S(1)} %get-tuple-element.26.m_0, f32[24,256]{1,0:T(8,128)S(1)} %get-tuple-element.27.m_1, ...), custom_call_target="tpu_custom_call" | custom-call | flops 1073741824 | bytes 1048576 | tf_op jit(solution)/shard_map/halo_query_grad/pallas_call | solution.py:311
  67.1 0.1 collective-permute-start.6
  67.2 3.3 %collective-permute-start.7 = (bf16[96,1280]{1,0:T(8,128)(2,1)S(1)}, bf16[96,1280]{1,0:T(8,128)(2,1)S(1)}, u32[]{:S(2)}, u32[]{:S(2)}) collective-permute-start(bf16[96,1280]{1,0:T(8,128)(2,1)S(1)} %get-tuple-element.30), channel_id=1, source_target_pairs={{1,2},{2,1},{3,4},{4,3},{5,6},{6,5},{7,0},{0,7},{9,10},{10,9},{11,... | collective-permute-start | bytes 737288 | tf_op jit(solution)/shard_map/ppermute | solution.py:430
  70.6 7.1 %collective-permute-done.6.b_0 = bf16[96,1280]{1,0:T(8,128)(2,1)S(1)} collective-permute-done((bf16[96,1280]{1,0:T(8,128)(2,1)S(1)}, bf16[96,1280]{1,0:T(8,128)(2,1)S(1)}, u32[]{:S(2)}, u32[]{:S(2)}) %collective-permute-start.6) | collective-permute-done | bytes 245792 | tf_op jit(solution)/shard_map/ppermute | solution.py:430
  77.6 0.0 collective-permute-done.7.b_1
  77.6 4.5 %finish_queries.1 = bf16[256,1280]{1,0:T(8,128)(2,1)} custom-call(f32[256,1280]{1,0:T(8,128)S(1)} %get-tuple-element.28.g_ref, bf16[96,1280]{1,0:T(8,128)(2,1)S(1)} %collective-permute-done.6.b_0, bf16[96,1280]{1,0:T(8,128)(2,1)S(1)} %collective-permute-done.7.b_1), custom_call_target="tpu_custom_call" | custom-call | flops 268435456 | bytes 1048576 | tf_op jit(solution)/shard_map/finish_queries/pallas_call | solution.py:391
  82.1 0.0 collective-permute-done.8.b_0
  82.1 0.0 collective-permute-done.9.b_1
  82.1 3.7 %finish_keys.1 = (bf16[256,1280]{1,0:T(8,128)(2,1)}, bf16[256,1280]{1,0:T(8,128)(2,1)}) custom-call(f32[256,1280]{1,0:T(8,128)S(1)} %get-tuple-element.31.dk_ref, f32[256,1280]{1,0:T(8,128)S(1)} %get-tuple-element.32.dv_ref, bf16[192,1280]{1,0:T(8,128)(2,1)S(1)} %collective-permute-done.8.b_0, bf16[192,1280]{1,0:T(8,128)(2,1)S(1)} %collective-permute-done.9.b_1), custom_call_target="tpu_custom_call" | custom-call | flops 268435456 | bytes 1048576 | tf_op jit(solution)/shard_map/finish_keys/pallas_call | solution.py:415
Async XLA Ops:
  0.6 7.3 %copy-start = (bf16[16,16,1280]{2,1,0:T(8,128)(2,1)S(1)}, bf16[16,16,1280]{2,1,0:T(8,128)(2,1)}, u32[]{:S(2)}) copy-start(bf16[16,16,1280]{2,1,0:T(8,128)(2,1)} %param.4) | copy-start | bytes 1966084
  0.6 7.3 %copy-start.1 = (bf16[16,16,1280]{2,1,0:T(8,128)(2,1)S(1)}, bf16[16,16,1280]{2,1,0:T(8,128)(2,1)}, u32[]{:S(2)}) copy-start(bf16[16,16,1280]{2,1,0:T(8,128)(2,1)} %param.7) | copy-start | bytes 1966084
  0.7 1.2 %copy-start.2 = (bf16[16,16,1280]{2,1,0:T(8,128)(2,1)S(1)}, bf16[16,16,1280]{2,1,0:T(8,128)(2,1)}, u32[]{:S(2)}) copy-start(bf16[16,16,1280]{2,1,0:T(8,128)(2,1)} %param.5) | copy-start | bytes 1966084
  1.8 1.1 %copy-start.4 = (bf16[16,16,1280]{2,1,0:T(8,128)(2,1)S(1)}, bf16[16,16,1280]{2,1,0:T(8,128)(2,1)}, u32[]{:S(2)}) copy-start(bf16[16,16,1280]{2,1,0:T(8,128)(2,1)} %param.6) | copy-start | bytes 1966084
  2.9 12.7 %copy-start.3 = (bf16[16,16,1280]{2,1,0:T(8,128)(2,1)S(1)}, bf16[16,16,1280]{2,1,0:T(8,128)(2,1)}, u32[]{:S(2)}) copy-start(bf16[16,16,1280]{2,1,0:T(8,128)(2,1)} %param.5) | copy-start | bytes 1966084
  2.9 12.7 %copy-start.5 = (bf16[16,16,1280]{2,1,0:T(8,128)(2,1)S(1)}, bf16[16,16,1280]{2,1,0:T(8,128)(2,1)}, u32[]{:S(2)}) copy-start(bf16[16,16,1280]{2,1,0:T(8,128)(2,1)} %param.6) | copy-start | bytes 1966084
  3.3 12.3 %collective-permute-start.2 = (bf16[192,1280]{1,0:T(8,128)(2,1)S(1)}, bf16[192,1280]{1,0:T(8,128)(2,1)S(1)}, u32[]{:S(2)}, u32[]{:S(2)}) collective-permute-start(bf16[192,1280]{1,0:T(8,128)(2,1)S(1)} %get-tuple-element.24), channel_id=1, source_target_pairs={{0,8},{8,0},{16,24},{24,16},{1,9},{9,1},{17,25},{25,17},{2,10},{10... | collective-permute-start | bytes 1474568 | tf_op jit(solution)/shard_map/ppermute | solution.py:430
  3.5 12.1 %collective-permute-start.3 = (bf16[192,1280]{1,0:T(8,128)(2,1)S(1)}, bf16[192,1280]{1,0:T(8,128)(2,1)S(1)}, u32[]{:S(2)}, u32[]{:S(2)}) collective-permute-start(bf16[192,1280]{1,0:T(8,128)(2,1)S(1)} %get-tuple-element.25), channel_id=1, source_target_pairs={{8,16},{16,8},{9,17},{17,9},{10,18},{18,10},{11,19},{19,11},{12,20... | collective-permute-start | bytes 1474568 | tf_op jit(solution)/shard_map/ppermute | solution.py:430
  11.0 21.2 %collective-permute-start = (bf16[192,1280]{1,0:T(8,128)(2,1)S(1)}, bf16[192,1280]{1,0:T(8,128)(2,1)S(1)}, u32[]{:S(2)}, u32[]{:S(2)}) collective-permute-start(bf16[192,1280]{1,0:T(8,128)(2,1)S(1)} %get-tuple-element.22), channel_id=1, source_target_pairs={{0,1},{1,0},{2,3},{3,2},{4,5},{5,4},{6,7},{7,6},{8,9},{9,8},{10,11... | collective-permute-start | bytes 1474568 | tf_op jit(solution)/shard_map/ppermute | solution.py:430
  12.3 19.9 %collective-permute-start.1 = (bf16[192,1280]{1,0:T(8,128)(2,1)S(1)}, bf16[192,1280]{1,0:T(8,128)(2,1)S(1)}, u32[]{:S(2)}, u32[]{:S(2)}) collective-permute-start(bf16[192,1280]{1,0:T(8,128)(2,1)S(1)} %get-tuple-element.23), channel_id=1, source_target_pairs={{1,2},{2,1},{3,4},{4,3},{5,6},{6,5},{7,0},{0,7},{9,10},{10,9},{11,... | collective-permute-start | bytes 1474568 | tf_op jit(solution)/shard_map/ppermute | solution.py:430
  37.4 5.1 %collective-permute-start.4 = (f32[24,256]{1,0:T(8,128)S(1)}, f32[24,256]{1,0:T(8,128)S(1)}, u32[]{:S(2)}, u32[]{:S(2)}) collective-permute-start(f32[24,256]{1,0:T(8,128)S(1)} %get-tuple-element.26.m_0), channel_id=1, source_target_pairs={{0,1},{1,0},{2,3},{3,2},{4,5},{5,4},{6,7},{7,6},{8,9},{9,8},{10,11... | collective-permute-start | bytes 73736 | tf_op jit(solution)/shard_map/ppermute | solution.py:430
  39.2 5.7 %collective-permute-start.5 = (f32[24,256]{1,0:T(8,128)S(1)}, f32[24,256]{1,0:T(8,128)S(1)}, u32[]{:S(2)}, u32[]{:S(2)}) collective-permute-start(f32[24,256]{1,0:T(8,128)S(1)} %get-tuple-element.27.m_1), channel_id=1, source_target_pairs={{1,2},{2,1},{3,4},{4,3},{5,6},{6,5},{7,0},{0,7},{9,10},{10,9},{11,... | collective-permute-start | bytes 73736 | tf_op jit(solution)/shard_map/ppermute | solution.py:430
  56.0 26.2 %collective-permute-start.8 = (bf16[192,1280]{1,0:T(8,128)(2,1)S(1)}, bf16[192,1280]{1,0:T(8,128)(2,1)S(1)}, u32[]{:S(2)}, u32[]{:S(2)}) collective-permute-start(bf16[192,1280]{1,0:T(8,128)(2,1)S(1)} %get-tuple-element.33), channel_id=1, source_target_pairs={{0,8},{8,0},{16,24},{24,16},{1,9},{9,1},{17,25},{25,17},{2,10},{10... | collective-permute-start | bytes 1474568 | tf_op jit(solution)/shard_map/ppermute | solution.py:430
  56.7 25.4 %collective-permute-start.9 = (bf16[192,1280]{1,0:T(8,128)(2,1)S(1)}, bf16[192,1280]{1,0:T(8,128)(2,1)S(1)}, u32[]{:S(2)}, u32[]{:S(2)}) collective-permute-start(bf16[192,1280]{1,0:T(8,128)(2,1)S(1)} %get-tuple-element.34), channel_id=1, source_target_pairs={{8,16},{16,8},{9,17},{17,9},{10,18},{18,10},{11,19},{19,11},{12,20... | collective-permute-start | bytes 1474568 | tf_op jit(solution)/shard_map/ppermute | solution.py:430
  67.1 10.5 %collective-permute-start.6 = (bf16[96,1280]{1,0:T(8,128)(2,1)S(1)}, bf16[96,1280]{1,0:T(8,128)(2,1)S(1)}, u32[]{:S(2)}, u32[]{:S(2)}) collective-permute-start(bf16[96,1280]{1,0:T(8,128)(2,1)S(1)} %get-tuple-element.29), channel_id=1, source_target_pairs={{0,1},{1,0},{2,3},{3,2},{4,5},{5,4},{6,7},{7,6},{8,9},{9,8},{10,11... | collective-permute-start | bytes 737288 | tf_op jit(solution)/shard_map/ppermute | solution.py:430
  67.2 10.4 %collective-permute-start.7 = (bf16[96,1280]{1,0:T(8,128)(2,1)S(1)}, bf16[96,1280]{1,0:T(8,128)(2,1)S(1)}, u32[]{:S(2)}, u32[]{:S(2)}) collective-permute-start(bf16[96,1280]{1,0:T(8,128)(2,1)S(1)} %get-tuple-element.30), channel_id=1, source_target_pairs={{1,2},{2,1},{3,4},{4,3},{5,6},{6,5},{7,0},{0,7},{9,10},{10,9},{11,... | collective-permute-start | bytes 737288 | tf_op jit(solution)/shard_map/ppermute | solution.py:430

commit v2 on v0

v2 whole, which is shorter than its diff:
```python
import math

import jax
import jax.numpy as jnp
from jax import lax
from jax.experimental import pallas as pl
from jax.experimental.pallas import tpu as pltpu
from jax.sharding import PartitionSpec as P

HEAD_DIM = 128
WINDOW = 13
RADIUS = WINDOW // 2
LANES = 128
MASKED = -1e30
LOG2E = math.log2(math.e)
VMEM_BYTES = 24 * 1024 * 1024


def split(index, width):
    if width & (width - 1) == 0:
        whole = index >> (width.bit_length() - 1)
    else:
        whole = (index * ((1 << 12) // width + 1)) >> 12
    return whole, index - whole * width


def odd(axis):
    return lax.axis_index(axis) & 1


def slot_side(axis, slot):
    parity = odd(axis)
    return 1 - parity if slot == 0 else parity


def own_query_cell(position, rows, cols):
    edge = rows * RADIUS
    group = position >> 7
    place = position & (LANES - 1)
    side = jnp.where(group == 0, slot_side("lon", 0), slot_side("lon", 1))
    row_a, col_a = split(place, RADIUS)
    inner = cols - 2 * RADIUS
    row_b, col_b = split(place - edge + (LANES - edge) * group, inner)
    at_edge = place < edge
    row = jnp.where(at_edge, row_a, row_b)
    col = jnp.where(at_edge, side * (cols - RADIUS) + col_a, RADIUS + col_b)
    return row, col


def halo_query_cell(position, rows, cols):
    edge = rows * RADIUS
    group = position >> 7
    place = position & (LANES - 1)
    side = jnp.where(group == 0, slot_side("lon", 0), slot_side("lon", 1))
    row, col = split(place, RADIUS)
    col = jnp.where(side == 1, cols, -RADIUS) + col
    col = jnp.where(place < edge, col, 1 << 12)
    return row, col


def edge_key_cell(slot, position, rows, cols):
    near = LANES * 3 // 8
    inner = cols - 2 * RADIUS
    group = jnp.where(position >= near, 1, 0)
    side = jnp.where(group == 0, slot_side("lon", 0), slot_side("lon", 1))
    row_a, col_a = split(position - near * group, RADIUS)
    row_b, col_b = split(jnp.maximum(position - 2 * near, 0), inner)
    in_middle = position >= 2 * near
    row = jnp.where(in_middle, row_b, row_a)
    col = jnp.where(in_middle, RADIUS + col_b, side * (cols - RADIUS) + col_a)
    return jnp.where(row < RADIUS, row, -1), col


def band_edge(slot, rows):
    return slot_side("lat", slot) * (rows - RADIUS)


NEAR = 192
KEYS = 512


def near_key_cell(group, position, rows, cols):
    edge = rows * RADIUS
    half = LANES * 3 // 8
    side = slot_side("lon", group)
    row_a, col_a = split(position, RADIUS)
    row, col = row_a, col_a
    for slot in (0, 1):
        place = position - edge - half * slot
        row_b, col_b = split(jnp.maximum(place, 0), RADIUS)
        outside = jnp.where(slot_side("lat", slot) == 1, rows, -RADIUS)
        row_b = jnp.where(row_b < RADIUS, row_b + outside, -(1 << 12))
        row = jnp.where(place >= 0, row_b, row)
        col = jnp.where(place >= 0, col_b, col)
    return row, side * (cols - RADIUS) + col


def middle_key_cell(position, rows, cols):
    inner = cols - 2 * RADIUS
    edge = rows * inner
    row, col = split(position, inner)
    for slot in (0, 1):
        place = position - edge - 32 * slot
        row_b, col_b = split(jnp.maximum(place, 0), inner)
        outside = jnp.where(slot_side("lat", slot) == 1, rows, -RADIUS)
        row_b = jnp.where(row_b < RADIUS, row_b + outside, -(1 << 12))
        row = jnp.where(place >= 0, row_b, row)
        col = jnp.where(place >= 0, col_b, col)
    return row, RADIUS + col


def bias_of(key_cells, query_cells, rows):
    total_rows = rows * lax.axis_size("lat")
    first = rows * lax.axis_index("lat")
    key_row, key_col = key_cells
    query_row, query_col = query_cells
    start = jnp.clip(first + query_row - RADIUS, 0, total_rows - WINDOW)
    from_start = first + key_row - start
    inside = (from_start >= 0) & (from_start < WINDOW)
    inside = inside & (jnp.abs(key_col - query_col) <= RADIUS)
    return jnp.where(inside, 0.0, MASKED)


def down(count):
    return lax.broadcasted_iota(jnp.int32, (count, 1), 0)


def across(count, start=0):
    return lax.broadcasted_iota(jnp.int32, (1, count), 1) + start


def dot(a, b, contract):
    return lax.dot_general(a, b, ((contract[:1], contract[1:]), ((), ())), preferred_element_type=jnp.float32)


def call(kernel, name, operands, out_shapes, scratch=(), flops=0, aliases=None, outs=None, ins=None):
    spec = pl.BlockSpec(memory_space=pltpu.VMEM)
    return pl.pallas_call(
        kernel,
        name=name,
        in_specs=ins or [spec] * len(operands),
        out_specs=outs or [spec] * len(out_shapes),
        out_shape=out_shapes,
        scratch_shapes=scratch,
        input_output_aliases=aliases or {},
        compiler_params=pltpu.CompilerParams(vmem_limit_bytes=VMEM_BYTES),
        cost_estimate=pl.CostEstimate(flops=flops, bytes_accessed=1 << 20, transcendentals=0),
    )(*operands)


def low(*shape):
    return jax.ShapeDtypeStruct(shape, jnp.bfloat16)


def full(*shape):
    return jax.ShapeDtypeStruct(shape, jnp.float32)


def lanes_of(head, count=1):
    return slice(head * HEAD_DIM, (head + count) * HEAD_DIM)


def selection(row, col, rows, cols):
    source = across(rows * cols)
    return jnp.where(source == row * cols + col, 1.0, 0.0).astype(jnp.bfloat16)


def pack_queries(queries, out_grad, rows, cols, first, count):
    own, edge = rows * cols, rows * RADIUS

    def kernel(q_ref, g_ref, qp_ref, gp_ref, send_0, send_1):
        order = selection(*own_query_cell(down(own), rows, cols), rows, cols)
        for place, (src, dst) in enumerate(((q_ref, qp_ref), (g_ref, gp_ref))):
            for at in range(0, count, 2):
                here = lanes_of(at, min(2, count - at))
                moved = dot(order, src[:, lanes_of(first + at, min(2, count - at))], (1, 0)).astype(jnp.bfloat16)
                dst[:, here] = moved
                for group, send in enumerate((send_0, send_1)):
                    send[place * edge : (place + 1) * edge, here] = moved[group * LANES : group * LANES + edge]

    width = count * HEAD_DIM
    return call(
        kernel, "pack_queries", (queries, out_grad),
        [low(own, width)] * 2 + [low(2 * edge, width)] * 2, flops=1 << 28,
    )


def pack_keys(key_field, value_field, rows, cols):
    own = rows * cols
    width = key_field.shape[1]

    def kernel(k_ref, v_ref, kp_ref, vp_ref, send_0, send_1):
        order = selection(*own_query_cell(down(own), rows, cols), rows, cols)
        picks = []
        for slot in (0, 1):
            row, col = edge_key_cell(slot, down(LANES), rows, cols)
            row = jnp.where(row < 0, rows, row + band_edge(slot, rows))
            picks.append(selection(row, col, rows, cols))
        for part, (src, dst) in enumerate(((k_ref, kp_ref), (v_ref, vp_ref))):
            for at in range(0, width, 256):
                here = slice(at, at + 256)
                block = src[:, here]
                dst[:, here] = dot(order, block, (1, 0)).astype(jnp.bfloat16)
                for pick, send in zip(picks, (send_0, send_1)):
                    send[part * LANES : (part + 1) * LANES, here] = dot(pick, block, (1, 0)).astype(jnp.bfloat16)

    return call(
        kernel, "pack_keys", (key_field, value_field),
        [low(own, width)] * 2 + [low(2 * LANES, width)] * 2, flops=1 << 28,
    )


def halo_head(ref, edge, part, head):
    rows = ref[part * edge : (part + 1) * edge, lanes_of(head)]
    return jnp.concatenate([rows, jnp.zeros((LANES - edge, HEAD_DIM), jnp.bfloat16)], axis=0)


def near_keys(group, own_ref, lat_refs, part, head):
    lanes, half = lanes_of(head), LANES * 3 // 8
    edge = NEAR - 2 * half
    pieces = [own_ref[group * LANES : group * LANES + edge, lanes]]
    at = part * LANES + group * half
    pieces += [ref[at : at + half, lanes] for ref in lat_refs]
    return jnp.concatenate(pieces, axis=0)


def middle_keys(own_ref, lat_refs, part, head):
    lanes, half = lanes_of(head), LANES * 3 // 8
    edge = NEAR - 2 * half
    pieces = [own_ref[edge:LANES, lanes], own_ref[LANES + edge :, lanes]]
    at = part * LANES + 2 * half
    pieces += [ref[at : part * LANES + LANES, lanes] for ref in lat_refs]
    return jnp.concatenate(pieces, axis=0)


def every_key(own_ref, lat_refs, part, head):
    near = [near_keys(group, own_ref, lat_refs, part, head) for group in (0, 1)]
    return jnp.concatenate(near + [middle_keys(own_ref, lat_refs, part, head)], axis=0)


SCORE_SCALE = 1.0 / math.sqrt(HEAD_DIM)


def part_stats(scores, weight_grad):
    peak = jnp.max(scores, axis=0, keepdims=True)
    weights = jnp.exp2(scores - peak)
    total = jnp.sum(weights, axis=0, keepdims=True)
    dotted = jnp.sum(weights * weight_grad, axis=0, keepdims=True)
    return peak + jnp.log(total) * LOG2E, dotted / total


def stat_rows(count):
    return -(-2 * count // 8) * 8


def own_stats(qp, gp, kp, vp, lat, rows, cols, first, count):
    own = rows * cols

    def kernel(q_ref, g_ref, k_ref, v_ref, lat_0, lat_1, out, s_ref, d_ref, bias):
        lat_refs = (lat_0, lat_1)
        queries = own_query_cell(across(own), rows, cols)
        for group in (0, 1):
            bias[group * NEAR : (group + 1) * NEAR, :] = bias_of(
                near_key_cell(group, down(NEAR), rows, cols), queries, rows
            )
        bias[2 * NEAR :, :] = bias_of(middle_key_cell(down(LANES), rows, cols), queries, rows)
        out[...] = jnp.zeros_like(out)
        for head in range(count):
            key = every_key(k_ref, lat_refs, 0, first + head)
            value = every_key(v_ref, lat_refs, 1, first + head)
            scores = dot(key, q_ref[:, lanes_of(head)], (1, 1)) * (SCORE_SCALE * LOG2E) + bias[...]
            weight_grad = dot(value, g_ref[:, lanes_of(head)], (1, 1))
            s_ref[head] = scores
            d_ref[head] = weight_grad
            log_total, delta = part_stats(scores, weight_grad)
            out[head : head + 1, :] = log_total
            out[count + head : count + head + 1, :] = delta

    return call(
        kernel, "own_stats", (qp, gp, kp, vp, *lat),
        [full(stat_rows(count), own)] + [full(count, KEYS, own)] * 2,
        [pltpu.VMEM((KEYS, own), jnp.float32)], flops=1 << 30,
    )


def halo_stats(halo, own_stat, kp, vp, lat, rows, cols, first, count):
    edge = RADIUS * rows

    def kernel(h_0, h_1, stat, k_ref, v_ref, lat_0, lat_1, out_0, out_1, s_ref, d_ref, bias):
        lat_refs = (lat_0, lat_1)
        for group, (halo_ref, out) in enumerate(zip((h_0, h_1), (out_0, out_1))):
            lanes = slice(group * LANES, (group + 1) * LANES)
            bias[...] = bias_of(
                near_key_cell(group, down(NEAR), rows, cols),
                halo_query_cell(across(LANES, group * LANES), rows, cols), rows,
            )
            out[:, :LANES] = stat[:, lanes]
            out[:, LANES:] = jnp.zeros((out.shape[0], LANES), jnp.float32)
            for head in range(count):
                key = near_keys(group, k_ref, lat_refs, 0, first + head)
                value = near_keys(group, v_ref, lat_refs, 1, first + head)
                scores = dot(key, halo_head(halo_ref, edge, 0, head), (1, 1)) * (SCORE_SCALE * LOG2E) + bias[...]
                weight_grad = dot(value, halo_head(halo_ref, edge, 1, head), (1, 1))
                s_ref[head, :, lanes] = scores
                d_ref[head, :, lanes] = weight_grad
                log_total, delta = part_stats(scores, weight_grad)
                out[head : head + 1, LANES:] = log_total
                out[count + head : count + head + 1, LANES:] = delta

    return call(
        kernel, "halo_stats", (*halo, own_stat, kp, vp, *lat),
        [full(stat_rows(count), 2 * LANES)] * 2 + [full(count, NEAR, 2 * LANES)] * 2,
        [pltpu.VMEM((NEAR, LANES), jnp.float32)], flops=1 << 30,
    )


def combined(mine, theirs, count):
    a, b = mine[:count], theirs[:count]
    peak = jnp.maximum(a, b)
    part_a, part_b = jnp.exp2(a - peak), jnp.exp2(b - peak)
    total = part_a + part_b
    delta = (part_a * mine[count : 2 * count] + part_b * theirs[count : 2 * count]) / total
    return peak + jnp.log(total) * LOG2E, delta


LOW, HIGH = slice(0, LANES), slice(LANES, 2 * LANES)


def gradients(scores, weight_grad, log_total, delta):
    weights = jnp.exp2(scores - log_total)
    return weights.astype(jnp.bfloat16), (weights * (weight_grad - delta)).astype(jnp.bfloat16)


def halo_query_grad(mine, theirs, scores, weight_grad, kp, lat, rows, cols, first, count):
    edge = RADIUS * rows

    def kernel(m_0, m_1, t_0, t_1, s_ref, d_ref, k_ref, lat_0, lat_1, out_0, out_1, p_ref, g_ref):
        for group, (m, t, out) in enumerate(((m_0, t_0, out_0), (m_1, t_1, out_1))):
            lanes = slice(group * LANES, (group + 1) * LANES)
            log_total, delta = combined(m[:, HIGH], t[:, LOW], count)
            for head in range(count):
                here = slice(head, head + 1)
                weights, grad = gradients(
                    s_ref[head, :, lanes], d_ref[head, :, lanes], log_total[here], delta[here]
                )
                p_ref[head, :, lanes] = weights
                g_ref[head, :, lanes] = grad
                key = near_keys(group, k_ref, (lat_0, lat_1), 0, first + head)
                query_grad = dot(grad, key, (0, 0)) * SCORE_SCALE
                out[:, lanes_of(head)] = query_grad[:edge].astype(jnp.bfloat16)

    return call(
        kernel, "halo_query_grad", (*mine, *theirs, scores, weight_grad, kp, *lat),
        [low(edge, count * HEAD_DIM)] * 2 + [low(count, NEAR, 2 * LANES)] * 2, flops=1 << 30,
    )


def own_grads(qp, gp, halo, mine, theirs, scores, weight_grad, low_weights, low_grad, kp, lat, rows, cols, first, count):
    own, edge = rows * cols, RADIUS * rows
    half = LANES * 3 // 8

    def kernel(
        q_ref, g_ref, h_0, h_1, m_0, m_1, t_0, t_1, s_ref, d_ref, p_ref, l_ref, k_ref, lat_0, lat_1,
        dq_ref, dk_ref, dv_ref, out_0, out_1, total,
    ):
        combos = [combined(m[:, LOW], t[:, HIGH], count) for m, t in ((m_0, t_0), (m_1, t_1))]
        logs, deltas = (jnp.concatenate([c[i] for c in combos], axis=1) for i in (0, 1))
        for head in range(count):
            here, lanes = slice(head, head + 1), lanes_of(head)
            weights, grad = gradients(s_ref[head], d_ref[head], logs[here], deltas[here])
            key = every_key(k_ref, (lat_0, lat_1), 0, first + head)
            dq_ref[:, lanes] = dot(grad, key, (0, 0)) * SCORE_SCALE
            sides = (
                (grad, l_ref, q_ref, 0, dk_ref, SCORE_SCALE),
                (weights, p_ref, g_ref, 1, dv_ref, None),
            )
            for mine_low, halo_low, own_ref, part, result, scale in sides:
                total[...] = dot(mine_low, own_ref[:, lanes], (1, 0))
                for group, halo_ref in enumerate((h_0, h_1)):
                    near = slice(group * NEAR, (group + 1) * NEAR)
                    total[near, :] += dot(
                        halo_low[head, :, group * LANES : (group + 1) * LANES],
                        halo_head(halo_ref, edge, part, head), (1, 0),
                    )
                scaled = (lambda x: x) if scale is None else (lambda x: x * scale)
                middle = 2 * NEAR
                for group in (0, 1):
                    at = group * LANES
                    result[at : at + edge, lanes] = scaled(total[group * NEAR : group * NEAR + edge, :])
                    rest = LANES - edge
                    result[at + edge : at + LANES, lanes] = scaled(
                        total[middle + group * rest : middle + (group + 1) * rest, :]
                    )
                for slot, out in enumerate((out_0, out_1)):
                    base = part * LANES
                    for group in (0, 1):
                        at = group * NEAR + edge + slot * half
                        out[base + group * half : base + (group + 1) * half, lanes] = scaled(
                            total[at : at + half, :]
                        ).astype(jnp.bfloat16)
                    at = middle + 2 * (LANES - edge) + slot * 32
                    out[base + 2 * half : base + LANES, lanes] = scaled(total[at : at + 32, :]).astype(jnp.bfloat16)

    width = count * HEAD_DIM
    return call(
        kernel, "own_grads",
        (qp, gp, *halo, *mine, *theirs, scores, weight_grad, low_weights, low_grad, kp, *lat),
        [full(own, width)] * 3 + [low(2 * LANES, width)] * 2,
        [pltpu.VMEM((KEYS, HEAD_DIM), jnp.float32)], flops=1 << 31,
    )


def restore(rows, cols):
    own = rows * cols
    row, col = own_query_cell(across(own), rows, cols)
    return jnp.where(down(own) == row * cols + col, 1.0, 0.0).astype(jnp.bfloat16)


def finish_queries(grad, back, result, rows, cols, first, count, width):
    own, edge = rows * cols, rows * RADIUS

    def kernel(g_ref, b_0, b_1, *rest):
        out, total = rest[-2:]
        order = restore(rows, cols)
        total[...] = g_ref[...].astype(jnp.bfloat16)
        for group, back_ref in enumerate((b_0, b_1)):
            piece = slice(group * LANES, group * LANES + edge)
            total[piece, :] = (g_ref[piece, :] + back_ref[...].astype(jnp.float32)).astype(jnp.bfloat16)
        for at in range(0, count, 2):
            n = min(2, count - at)
            out[:, lanes_of(first + at, n)] = dot(order, total[:, lanes_of(at, n)], (1, 0)).astype(jnp.bfloat16)

    return call(
        kernel, "finish_queries", (grad, *back), [low(own, width)],
        [pltpu.VMEM((own, count * HEAD_DIM), jnp.bfloat16)], flops=1 << 28,
    )[0]


def finish_keys(key_grad, value_grad, back, rows, cols, first, count, width):
    own = rows * cols

    def kernel(dk_ref, dv_ref, b_0, b_1, out_k, out_v):
        order = restore(rows, cols)
        own_row, own_col = own_query_cell(down(own), rows, cols)
        spread = []
        for slot in (0, 1):
            row, col = edge_key_cell(slot, across(LANES), rows, cols)
            cell = jnp.where(row < 0, -1, (row + band_edge(slot, rows)) * cols + col)
            spread.append(jnp.where(own_row * cols + own_col == cell, 1.0, 0.0).astype(jnp.bfloat16))
        spread = jnp.concatenate(spread, axis=1)
        for part, (grad, out) in enumerate(((dk_ref, out_k), (dv_ref, out_v))):
            for at in range(0, count, 2):
                n = min(2, count - at)
                lanes = lanes_of(at, n)
                piece = slice(part * LANES, (part + 1) * LANES)
                arrived = jnp.concatenate([b_0[piece, lanes], b_1[piece, lanes]], axis=0)
                total = (grad[:, lanes] + dot(spread, arrived, (1, 0))).astype(jnp.bfloat16)
                out[:, lanes_of(first + at, n)] = dot(order, total, (1, 0)).astype(jnp.bfloat16)

    return call(kernel, "finish_keys", (key_grad, value_grad, *back), [low(own, width)] * 2, flops=1 << 28)


def swap(axis, slot, wrap, array):
    count = lax.axis_size(axis)
    pairs = []
    for lower in range(slot, count if wrap else count - 1, 2):
        upper = (lower + 1) % count
        pairs += [(lower, upper), (upper, lower)]
    return lax.ppermute(array, axis, pairs)


def swap_lon(arrays):
    second = swap("lon", 1, True, arrays[1])
    return [swap("lon", 0, True, arrays[0]), second]


def swap_lat(arrays):
    return [swap("lat", slot, False, array) for slot, array in enumerate(arrays)]


def after(value, *earlier):
    return lax.optimization_barrier((value, *earlier))[0]


def shards(queries, key_field, value_field, out_grad):
    rows, cols, width = queries.shape
    own = rows * cols
    flat = lambda x: x.reshape(own, width)
    queries, key_field, value_field, out_grad = map(flat, (queries, key_field, value_field, out_grad))
    size = (rows, cols)
    f, n = 0, width // HEAD_DIM

    qp, gp, *sends = pack_queries(queries, out_grad, *size, f, n)
    halo = swap_lon(sends)
    kp, vp, *sends = pack_keys(key_field, value_field, *size)
    lat = swap_lat(sends)
    own_stat, own_s, own_d = own_stats(qp, gp, kp, vp, lat, *size, f, n)
    *mine, halo_s, halo_d = halo_stats(halo, own_stat, kp, vp, lat, *size, f, n)
    theirs = swap_lon(mine)
    *back, low_weights, low_grad = halo_query_grad(mine, theirs, halo_s, halo_d, kp, lat, *size, f, n)
    back = swap_lon(back)
    dq, dk, dv, *lat_back = own_grads(
        qp, gp, halo, mine, theirs, own_s, own_d, low_weights, low_grad, kp, lat, *size, f, n
    )
    lat_back = swap_lat(lat_back)
    grad_query = finish_queries(dq, back, None, *size, f, n, width)
    grad_key, grad_value = finish_keys(dk, dv, lat_back, *size, f, n, width)
    shape = (rows, cols, width)
    return tuple(x.reshape(shape) for x in (grad_query, grad_key, grad_value))


def solution(mesh):
    spec = P("lat", "lon", None)
    return jax.shard_map(
        shards, mesh=mesh, in_specs=(spec,) * 4, out_specs=(spec,) * 3, check_vma=False
    )
```

time: 366 us -> 62.9 us (0.17)
  matrix products: 136 us -> 0 us
  local copies, waits for them, and re-layouts: 84.6 us -> 4.34 us
  waiting for transfers between devices: 99.6 us -> 23.9 us
  other arithmetic: 22.5 us -> 0 us
  Pallas kernels: 0 us -> 11.6 us
  starting transfers between devices: 17.8 us -> 22 us
    dot_general x100 -> x0, matrix products: 136 us -> none  [the longest x20 41.2 us: fold_of(): jnp.einsum('rwe,rwcd->ecd', pick_rows, partial_value, precision=lax.Preci...]
    ppermute x8 -> x10, waiting for transfers between devices: 99.6 us -> 23.9 us  [swap(): return lax.ppermute(array, axis, pairs)]
    dynamic_update_slice x30 -> x0, local copies, waits for them, and re-layouts: 16.8 us -> none  [the longest x10 8.39 us: head_pass(): pair_part = lax.dynamic_update_slice_in_dim(pair_part, key_fold, offset, 1)]
    dot_general x30 -> x0, local copies, waits for them, and re-layouts: 14.4 us -> none  [the longest x10 9.61 us: head_pass(): jnp.einsum('rqk,rqd->rkd', low_weights, grad_head, preferred_element_type...]
    pallas_call x0 -> x8, Pallas kernels: none -> 11.6 us  [call(): pl.pallas_call(kernel, name=name, in_specs=ins or [spec] * len(operands),...]
    another operation x3 -> x0, other arithmetic: 11 us -> none
    dynamic_slice x10 -> x0, local copies, waits for them, and re-layouts: 10.9 us -> none  [head_slice(): return lax.dynamic_slice_in_dim(tensor, offset, HEAD_DIM, tensor.ndim - 1)]
    reshape x21 -> x0, local copies, waits for them, and re-layouts: 10.2 us -> none  [the longest x1 9.6 us: shards(): partial_value = pair_part.reshape(ext_rows, ext_cols, 2 * feat_width)]
  transfers between devices with their start and end apart: 8 -> 10, of which waited for: 6 -> 4; matrix products, arithmetic and copies ran while one was open for 0% -> 0% of each run, Pallas kernels for 0% -> 6%
where the time goes in v2:
time: 62.9 us; the launch traced here: 62.5 us
  waiting for transfers between devices  23.9 us (38%)
  starting transfers between devices  22 us (35%)
  Pallas kernels  11.6 us (18%)
  local copies, waits for them, and re-layouts  4.34 us (7%)
  between operations  0.71 us (1%)
    ppermute x10, waiting for transfers between devices, swap(): return lax.ppermute(array, axis, pairs)  23.9 us
    ppermute x10, starting transfers between devices, swap(): return lax.ppermute(array, axis, pairs)  22 us
    pallas_call x8, Pallas kernels, call(): pl.pallas_call(kernel, name=name, in_specs=ins or [spec] * len(operands),...  11.6 us
    unnamed x8, local copies, waits for them, and re-layouts  4.34 us
  transfers between devices with their start and end apart: 10, of which 4 were waited for; matrix products, arithmetic and copies ran while one was open for 0% of the time, Pallas kernels for 6%

profile of v2, /device:TPU:1, one launch (start us, length us, event | category | flops | bytes accessed | tf_op | source)
XLA Modules:
  0.0 62.5 jit_solution(12376544712241511664)
XLA Ops:
  0.6 0.0 copy-start
  0.6 1.1 %copy-done = bf16[16,16,1280]{2,1,0:T(8,128)(2,1)S(1)} copy-done((bf16[16,16,1280]{2,1,0:T(8,128)(2,1)S(1)}, bf16[16,16,1280]{2,1,0:T(8,128)(2,1)}, u32[]{:S(2)}) %copy-start) | copy-done | bytes 655384
  1.7 0.0 copy-start.1
  1.7 1.1 %copy-done.1 = bf16[16,16,1280]{2,1,0:T(8,128)(2,1)S(1)} copy-done((bf16[16,16,1280]{2,1,0:T(8,128)(2,1)S(1)}, bf16[16,16,1280]{2,1,0:T(8,128)(2,1)}, u32[]{:S(2)}) %copy-start.1) | copy-done | bytes 655384
  2.8 0.9 %pack_keys.1 = (bf16[256,1280]{1,0:T(8,128)(2,1)S(1)}, bf16[256,1280]{1,0:T(8,128)(2,1)S(1)}, bf16[256,1280]{1,0:T(8,128)(2,1)S(1)}, bf16[256,1280]{1,0:T(8,128)(2,1)S(1)}) custom-call(bf16[256,1280]{1,0:T(8,128)(2,1)S(1)} %bitcast.7, bf16[256,1280]{1,0:T(8,128)(2,1)S(1)} %bitcast.8), custom_call_target="tpu_custom_call" | custom-call | flops 268435456 | bytes 1048576 | tf_op jit(solution)/shard_map/pack_keys/pallas_call | solution.py:138
  3.7 0.1 collective-permute-start.2
  3.8 4.5 %collective-permute-start.3 = (bf16[256,1280]{1,0:T(8,128)(2,1)S(1)}, bf16[256,1280]{1,0:T(8,128)(2,1)S(1)}, u32[]{:S(2)}, u32[]{:S(2)}) collective-permute-start(bf16[256,1280]{1,0:T(8,128)(2,1)S(1)} %get-tuple-element.36), channel_id=1, source_target_pairs={{8,16},{16,8},{9,17},{17,9},{10,18},{18,10},{11,19},{19,11},{12,20... | collective-permute-start | bytes 1966088 | tf_op jit(solution)/shard_map/ppermute | solution.py:469
  8.3 0.0 copy-start.2
  8.3 1.1 %copy-done.2 = bf16[16,16,1280]{2,1,0:T(8,128)(2,1)S(1)} copy-done((bf16[16,16,1280]{2,1,0:T(8,128)(2,1)S(1)}, bf16[16,16,1280]{2,1,0:T(8,128)(2,1)}, u32[]{:S(2)}) %copy-start.2) | copy-done | bytes 655384
  9.4 0.0 copy-start.3
  9.4 1.1 %copy-done.3 = bf16[16,16,1280]{2,1,0:T(8,128)(2,1)S(1)} copy-done((bf16[16,16,1280]{2,1,0:T(8,128)(2,1)S(1)}, bf16[16,16,1280]{2,1,0:T(8,128)(2,1)}, u32[]{:S(2)}) %copy-start.3) | copy-done | bytes 655384
  10.5 0.5 pack_queries.1
  11.0 1.3 %collective-permute-start = (bf16[192,1280]{1,0:T(8,128)(2,1)S(1)}, bf16[192,1280]{1,0:T(8,128)(2,1)S(1)}, u32[]{:S(2)}, u32[]{:S(2)}) collective-permute-start(bf16[192,1280]{1,0:T(8,128)(2,1)S(1)} %get-tuple-element.31), channel_id=1, source_target_pairs={{0,1},{1,0},{2,3},{3,2},{4,5},{5,4},{6,7},{7,6},{8,9},{9,8},{10,11... | collective-permute-start | bytes 1474568 | tf_op jit(solution)/shard_map/ppermute | solution.py:469
  12.3 3.3 %collective-permute-start.1 = (bf16[192,1280]{1,0:T(8,128)(2,1)S(1)}, bf16[192,1280]{1,0:T(8,128)(2,1)S(1)}, u32[]{:S(2)}, u32[]{:S(2)}) collective-permute-start(bf16[192,1280]{1,0:T(8,128)(2,1)S(1)} %get-tuple-element.32), channel_id=1, source_target_pairs={{1,2},{2,1},{3,4},{4,3},{5,6},{6,5},{7,0},{0,7},{9,10},{10,9},{11,... | collective-permute-start | bytes 1474568 | tf_op jit(solution)/shard_map/ppermute | solution.py:469
  15.6 0.0 collective-permute-done.2.lat_0
  15.6 1.3 %collective-permute-done.3.lat_1 = bf16[256,1280]{1,0:T(8,128)(2,1)S(1)} collective-permute-done((bf16[256,1280]{1,0:T(8,128)(2,1)S(1)}, bf16[256,1280]{1,0:T(8,128)(2,1)S(1)}, u32[]{:S(2)}, u32[]{:S(2)}) %collective-permute-start.3) | collective-permute-done | bytes 655392 | tf_op jit(solution)/shard_map/ppermute | solution.py:469
  16.8 2.3 %own_stats.1 = (f32[24,256]{1,0:T(8,128)S(1)}, f32[10,512,256]{2,1,0:T(8,128)S(1)}, f32[10,512,256]{2,1,0:T(8,128)S(1)}) custom-call(bf16[256,1280]{1,0:T(8,128)(2,1)S(1)} %get-tuple-element.29.q_ref, bf16[256,1280]{1,0:T(8,128)(2,1)S(1)} %get-tuple-element.30.g_ref, bf16[256,1280]{1,0:T(8,128)(2,1)S(1)} %get-tuple-element.33.k_ref, ...), custom_call_target="tpu_custom_call" | custom-call | flops 1073741824 | bytes 1048576 | tf_op jit(solution)/shard_map/own_stats/pallas_call | solution.py:138
  19.1 13.1 %collective-permute-done.h_0 = bf16[192,1280]{1,0:T(8,128)(2,1)S(1)} collective-permute-done((bf16[192,1280]{1,0:T(8,128)(2,1)S(1)}, bf16[192,1280]{1,0:T(8,128)(2,1)S(1)}, u32[]{:S(2)}, u32[]{:S(2)}) %collective-permute-start) | collective-permute-done | bytes 491552 | tf_op jit(solution)/shard_map/ppermute | solution.py:469
  32.2 0.0 collective-permute-done.1.h_1
  32.2 1.0 %halo_stats.1 = (f32[24,256]{1,0:T(8,128)S(1)}, f32[24,256]{1,0:T(8,128)S(1)}, f32[10,192,256]{2,1,0:T(8,128)S(1)}, f32[10,192,256]{2,1,0:T(8,128)S(1)}) custom-call(bf16[192,1280]{1,0:T(8,128)(2,1)S(1)} %collective-permute-done.h_0, bf16[192,1280]{1,0:T(8,128)(2,1)S(1)} %collective-permute-done.1.h_1, f32[24,256]{1,0:T(8,128)S(1)} %get-tuple-element.37.stat, ...), custom_call_target="tpu_custom_call" | custom-call | flops 1073741824 | bytes 1048576 | tf_op jit(solution)/shard_map/halo_stats/pallas_call | solution.py:138
  33.2 1.8 %collective-permute-start.4 = (f32[24,256]{1,0:T(8,128)S(1)}, f32[24,256]{1,0:T(8,128)S(1)}, u32[]{:S(2)}, u32[]{:S(2)}) collective-permute-start(f32[24,256]{1,0:T(8,128)S(1)} %get-tuple-element.38.m_0), channel_id=1, source_target_pairs={{0,1},{1,0},{2,3},{3,2},{4,5},{5,4},{6,7},{7,6},{8,9},{9,8},{10,11... | collective-permute-start | bytes 73736 | tf_op jit(solution)/shard_map/ppermute | solution.py:469
  35.0 3.3 %collective-permute-start.5 = (f32[24,256]{1,0:T(8,128)S(1)}, f32[24,256]{1,0:T(8,128)S(1)}, u32[]{:S(2)}, u32[]{:S(2)}) collective-permute-start(f32[24,256]{1,0:T(8,128)S(1)} %get-tuple-element.39.m_1), channel_id=1, source_target_pairs={{1,2},{2,1},{3,4},{4,3},{5,6},{6,5},{7,0},{0,7},{9,10},{10,9},{11,... | collective-permute-start | bytes 73736 | tf_op jit(solution)/shard_map/ppermute | solution.py:469
  38.2 0.0 collective-permute-done.4.t_0
  38.2 2.4 %collective-permute-done.5.t_1 = f32[24,256]{1,0:T(8,128)S(1)} collective-permute-done((f32[24,256]{1,0:T(8,128)S(1)}, f32[24,256]{1,0:T(8,128)S(1)}, u32[]{:S(2)}, u32[]{:S(2)}) %collective-permute-start.5) | collective-permute-done | bytes 24608 | tf_op jit(solution)/shard_map/ppermute | solution.py:469
  40.7 0.9 %halo_query_grad.1 = (bf16[96,1280]{1,0:T(8,128)(2,1)S(1)}, bf16[96,1280]{1,0:T(8,128)(2,1)S(1)}, bf16[10,192,256]{2,1,0:T(8,128)(2,1)S(1)}, bf16[10,192,256]{2,1,0:T(8,128)(2,1)S(1)}) custom-call(f32[24,256]{1,0:T(8,128)S(1)} %get-tuple-element.38.m_0, f32[24,256]{1,0:T(8,128)S(1)} %get-tuple-element.39.m_1, f32[24,256]{1,0:T(8,128)S(1)} %collective-permute-done.4.t_0, ...), custom_call_target="tpu_custom_call" | custom-call | flops 1073741824 | bytes 1048576 | tf_op jit(solution)/shard_map/halo_query_grad/pallas_call | solution.py:138
  41.6 3.0 %own_grads.1 = (f32[256,1280]{1,0:T(8,128)S(1)}, f32[256,1280]{1,0:T(8,128)S(1)}, f32[256,1280]{1,0:T(8,128)S(1)}, bf16[256,1280]{1,0:T(8,128)(2,1)S(1)}, bf16[256,1280]{1,0:T(8,128)(2,1)S(1)}) custom-call(bf16[256,1280]{1,0:T(8,128)(2,1)S(1)} %get-tuple-element.29.q_ref, bf16[256,1280]{1,0:T(8,128)(2,1)S(1)} %get-tuple-element.30.g_ref, ...), custom_call_target="tpu_custom_call" | custom-call | flops 2147483648 | bytes 1048576 | tf_op jit(solution)/shard_map/own_grads/pallas_call | solution.py:138
  44.6 0.7 %collective-permute-start.8 = (bf16[256,1280]{1,0:T(8,128)(2,1)S(1)}, bf16[256,1280]{1,0:T(8,128)(2,1)S(1)}, u32[]{:S(2)}, u32[]{:S(2)}) collective-permute-start(bf16[256,1280]{1,0:T(8,128)(2,1)S(1)} %get-tuple-element.51), channel_id=1, source_target_pairs={{0,8},{8,0},{16,24},{24,16},{1,9},{9,1},{17,25},{25,17},{2,10},{10... | collective-permute-start | bytes 1966088 | tf_op jit(solution)/shard_map/ppermute | solution.py:469
  45.3 3.7 %collective-permute-start.9 = (bf16[256,1280]{1,0:T(8,128)(2,1)S(1)}, bf16[256,1280]{1,0:T(8,128)(2,1)S(1)}, u32[]{:S(2)}, u32[]{:S(2)}) collective-permute-start(bf16[256,1280]{1,0:T(8,128)(2,1)S(1)} %get-tuple-element.52), channel_id=1, source_target_pairs={{8,16},{16,8},{9,17},{17,9},{10,18},{18,10},{11,19},{19,11},{12,20... | collective-permute-start | bytes 1966088 | tf_op jit(solution)/shard_map/ppermute | solution.py:469
  49.0 0.1 collective-permute-start.6
  49.0 3.3 %collective-permute-start.7 = (bf16[96,1280]{1,0:T(8,128)(2,1)S(1)}, bf16[96,1280]{1,0:T(8,128)(2,1)S(1)}, u32[]{:S(2)}, u32[]{:S(2)}) collective-permute-start(bf16[96,1280]{1,0:T(8,128)(2,1)S(1)} %get-tuple-element.48), channel_id=1, source_target_pairs={{1,2},{2,1},{3,4},{4,3},{5,6},{6,5},{7,0},{0,7},{9,10},{10,9},{11,... | collective-permute-start | bytes 737288 | tf_op jit(solution)/shard_map/ppermute | solution.py:469
  52.4 7.1 %collective-permute-done.6.b_0 = bf16[96,1280]{1,0:T(8,128)(2,1)S(1)} collective-permute-done((bf16[96,1280]{1,0:T(8,128)(2,1)S(1)}, bf16[96,1280]{1,0:T(8,128)(2,1)S(1)}, u32[]{:S(2)}, u32[]{:S(2)}) %collective-permute-start.6) | collective-permute-done | bytes 245792 | tf_op jit(solution)/shard_map/ppermute | solution.py:469
  59.5 0.0 collective-permute-done.7.b_1
  59.5 1.2 %finish_queries.1 = bf16[256,1280]{1,0:T(8,128)(2,1)} custom-call(f32[256,1280]{1,0:T(8,128)S(1)} %get-tuple-element.46.g_ref, bf16[96,1280]{1,0:T(8,128)(2,1)S(1)} %collective-permute-done.6.b_0, bf16[96,1280]{1,0:T(8,128)(2,1)S(1)} %collective-permute-done.7.b_1), custom_call_target="tpu_custom_call" | custom-call | flops 268435456 | bytes 1048576 | tf_op jit(solution)/shard_map/finish_queries/pallas_call | solution.py:138
  60.7 0.0 collective-permute-done.8.b_0
  60.7 0.0 collective-permute-done.9.b_1
  60.7 1.9 %finish_keys.1 = (bf16[256,1280]{1,0:T(8,128)(2,1)}, bf16[256,1280]{1,0:T(8,128)(2,1)}) custom-call(f32[256,1280]{1,0:T(8,128)S(1)} %get-tuple-element.49.dk_ref, f32[256,1280]{1,0:T(8,128)S(1)} %get-tuple-element.50.dv_ref, bf16[256,1280]{1,0:T(8,128)(2,1)S(1)} %collective-permute-done.8.b_0, bf16[256,1280]{1,0:T(8,128)(2,1)S(1)} %collective-permute-done.9.b_1), custom_call_target="tpu_custom_call" | custom-call | flops 268435456 | bytes 1048576 | tf_op jit(solution)/shard_map/finish_keys/pallas_call | solution.py:138
Async XLA Ops:
  0.6 1.1 %copy-start = (bf16[16,16,1280]{2,1,0:T(8,128)(2,1)S(1)}, bf16[16,16,1280]{2,1,0:T(8,128)(2,1)}, u32[]{:S(2)}) copy-start(bf16[16,16,1280]{2,1,0:T(8,128)(2,1)} %param.5) | copy-start | bytes 1966084
  1.7 1.1 %copy-start.1 = (bf16[16,16,1280]{2,1,0:T(8,128)(2,1)S(1)}, bf16[16,16,1280]{2,1,0:T(8,128)(2,1)}, u32[]{:S(2)}) copy-start(bf16[16,16,1280]{2,1,0:T(8,128)(2,1)} %param.6) | copy-start | bytes 1966084
  3.7 11.9 %collective-permute-start.2 = (bf16[256,1280]{1,0:T(8,128)(2,1)S(1)}, bf16[256,1280]{1,0:T(8,128)(2,1)S(1)}, u32[]{:S(2)}, u32[]{:S(2)}) collective-permute-start(bf16[256,1280]{1,0:T(8,128)(2,1)S(1)} %get-tuple-element.35), channel_id=1, source_target_pairs={{0,8},{8,0},{16,24},{24,16},{1,9},{9,1},{17,25},{25,17},{2,10},{10... | collective-permute-start | bytes 1966088 | tf_op jit(solution)/shard_map/ppermute | solution.py:469
  3.8 13.0 %collective-permute-start.3 = (bf16[256,1280]{1,0:T(8,128)(2,1)S(1)}, bf16[256,1280]{1,0:T(8,128)(2,1)S(1)}, u32[]{:S(2)}, u32[]{:S(2)}) collective-permute-start(bf16[256,1280]{1,0:T(8,128)(2,1)S(1)} %get-tuple-element.36), channel_id=1, source_target_pairs={{8,16},{16,8},{9,17},{17,9},{10,18},{18,10},{11,19},{19,11},{12,20... | collective-permute-start | bytes 1966088 | tf_op jit(solution)/shard_map/ppermute | solution.py:469
  8.3 1.1 %copy-start.2 = (bf16[16,16,1280]{2,1,0:T(8,128)(2,1)S(1)}, bf16[16,16,1280]{2,1,0:T(8,128)(2,1)}, u32[]{:S(2)}) copy-start(bf16[16,16,1280]{2,1,0:T(8,128)(2,1)} %param.4) | copy-start | bytes 1966084
  9.4 1.1 %copy-start.3 = (bf16[16,16,1280]{2,1,0:T(8,128)(2,1)S(1)}, bf16[16,16,1280]{2,1,0:T(8,128)(2,1)}, u32[]{:S(2)}) copy-start(bf16[16,16,1280]{2,1,0:T(8,128)(2,1)} %param.7) | copy-start | bytes 1966084
  11.0 21.2 %collective-permute-start = (bf16[192,1280]{1,0:T(8,128)(2,1)S(1)}, bf16[192,1280]{1,0:T(8,128)(2,1)S(1)}, u32[]{:S(2)}, u32[]{:S(2)}) collective-permute-start(bf16[192,1280]{1,0:T(8,128)(2,1)S(1)} %get-tuple-element.31), channel_id=1, source_target_pairs={{0,1},{1,0},{2,3},{3,2},{4,5},{5,4},{6,7},{7,6},{8,9},{9,8},{10,11... | collective-permute-start | bytes 1474568 | tf_op jit(solution)/shard_map/ppermute | solution.py:469
  12.3 19.9 %collective-permute-start.1 = (bf16[192,1280]{1,0:T(8,128)(2,1)S(1)}, bf16[192,1280]{1,0:T(8,128)(2,1)S(1)}, u32[]{:S(2)}, u32[]{:S(2)}) collective-permute-start(bf16[192,1280]{1,0:T(8,128)(2,1)S(1)} %get-tuple-element.32), channel_id=1, source_target_pairs={{1,2},{2,1},{3,4},{4,3},{5,6},{6,5},{7,0},{0,7},{9,10},{10,9},{11,... | collective-permute-start | bytes 1474568 | tf_op jit(solution)/shard_map/ppermute | solution.py:469
  33.2 5.1 %collective-permute-start.4 = (f32[24,256]{1,0:T(8,128)S(1)}, f32[24,256]{1,0:T(8,128)S(1)}, u32[]{:S(2)}, u32[]{:S(2)}) collective-permute-start(f32[24,256]{1,0:T(8,128)S(1)} %get-tuple-element.38.m_0), channel_id=1, source_target_pairs={{0,1},{1,0},{2,3},{3,2},{4,5},{5,4},{6,7},{7,6},{8,9},{9,8},{10,11... | collective-permute-start | bytes 73736 | tf_op jit(solution)/shard_map/ppermute | solution.py:469
  35.0 5.7 %collective-permute-start.5 = (f32[24,256]{1,0:T(8,128)S(1)}, f32[24,256]{1,0:T(8,128)S(1)}, u32[]{:S(2)}, u32[]{:S(2)}) collective-permute-start(f32[24,256]{1,0:T(8,128)S(1)} %get-tuple-element.39.m_1), channel_id=1, source_target_pairs={{1,2},{2,1},{3,4},{4,3},{5,6},{6,5},{7,0},{0,7},{9,10},{10,9},{11,... | collective-permute-start | bytes 73736 | tf_op jit(solution)/shard_map/ppermute | solution.py:469
  44.6 16.1 %collective-permute-start.8 = (bf16[256,1280]{1,0:T(8,128)(2,1)S(1)}, bf16[256,1280]{1,0:T(8,128)(2,1)S(1)}, u32[]{:S(2)}, u32[]{:S(2)}) collective-permute-start(bf16[256,1280]{1,0:T(8,128)(2,1)S(1)} %get-tuple-element.51), channel_id=1, source_target_pairs={{0,8},{8,0},{16,24},{24,16},{1,9},{9,1},{17,25},{25,17},{2,10},{10... | collective-permute-start | bytes 1966088 | tf_op jit(solution)/shard_map/ppermute | solution.py:469
  45.3 15.4 %collective-permute-start.9 = (bf16[256,1280]{1,0:T(8,128)(2,1)S(1)}, bf16[256,1280]{1,0:T(8,128)(2,1)S(1)}, u32[]{:S(2)}, u32[]{:S(2)}) collective-permute-start(bf16[256,1280]{1,0:T(8,128)(2,1)S(1)} %get-tuple-element.52), channel_id=1, source_target_pairs={{8,16},{16,8},{9,17},{17,9},{10,18},{18,10},{11,19},{19,11},{12,20... | collective-permute-start | bytes 1966088 | tf_op jit(solution)/shard_map/ppermute | solution.py:469
  49.0 10.5 %collective-permute-start.6 = (bf16[96,1280]{1,0:T(8,128)(2,1)S(1)}, bf16[96,1280]{1,0:T(8,128)(2,1)S(1)}, u32[]{:S(2)}, u32[]{:S(2)}) collective-permute-start(bf16[96,1280]{1,0:T(8,128)(2,1)S(1)} %get-tuple-element.47), channel_id=1, source_target_pairs={{0,1},{1,0},{2,3},{3,2},{4,5},{5,4},{6,7},{7,6},{8,9},{9,8},{10,11... | collective-permute-start | bytes 737288 | tf_op jit(solution)/shard_map/ppermute | solution.py:469
  49.0 10.4 %collective-permute-start.7 = (bf16[96,1280]{1,0:T(8,128)(2,1)S(1)}, bf16[96,1280]{1,0:T(8,128)(2,1)S(1)}, u32[]{:S(2)}, u32[]{:S(2)}) collective-permute-start(bf16[96,1280]{1,0:T(8,128)(2,1)S(1)} %get-tuple-element.48), channel_id=1, source_target_pairs={{1,2},{2,1},{3,4},{4,3},{5,6},{6,5},{7,0},{0,7},{9,10},{10,9},{11,... | collective-permute-start | bytes 737288 | tf_op jit(solution)/shard_map/ppermute | solution.py:469

commit v3 on v2

v3 whole, which is shorter than its diff:
```python
import math

import jax
import jax.numpy as jnp
from jax import lax
from jax.experimental import pallas as pl
from jax.experimental.pallas import tpu as pltpu
from jax.sharding import PartitionSpec as P

HEAD_DIM = 128
WINDOW = 13
RADIUS = WINDOW // 2
LANES = 128
FIRST = 0
MASKED = -1e30
LOG2E = math.log2(math.e)
VMEM_BYTES = 24 * 1024 * 1024


def split(index, width):
    if width & (width - 1) == 0:
        whole = index >> (width.bit_length() - 1)
    else:
        whole = (index * ((1 << 12) // width + 1)) >> 12
    return whole, index - whole * width


def odd(axis):
    return lax.axis_index(axis) & 1


def slot_side(axis, slot):
    parity = odd(axis)
    return parity if slot == 0 else 1 - parity


def own_query_cell(position, rows, cols):
    edge = rows * RADIUS
    group = position >> 7
    place = position & (LANES - 1)
    side = jnp.where(group == 0, slot_side("lon", 0), slot_side("lon", 1))
    row_a, col_a = split(place, RADIUS)
    inner = cols - 2 * RADIUS
    row_b, col_b = split(place - edge + (LANES - edge) * group, inner)
    at_edge = place < edge
    row = jnp.where(at_edge, row_a, row_b)
    col = jnp.where(at_edge, side * (cols - RADIUS) + col_a, RADIUS + col_b)
    return row, col


def halo_query_cell(position, rows, cols):
    edge = rows * RADIUS
    group = position >> 7
    place = position & (LANES - 1)
    side = jnp.where(group == 0, slot_side("lon", 0), slot_side("lon", 1))
    row, col = split(place, RADIUS)
    col = jnp.where(side == 1, cols, -RADIUS) + col
    col = jnp.where(place < edge, col, 1 << 12)
    return row, col


def lat_key_cell(slot, position, rows, cols):
    row, col = split(position, cols)
    return row + jnp.where(slot_side("lat", slot) == 1, rows, -RADIUS), col


def bias_of(key_cells, query_cells, rows):
    total_rows = rows * lax.axis_size("lat")
    first = rows * lax.axis_index("lat")
    key_row, key_col = key_cells
    query_row, query_col = query_cells
    start = jnp.clip(first + query_row - RADIUS, 0, total_rows - WINDOW)
    from_start = first + key_row - start
    inside = (from_start >= 0) & (from_start < WINDOW)
    inside = inside & (jnp.abs(key_col - query_col) <= RADIUS)
    return jnp.where(inside, 0.0, MASKED)


def down(count):
    return lax.broadcasted_iota(jnp.int32, (count, 1), 0)


def across(count, start=0):
    return lax.broadcasted_iota(jnp.int32, (1, count), 1) + start


def dot(a, b, contract):
    return lax.dot_general(a, b, ((contract[:1], contract[1:]), ((), ())), preferred_element_type=jnp.float32)


def call(kernel, name, operands, out_shapes, scratch=(), flops=0, aliases=None, outs=None, ins=None):
    return pl.pallas_call(
        kernel,
        name=name,
        in_specs=ins or [VMEM_SPEC] * len(operands),
        out_specs=outs or [VMEM_SPEC] * len(out_shapes),
        out_shape=out_shapes,
        scratch_shapes=scratch,
        input_output_aliases=aliases or {},
        compiler_params=pltpu.CompilerParams(vmem_limit_bytes=VMEM_BYTES),
        cost_estimate=pl.CostEstimate(flops=flops, bytes_accessed=0, transcendentals=0),
    )(*operands)


def low(*shape):
    return jax.ShapeDtypeStruct(shape, jnp.bfloat16)


def full(*shape):
    return jax.ShapeDtypeStruct(shape, jnp.float32)


def lanes_of(head, count=1):
    return slice(head * HEAD_DIM, (head + count) * HEAD_DIM)


def selection(row, col, rows, cols):
    source = across(rows * cols)
    return jnp.where(source == row * cols + col, 1.0, 0.0).astype(jnp.bfloat16)


HBM_SPEC, VMEM_SPEC = pl.BlockSpec(memory_space=pltpu.HBM), pl.BlockSpec(memory_space=pltpu.VMEM)
BLOCK = 2 * HEAD_DIM


def pack_queries(queries, out_grad, key_field, value_field, rows, cols, count):
    own, edge, width = rows * cols, rows * RADIUS, count * HEAD_DIM

    def kernel(q_hbm, g_hbm, k_hbm, v_hbm, qp_ref, gp_ref, send_0, send_1, k_ref, v_ref, q_ref, g_ref, sems):
        copies = [
            pltpu.make_async_copy(src, dst, sems.at[i])
            for i, (src, dst) in enumerate(
                ((q_hbm, q_ref), (g_hbm, g_ref), (k_hbm, k_ref), (v_hbm, v_ref))
            )
        ]
        for copy in copies:
            copy.start()
        order = selection(*own_query_cell(down(own), rows, cols), rows, cols)
        for place, (src, dst) in enumerate(((q_ref, qp_ref), (g_ref, gp_ref))):
            copies[place].wait()
            for at in range(0, width, BLOCK):
                here = slice(at, at + BLOCK)
                moved = dot(order, src[:, here], (1, 0)).astype(jnp.bfloat16)
                dst[:, here] = moved
                for group, send in enumerate((send_0, send_1)):
                    send[place * edge : (place + 1) * edge, here] = moved[group * LANES : group * LANES + edge]
        copies[2].wait()
        copies[3].wait()

    operands = [
        pltpu.with_memory_space_constraint(x, pltpu.HBM) for x in (queries, out_grad, key_field, value_field)
    ]
    return call(
        kernel, "pack_queries", operands,
        [low(own, width)] * 2 + [low(2 * edge, width)] * 2 + [low(own, width)] * 2,
        [pltpu.VMEM((own, width), jnp.bfloat16)] * 2 + [pltpu.SemaphoreType.DMA((4,))],
        ins=[HBM_SPEC] * 4,
    )


def pack_keys(key_field, value_field, rows, cols):
    own, edge = rows * cols, RADIUS * cols
    width = key_field.shape[1]

    def kernel(k_ref, v_ref, kp_ref, vp_ref, k_0, k_1, v_0, v_1):
        order = selection(*own_query_cell(down(own), rows, cols), rows, cols)
        for src, dst, sends in zip((k_ref, v_ref), (kp_ref, vp_ref), ((k_0, k_1), (v_0, v_1))):
            for slot, send in enumerate(sends):
                start = pl.multiple_of(slot_side("lat", slot) * (own - edge), 16)
                send[...] = src[pl.ds(start, edge), :]
            for at in range(0, width, BLOCK):
                here = slice(at, at + BLOCK)
                dst[:, here] = dot(order, src[:, here], (1, 0)).astype(jnp.bfloat16)

    return call(
        kernel, "pack_keys", (key_field, value_field),
        [low(own, width)] * 2 + [low(edge, width)] * 4,
    )


def halo_head(ref, edge, part, head):
    rows = ref[part * edge : (part + 1) * edge, lanes_of(head)]
    return jnp.concatenate([rows, jnp.zeros((LANES - edge, HEAD_DIM), jnp.bfloat16)], axis=0)


def near_keys(group, own_ref, lat_refs, head):
    lanes, edge = lanes_of(head), lat_refs[0].shape[0]
    pieces = [own_ref[group * LANES : group * LANES + edge, lanes]]
    return jnp.concatenate(pieces + [ref[:, lanes] for ref in lat_refs], axis=0)


def every_key(own_ref, lat_refs, head):
    lanes = lanes_of(head)
    return jnp.concatenate([ref[:, lanes] for ref in (own_ref, *lat_refs)], axis=0)


def fill_bias(bias, own_position, queries, rows, cols):
    at, edge = own_position.shape[0], RADIUS * cols
    bias[:at, :] = bias_of(own_query_cell(own_position, rows, cols), queries, rows)
    for slot in (0, 1):
        here = slice(at + slot * edge, at + (slot + 1) * edge)
        bias[here, :] = bias_of(lat_key_cell(slot, down(edge), rows, cols), queries, rows)


LOW, HIGH = slice(0, LANES), slice(LANES, 2 * LANES)
SCORE_SCALE = 1.0 / math.sqrt(HEAD_DIM)


def part_stats(scores, weight_grad):
    peak = jnp.max(scores, axis=0, keepdims=True)
    weights = jnp.exp2(scores - peak)
    total = jnp.sum(weights, axis=0, keepdims=True)
    dotted = jnp.sum(weights * weight_grad, axis=0, keepdims=True)
    return peak + jnp.log(total) * LOG2E, dotted / total


def stat_rows(count):
    return -(-2 * count // 8) * 8


def own_stats(qp, gp, kp, vp, lat, rows, cols, count):
    own, keys = rows * cols, (rows + 2 * RADIUS) * cols

    def kernel(q_ref, g_ref, k_ref, v_ref, k_0, k_1, v_0, v_1, out, s_ref, d_ref, bias):
        fill_bias(bias, down(own), own_query_cell(across(own), rows, cols), rows, cols)
        out[...] = jnp.zeros_like(out)
        for head in range(count):
            key = every_key(k_ref, (k_0, k_1), head)
            value = every_key(v_ref, (v_0, v_1), head)
            scores = dot(key, q_ref[:, lanes_of(head)], (1, 1)) * (SCORE_SCALE * LOG2E) + bias[...]
            weight_grad = dot(value, g_ref[:, lanes_of(head)], (1, 1))
            s_ref[head] = scores
            d_ref[head] = weight_grad
            log_total, delta = part_stats(scores, weight_grad)
            out[head : head + 1, :] = log_total
            out[count + head : count + head + 1, :] = delta

    return call(
        kernel, "own_stats", (qp, gp, kp, vp, *lat),
        [full(stat_rows(count), own)] + [full(count, keys, own)] * 2,
        [pltpu.VMEM((keys, own), jnp.float32)],
    )


def halo_stats(group, halo, own_stat, kp, vp, lat, rows, cols, count):
    edge = RADIUS * rows
    near = edge + 2 * RADIUS * cols

    def kernel(halo_ref, stat, k_ref, v_ref, k_0, k_1, v_0, v_1, out, s_ref, d_ref, bias):
        queries = halo_query_cell(across(LANES, group * LANES), rows, cols)
        fill_bias(bias, down(edge) + group * LANES, queries, rows, cols)
        out[:, LOW] = stat[:, group * LANES : (group + 1) * LANES]
        out[:, HIGH] = jnp.zeros((out.shape[0], LANES), jnp.float32)
        for head in range(count):
            key = near_keys(group, k_ref, (k_0, k_1), head)
            value = near_keys(group, v_ref, (v_0, v_1), head)
            scores = dot(key, halo_head(halo_ref, edge, 0, head), (1, 1)) * (SCORE_SCALE * LOG2E) + bias[...]
            weight_grad = dot(value, halo_head(halo_ref, edge, 1, head), (1, 1))
            s_ref[head] = scores
            d_ref[head] = weight_grad
            log_total, delta = part_stats(scores, weight_grad)
            out[head : head + 1, HIGH] = log_total
            out[count + head : count + head + 1, HIGH] = delta

    return call(
        kernel, f"halo_stats_{group}", (halo, own_stat, kp, vp, *lat),
        [full(stat_rows(count), 2 * LANES)] + [full(count, near, LANES)] * 2,
        [pltpu.VMEM((near, LANES), jnp.float32)],
    )


def combined(mine, theirs, count):
    a, b = mine[:count], theirs[:count]
    peak = jnp.maximum(a, b)
    part_a, part_b = jnp.exp2(a - peak), jnp.exp2(b - peak)
    total = part_a + part_b
    delta = (part_a * mine[count : 2 * count] + part_b * theirs[count : 2 * count]) / total
    return peak + jnp.log(total) * LOG2E, delta


def gradients(scores, weight_grad, log_total, delta):
    weights = jnp.exp2(scores - log_total)
    return weights.astype(jnp.bfloat16), (weights * (weight_grad - delta)).astype(jnp.bfloat16)


def halo_query_grad(group, mine, theirs, scores, weight_grad, kp, lat, rows, cols, count):
    edge = RADIUS * rows

    def kernel(m, t, s_ref, d_ref, k_ref, lat_0, lat_1, out, p_ref, g_ref):
        log_total, delta = combined(m[:, HIGH], t[:, LOW], count)
        for head in range(count):
            here = slice(head, head + 1)
            p_ref[head], grad = gradients(s_ref[head], d_ref[head], log_total[here], delta[here])
            g_ref[head] = grad
            key = near_keys(group, k_ref, (lat_0, lat_1), head)
            query_grad = dot(grad, key, (0, 0)) * SCORE_SCALE
            out[:, lanes_of(head)] = query_grad[:edge].astype(jnp.bfloat16)

    return call(
        kernel, f"halo_query_grad_{group}", (mine, theirs, scores, weight_grad, kp, *lat),
        [low(edge, count * HEAD_DIM)] + [low(count, *scores.shape[1:])] * 2,
    )


def group_grads(group, refs, dq_ref, use, rows, cols, count):
    q_ref, g_ref, halo_ref, m, t, s_ref, d_ref, p_ref, l_ref, k_ref, *lat_refs = refs
    own, edge = rows * cols, RADIUS * rows
    here = slice(group * LANES, (group + 1) * LANES)
    near = slice(group * LANES, group * LANES + edge)
    logs, deltas = combined(m[:, LOW], t[:, HIGH], count)
    for head in range(count):
        row, lanes = slice(head, head + 1), lanes_of(head)
        weights, grad = gradients(s_ref[head, :, here], d_ref[head, :, here], logs[row], deltas[row])
        dq_ref[:, lanes] = dot(grad, every_key(k_ref, lat_refs, head), (0, 0)) * SCORE_SCALE
        for part, (own_low, halo_low, own_ref) in enumerate(((grad, l_ref, q_ref), (weights, p_ref, g_ref))):
            own_rows = own_ref[here, lanes]
            both = jnp.concatenate([own_rows, halo_head(halo_ref, edge, part, head)], axis=0)
            met = jnp.concatenate([own_low[near], own_low[own:]], axis=0)
            met = dot(jnp.concatenate([met, halo_low[head]], axis=1), both, (1, 0))
            apart = [] if group == 0 else [dot(own_low[: group * LANES], own_rows, (1, 0))]
            apart.append(dot(own_low[near.stop : own], own_rows, (1, 0)))
            use(part, head, lanes, jnp.concatenate(apart[:-1] + [met[:edge], apart[-1]], axis=0), met[edge:])


def first_grads(group, operands, rows, cols, count):
    own, keys, width = rows * cols, (rows + 2 * RADIUS) * cols, count * HEAD_DIM

    def kernel(*refs):
        *refs, dq_ref, dk_ref, dv_ref = refs

        def use(part, head, lanes, inside, outside):
            result = (dk_ref, dv_ref)[part]
            result[:own, lanes] = inside
            result[own:, lanes] = outside

        group_grads(group, refs, dq_ref, use, rows, cols, count)

    return call(kernel, "first_grads", operands, [full(LANES, width)] + [full(keys, width)] * 2)


def second_grads(group, operands, key_part, value_part, rows, cols, count):
    own, width, edge = rows * cols, count * HEAD_DIM, RADIUS * cols

    def kernel(*refs):
        *refs, kpart, vpart, dq_ref, dk_ref, dv_ref, out_0, out_1 = refs

        def use(part, head, lanes, inside, outside):
            before, result, scale = ((kpart, dk_ref, SCORE_SCALE), (vpart, dv_ref, 1.0))[part]
            result[:, lanes] = (inside + before[:own, lanes]) * scale
            outside = (outside + before[own:, lanes]) * scale
            for slot, out in enumerate((out_0, out_1)):
                out[part * edge : (part + 1) * edge, lanes] = outside[
                    slot * edge : (slot + 1) * edge
                ].astype(jnp.bfloat16)

        group_grads(group, refs, dq_ref, use, rows, cols, count)

    return call(
        kernel, "second_grads", (*operands, key_part, value_part),
        [full(LANES, width)] + [full(own, width)] * 2 + [low(2 * edge, width)] * 2,
    )


def restore(rows, cols):
    own = rows * cols
    row, col = own_query_cell(across(own), rows, cols)
    return jnp.where(down(own) == row * cols + col, 1.0, 0.0).astype(jnp.bfloat16)


def finish_queries(grads, back, rows, cols, count):
    own, edge, width = rows * cols, rows * RADIUS, count * HEAD_DIM

    def kernel(g_0, g_1, b_0, b_1, out, total):
        order = restore(rows, cols)
        for group, (grad, arrived) in enumerate(((g_0, b_0), (g_1, b_1))):
            at = group * LANES
            total[at : at + edge, :] = (grad[:edge, :] + arrived[...].astype(jnp.float32)).astype(jnp.bfloat16)
            total[at + edge : at + LANES, :] = grad[edge:, :].astype(jnp.bfloat16)
        for at in range(0, width, 256):
            lanes = slice(at, at + 256)
            out[:, lanes] = dot(order, total[:, lanes], (1, 0)).astype(jnp.bfloat16)

    return call(
        kernel, "finish_queries", (*grads, *back), [low(own, width)],
        [pltpu.VMEM((own, width), jnp.bfloat16)], flops=1 << 36,
    )[0]


def finish_keys(key_grad, value_grad, back, rows, cols, count):
    own, width, edge = rows * cols, count * HEAD_DIM, RADIUS * cols

    def kernel(dk_ref, dv_ref, b_0, b_1, out_k, out_v):
        order = restore(rows, cols)
        row, col = own_query_cell(down(own), rows, cols)
        position = across(2 * edge)
        starts = [slot_side("lat", slot) * (own - edge) for slot in (0, 1)]
        cell = jnp.where(position < edge, position + starts[0], position - edge + starts[1])
        spread = jnp.where(row * cols + col == cell, 1.0, 0.0).astype(jnp.bfloat16)
        for part, (grad, out) in enumerate(((dk_ref, out_k), (dv_ref, out_v))):
            piece = slice(part * edge, (part + 1) * edge)
            for at in range(0, width, BLOCK):
                lanes = slice(at, at + BLOCK)
                arrived = jnp.concatenate([b_0[piece, lanes], b_1[piece, lanes]], axis=0)
                total = (grad[:, lanes] + dot(spread, arrived, (1, 0))).astype(jnp.bfloat16)
                out[:, lanes] = dot(order, total, (1, 0)).astype(jnp.bfloat16)

    return call(kernel, "finish_keys", (key_grad, value_grad, *back), [low(own, width)] * 2)


def swap(axis, slot, wrap, array):
    count = lax.axis_size(axis)
    pairs = []
    for lower in range(slot, count if wrap else count - 1, 2):
        upper = (lower + 1) % count
        pairs += [(lower, upper), (upper, lower)]
    return lax.ppermute(array, axis, pairs)


def swap_lon(slot, array):
    return swap("lon", 1 - slot, True, array)


def swap_lat(slot, array):
    return swap("lat", 1 - slot, False, array)


def after(value, *earlier):
    return lax.optimization_barrier((value, *earlier))[0]


def held(value, flops=1 << 36):
    spec = pl.BlockSpec(memory_space=pl.ANY)
    return call(
        lambda src, dst: None, "held", (value,), [jax.ShapeDtypeStruct(value.shape, value.dtype)],
        flops=flops, aliases={0: 0}, ins=[spec], outs=[spec],
    )[0]


def shards(queries, key_field, value_field, out_grad):
    rows, cols, width = queries.shape
    own = rows * cols
    flat = lambda x: x.reshape(own, width)
    queries, key_field, value_field, out_grad = map(flat, (queries, key_field, value_field, out_grad))
    size = (rows, cols, width // HEAD_DIM)

    qp, gp, *sends, key_field, value_field = pack_queries(queries, out_grad, key_field, value_field, *size)
    halo = [swap_lon(slot, send) for slot, send in enumerate(sends)]
    kp, vp, *sends = pack_keys(key_field, value_field, rows, cols)
    lat = [swap_lat(place & 1, send) for place, send in enumerate(sends)]
    own_stat, own_s, own_d = own_stats(qp, gp, kp, vp, lat, *size)

    def stats(group):
        mine, s, d = halo_stats(group, halo[group], own_stat, kp, vp, lat, *size)
        return mine, swap_lon(group, mine), s, d

    def query_grad(group, mine, theirs, s, d):
        return halo_query_grad(group, mine, theirs, s, d, kp, lat[:2], *size)

    def operands(group, mine, theirs, low_weights, low_grad):
        return (qp, gp, halo[group], mine, theirs, own_s, own_d, low_weights, low_grad, kp, *lat[:2])

    first, second = FIRST, 1 - FIRST
    dq, back = [None, None], [None, None]
    halo[first] = held(after(halo[first], own_stat))
    mine_a, theirs_a, s, d = stats(first)
    result, *lows_a = query_grad(first, mine_a, theirs_a, s, d)
    back[first] = held(swap_lon(first, result))
    halo[second] = held(after(halo[second], result))
    mine_b, theirs_b, s, d = stats(second)
    dq[first], key_part, value_part = first_grads(first, operands(first, mine_a, theirs_a, *lows_a), *size)
    result, *lows_b = query_grad(second, mine_b, after(theirs_b, key_part), s, d)
    back[second] = swap_lon(second, result)
    dq[second], dk, dv, *lat_back = second_grads(
        second, operands(second, mine_b, theirs_b, *lows_b), after(key_part, back[first]), value_part, *size
    )
    lat_back = [swap_lat(slot, send) for slot, send in enumerate(lat_back)]
    grad_query = finish_queries(dq, back, *size)
    grad_key, grad_value = finish_keys(dk, dv, lat_back, *size)
    shape = (rows, cols, width)
    return tuple(x.reshape(shape) for x in (grad_query, grad_key, grad_value))


def solution(mesh):
    spec = P("lat", "lon", None)
    return jax.shard_map(
        shards, mesh=mesh, in_specs=(spec,) * 4, out_specs=(spec,) * 3, check_vma=False
    )
```

time: 62.9 us -> 54.4 us (0.86)
  local copies, waits for them, and re-layouts: 4.34 us -> 0 us
  starting transfers between devices: 22 us -> 17.8 us
  Pallas kernels: 11.6 us -> 13.5 us
  waiting for transfers between devices: 23.9 us -> 22.2 us
    unnamed x8 -> x0, local copies, waits for them, and re-layouts: 4.34 us -> none
    ppermute x10 -> x12, starting transfers between devices: 22 us -> 17.8 us  [swap(): return lax.ppermute(array, axis, pairs)]
    pallas_call x8 -> x14, Pallas kernels: 11.6 us -> 13.5 us  [call(): pl.pallas_call(kernel, name=name, in_specs=ins or [VMEM_SPEC] * len(opera...]
    ppermute x10 -> x12, waiting for transfers between devices: 23.9 us -> 22.2 us  [swap(): return lax.ppermute(array, axis, pairs)]
  transfers between devices with their start and end apart: 10 -> 12, of which waited for: 4 -> 7; matrix products, arithmetic and copies ran while one was open for 0% -> 0% of each run, Pallas kernels for 6% -> 18%
where the time goes in v3:
time: 54.4 us; the launch traced here: 54.3 us
  waiting for transfers between devices  22.2 us (41%)
  starting transfers between devices  17.8 us (33%)
  Pallas kernels  13.5 us (25%)
  between operations  0.78 us (1%)
    ppermute x12, waiting for transfers between devices, swap(): return lax.ppermute(array, axis, pairs)  22.2 us
    ppermute x12, starting transfers between devices, swap(): return lax.ppermute(array, axis, pairs)  17.8 us
    pallas_call x14, Pallas kernels, call(): pl.pallas_call(kernel, name=name, in_specs=ins or [VMEM_SPEC] * len(opera...  13.5 us
  transfers between devices with their start and end apart: 12, of which 7 were waited for; matrix products, arithmetic and copies ran while one was open for 0% of the time, Pallas kernels for 18%

profile of v3, /device:TPU:1, one launch (start us, length us, event | category | flops | bytes accessed | tf_op | source)
XLA Modules:
  0.0 54.3 jit_solution(13039441740006068410)
XLA Ops:
  0.6 1.9 %pack_queries.1 = (bf16[256,1280]{1,0:T(8,128)(2,1)S(1)}, bf16[256,1280]{1,0:T(8,128)(2,1)S(1)}, bf16[192,1280]{1,0:T(8,128)(2,1)S(1)}, bf16[192,1280]{1,0:T(8,1...) custom-call(bf16[256,1280]{1,0:T(8,128)(2,1)} %bitcast.7, bf16[256,1280]{1,0:T(8,128)(2,1)} %bitcast.8, ...), custom_call_target="tpu_custom_call" | custom-call | tf_op jit(solution)/shard_map/pack_queries/pallas_call | solution.py:92
  2.5 5.2 %collective-permute-start = (bf16[192,1280]{1,0:T(8,128)(2,1)S(1)}, bf16[192,1280]{1,0:T(8,128)(2,1)S(1)}, u32[]{:S(2)}, u32[]{:S(2)}) collective-permute-start(bf16[192,1280]{1,0:T(8,128)(2,1)S(1)} %get-tuple-element.46), channel_id=1, source_target_pairs={{1,2},{2,1},{3,4},{4,3},{5,6},{6,5},{7,0},{0,7},{9,10},{10,9},{11,... | collective-permute-start | bytes 1474568 | tf_op jit(solution)/shard_map/ppermute | solution.py:416
  7.7 0.5 %pack_keys.1 = (bf16[256,1280]{1,0:T(8,128)(2,1)S(1)}, bf16[256,1280]{1,0:T(8,128)(2,1)S(1)}, bf16[96,1280]{1,0:T(8,128)(2,1)S(1)}, bf16[96,1280]{1,0:T(8,128)(2...) custom-call(bf16[256,1280]{1,0:T(8,128)(2,1)S(1)} %get-tuple-element.47.k_ref, ...), custom_call_target="tpu_custom_call" | custom-call | tf_op jit(solution)/shard_map/pack_keys/pallas_call | solution.py:92
  8.2 4.0 %collective-permute-start.1 = (bf16[96,1280]{1,0:T(8,128)(2,1)S(1)}, bf16[96,1280]{1,0:T(8,128)(2,1)S(1)}, u32[]{:S(2)}, u32[]{:S(2)}) collective-permute-start(bf16[96,1280]{1,0:T(8,128)(2,1)S(1)} %get-tuple-element.51), channel_id=1, source_target_pairs={{8,16},{16,8},{9,17},{17,9},{10,18},{18,10},{11,19},{19,11},{12,20... | collective-permute-start | bytes 737288 | tf_op jit(solution)/shard_map/ppermute | solution.py:416
  12.2 0.1 collective-permute-start.2
  12.3 1.9 %collective-permute-start.3 = (bf16[96,1280]{1,0:T(8,128)(2,1)S(1)}, bf16[96,1280]{1,0:T(8,128)(2,1)S(1)}, u32[]{:S(2)}, u32[]{:S(2)}) collective-permute-start(bf16[96,1280]{1,0:T(8,128)(2,1)S(1)} %get-tuple-element.53), channel_id=1, source_target_pairs={{8,16},{16,8},{9,17},{17,9},{10,18},{18,10},{11,19},{19,11},{12,20... | collective-permute-start | bytes 737288 | tf_op jit(solution)/shard_map/ppermute | solution.py:416
  14.2 0.1 collective-permute-start.4
  14.3 2.1 %collective-permute-done.1.k_0.lat_0.refs_10_ = bf16[96,1280]{1,0:T(8,128)(2,1)S(1)} collective-permute-done((bf16[96,1280]{1,0:T(8,128)(2,1)S(1)}, bf16[96,1280]{1,0:T(8,128)(2,1)S(1)}, u32[]{:S(2)}, u32[]{:S(2)}) %collective-permute-start.1) | collective-permute-done | bytes 245792 | tf_op jit(solution)/shard_map/ppermute | solution.py:416
  16.4 0.0 collective-permute-start.6
  16.4 0.0 collective-permute-done.2.k_1.lat_1.refs_11_
  16.4 3.7 %collective-permute-done.3.v_0 = bf16[96,1280]{1,0:T(8,128)(2,1)S(1)} collective-permute-done((bf16[96,1280]{1,0:T(8,128)(2,1)S(1)}, bf16[96,1280]{1,0:T(8,128)(2,1)S(1)}, u32[]{:S(2)}, u32[]{:S(2)}) %collective-permute-start.3) | collective-permute-done | bytes 245792 | tf_op jit(solution)/shard_map/ppermute | solution.py:416
  20.1 0.0 collective-permute-done.4.v_1
  20.1 2.0 %own_stats.1 = (f32[24,256]{1,0:T(8,128)S(1)}, f32[10,448,256]{2,1,0:T(8,128)S(1)}, f32[10,448,256]{2,1,0:T(8,128)S(1)}) custom-call(bf16[256,1280]{1,0:T(8,128)(2,1)S(1)} %get-tuple-element.44.q_ref.refs_0_, bf16[256,1280]{1,0:T(8,128)(2,1)S(1)} %get-tuple-element.45.g_ref.refs_1_, bf16[256,1280]{1,0:T(8,128)(2,1)S(1)} %get-tuple-element.49.k_ref.refs_9_, ...), custom_call_target="tpu_custom_call" | custom-call | tf_op jit(solution)/shard_map/own_stats/pallas_call | solution.py:92
  22.1 0.0 collective-permute-done.src
  22.1 0.7 %halo_stats_0.1 = (f32[24,256]{1,0:T(8,128)S(1)}, f32[10,288,128]{2,1,0:T(8,128)S(1)}, f32[10,288,128]{2,1,0:T(8,128)S(1)}) custom-call(bf16[192,1280]{1,0:T(8,128)(2,1)S(1)} %held.3.halo_ref.refs_2_, f32[24,256]{1,0:T(8,128)S(1)} %get-tuple-element.55.stat, bf16[256,1280]{1,0:T(8,128)(2,1)S(1)} %get-tuple-element.49.k_ref.refs_9_, ...), custom_call_target="tpu_custom_call" | custom-call | tf_op jit(solution)/shard_map/halo_stats_0/pallas_call | solution.py:92
  22.8 0.4 collective-permute-start.5
  23.2 5.2 %collective-permute-done.5.t.refs_4_ = f32[24,256]{1,0:T(8,128)S(1)} collective-permute-done((f32[24,256]{1,0:T(8,128)S(1)}, f32[24,256]{1,0:T(8,128)S(1)}, u32[]{:S(2)}, u32[]{:S(2)}) %collective-permute-start.5) | collective-permute-done | bytes 24608 | tf_op jit(solution)/shard_map/ppermute | solution.py:416
  28.4 0.5 %halo_query_grad_0.1 = (bf16[96,1280]{1,0:T(8,128)(2,1)S(1)}, bf16[10,288,128]{2,1,0:T(8,128)(2,1)S(1)}, bf16[10,288,128]{2,1,0:T(8,128)(2,1)S(1)}) custom-call(f32[24,256]{1,0:T(8,128)S(1)} %get-tuple-element.57.m.refs_3_, f32[24,256]{1,0:T(8,128)S(1)} %collective-permute-done.5.t.refs_4_, f32[10,288,128]{2,1,0:T(8,128)S(1)} %get-tuple-element.60.s_ref, ...), custom_call_target="tpu_custom_call" | custom-call | tf_op jit(solution)/shard_map/halo_query_grad_0/pallas_call | solution.py:92
  28.9 0.4 collective-permute-start.8
  29.3 3.6 %collective-permute-done.6.src = bf16[192,1280]{1,0:T(8,128)(2,1)S(1)} collective-permute-done((bf16[192,1280]{1,0:T(8,128)(2,1)S(1)}, bf16[192,1280]{1,0:T(8,128)(2,1)S(1)}, u32[]{:S(2)}, u32[]{:S(2)}) %collective-permute-start.6) | collective-permute-done | bytes 491552 | tf_op jit(solution)/shard_map/ppermute | solution.py:416
  32.9 0.7 %halo_stats_1.1 = (f32[24,256]{1,0:T(8,128)S(1)}, f32[10,288,128]{2,1,0:T(8,128)S(1)}, f32[10,288,128]{2,1,0:T(8,128)S(1)}) custom-call(bf16[192,1280]{1,0:T(8,128)(2,1)S(1)} %held.4.halo_ref.refs_2_, f32[24,256]{1,0:T(8,128)S(1)} %get-tuple-element.55.stat, bf16[256,1280]{1,0:T(8,128)(2,1)S(1)} %get-tuple-element.49.k_ref.refs_9_, ...), custom_call_target="tpu_custom_call" | custom-call | tf_op jit(solution)/shard_map/halo_stats_1/pallas_call | solution.py:92
  33.6 2.0 %collective-permute-start.7 = (f32[24,256]{1,0:T(8,128)S(1)}, f32[24,256]{1,0:T(8,128)S(1)}, u32[]{:S(2)}, u32[]{:S(2)}) collective-permute-start(f32[24,256]{1,0:T(8,128)S(1)} %get-tuple-element.68.m.refs_3_), channel_id=1, source_target_pairs={{0,1},{1,0},{2,3},{3,2},{4,5},{5,4},{6,7},{7,6},{8,9},{9,8},{10,11... | collective-permute-start | bytes 73736 | tf_op jit(solution)/shard_map/ppermute | solution.py:416
  35.6 1.6 %first_grads.1 = (f32[128,1280]{1,0:T(8,128)S(1)}, f32[448,1280]{1,0:T(8,128)S(1)}, f32[448,1280]{1,0:T(8,128)S(1)}) custom-call(bf16[256,1280]{1,0:T(8,128)(2,1)S(1)} %get-tuple-element.44.q_ref.refs_0_, bf16[256,1280]{1,0:T(8,128)(2,1)S(1)} %get-tuple-element.45.g_ref.refs_1_, bf16[192,1280]{1,0:T(8,128)(2,1)S(1)} %held.3.halo_ref.refs_2_, ...), custom_call_target="tpu_custom_call" | custom-call | tf_op jit(solution)/shard_map/first_grads/pallas_call | solution.py:92
  37.2 2.4 %collective-permute-done.7.t.refs_4_ = f32[24,256]{1,0:T(8,128)S(1)} collective-permute-done((f32[24,256]{1,0:T(8,128)S(1)}, f32[24,256]{1,0:T(8,128)S(1)}, u32[]{:S(2)}, u32[]{:S(2)}) %collective-permute-start.7) | collective-permute-done | bytes 24608 | tf_op jit(solution)/shard_map/ppermute | solution.py:416
  39.6 0.5 halo_query_grad_1.1
  40.1 0.1 collective-permute-start.9
  40.2 0.0 collective-permute-done.8.src
  40.2 1.9 %second_grads.1 = (f32[128,1280]{1,0:T(8,128)S(1)}, f32[256,1280]{1,0:T(8,128)S(1)}, f32[256,1280]{1,0:T(8,128)S(1)}, bf16[192,1280]{1,0:T(8,128)(2,1)S(1)}, bf16[192,1280]{1,0:T(8,128)(2,1)S(1)}) custom-call(bf16[256,1280]{1,0:T(8,128)(2,1)S(1)} %get-tuple-element.44.q_ref.refs_0_, bf16[256,1280]{1,0:T(8,128)(2,1)S(1)} %get-tuple-element.45.g_ref.refs_1_, ...), custom_call_target="tpu_custom_call" | custom-call | tf_op jit(solution)/shard_map/second_grads/pallas_call | solution.py:92
  42.1 3.7 %collective-permute-start.10 = (bf16[192,1280]{1,0:T(8,128)(2,1)S(1)}, bf16[192,1280]{1,0:T(8,128)(2,1)S(1)}, u32[]{:S(2)}, u32[]{:S(2)}) collective-permute-start(bf16[192,1280]{1,0:T(8,128)(2,1)S(1)} %get-tuple-element.81), channel_id=1, source_target_pairs={{8,16},{16,8},{9,17},{17,9},{10,18},{18,10},{11,19},{19,11},{12,20... | collective-permute-start | bytes 1474568 | tf_op jit(solution)/shard_map/ppermute | solution.py:416
  45.9 0.1 collective-permute-start.11
  46.0 1.3 %collective-permute-done.9.b_1 = bf16[96,1280]{1,0:T(8,128)(2,1)S(1)} collective-permute-done((bf16[96,1280]{1,0:T(8,128)(2,1)S(1)}, bf16[96,1280]{1,0:T(8,128)(2,1)S(1)}, u32[]{:S(2)}, u32[]{:S(2)}) %collective-permute-start.9) | collective-permute-done | bytes 245792 | tf_op jit(solution)/shard_map/ppermute | solution.py:416
  47.3 1.2 %finish_queries.1 = bf16[256,1280]{1,0:T(8,128)(2,1)} custom-call(f32[128,1280]{1,0:T(8,128)S(1)} %get-tuple-element.64.g_0, f32[128,1280]{1,0:T(8,128)S(1)} %get-tuple-element.77.g_1, bf16[96,1280]{1,0:T(8,128)(2,1)S(1)} %held.5.b_0, bf16[96,1280]{1,0:T(8,128)(2,1)S(1)} %collective-permute-done.9.b_1), custom_call_target="tpu_custom_call" | custom-call | flops 68719476736 | tf_op jit(solution)/shard_map/finish_queries/pallas_call | solution.py:92
  48.5 3.9 %collective-permute-done.10.b_0 = bf16[192,1280]{1,0:T(8,128)(2,1)S(1)} collective-permute-done((bf16[192,1280]{1,0:T(8,128)(2,1)S(1)}, bf16[192,1280]{1,0:T(8,128)(2,1)S(1)}, u32[]{:S(2)}, u32[]{:S(2)}) %collective-permute-start.10) | collective-permute-done | bytes 491552 | tf_op jit(solution)/shard_map/ppermute | solution.py:416
  52.4 0.0 collective-permute-done.11.b_1
  52.4 1.9 %finish_keys.1 = (bf16[256,1280]{1,0:T(8,128)(2,1)}, bf16[256,1280]{1,0:T(8,128)(2,1)}) custom-call(f32[256,1280]{1,0:T(8,128)S(1)} %get-tuple-element.79.dk_ref, f32[256,1280]{1,0:T(8,128)S(1)} %get-tuple-element.80.dv_ref, bf16[192,1280]{1,0:T(8,128)(2,1)S(1)} %collective-permute-done.10.b_0, bf16[192,1280]{1,0:T(8,128)(2,1)S(1)} %collective-permute-done.11.b_1), custom_call_target="tpu_custom_call" | custom-call | tf_op jit(solution)/shard_map/finish_keys/pallas_call | solution.py:92
  (3 shorter events, 0.0 us)
Async XLA Ops:
  2.5 19.6 %collective-permute-start = (bf16[192,1280]{1,0:T(8,128)(2,1)S(1)}, bf16[192,1280]{1,0:T(8,128)(2,1)S(1)}, u32[]{:S(2)}, u32[]{:S(2)}) collective-permute-start(bf16[192,1280]{1,0:T(8,128)(2,1)S(1)} %get-tuple-element.46), channel_id=1, source_target_pairs={{1,2},{2,1},{3,4},{4,3},{5,6},{6,5},{7,0},{0,7},{9,10},{10,9},{11,... | collective-permute-start | bytes 1474568 | tf_op jit(solution)/shard_map/ppermute | solution.py:416
  8.2 8.1 %collective-permute-start.1 = (bf16[96,1280]{1,0:T(8,128)(2,1)S(1)}, bf16[96,1280]{1,0:T(8,128)(2,1)S(1)}, u32[]{:S(2)}, u32[]{:S(2)}) collective-permute-start(bf16[96,1280]{1,0:T(8,128)(2,1)S(1)} %get-tuple-element.51), channel_id=1, source_target_pairs={{8,16},{16,8},{9,17},{17,9},{10,18},{18,10},{11,19},{19,11},{12,20... | collective-permute-start | bytes 737288 | tf_op jit(solution)/shard_map/ppermute | solution.py:416
  12.2 4.2 %collective-permute-start.2 = (bf16[96,1280]{1,0:T(8,128)(2,1)S(1)}, bf16[96,1280]{1,0:T(8,128)(2,1)S(1)}, u32[]{:S(2)}, u32[]{:S(2)}) collective-permute-start(bf16[96,1280]{1,0:T(8,128)(2,1)S(1)} %get-tuple-element.52), channel_id=1, source_target_pairs={{0,8},{8,0},{16,24},{24,16},{1,9},{9,1},{17,25},{25,17},{2,10},{10... | collective-permute-start | bytes 737288 | tf_op jit(solution)/shard_map/ppermute | solution.py:416
  12.3 7.8 %collective-permute-start.3 = (bf16[96,1280]{1,0:T(8,128)(2,1)S(1)}, bf16[96,1280]{1,0:T(8,128)(2,1)S(1)}, u32[]{:S(2)}, u32[]{:S(2)}) collective-permute-start(bf16[96,1280]{1,0:T(8,128)(2,1)S(1)} %get-tuple-element.53), channel_id=1, source_target_pairs={{8,16},{16,8},{9,17},{17,9},{10,18},{18,10},{11,19},{19,11},{12,20... | collective-permute-start | bytes 737288 | tf_op jit(solution)/shard_map/ppermute | solution.py:416
  14.2 5.9 %collective-permute-start.4 = (bf16[96,1280]{1,0:T(8,128)(2,1)S(1)}, bf16[96,1280]{1,0:T(8,128)(2,1)S(1)}, u32[]{:S(2)}, u32[]{:S(2)}) collective-permute-start(bf16[96,1280]{1,0:T(8,128)(2,1)S(1)} %get-tuple-element.54), channel_id=1, source_target_pairs={{0,8},{8,0},{16,24},{24,16},{1,9},{9,1},{17,25},{25,17},{2,10},{10... | collective-permute-start | bytes 737288 | tf_op jit(solution)/shard_map/ppermute | solution.py:416
  16.4 16.5 %collective-permute-start.6 = (bf16[192,1280]{1,0:T(8,128)(2,1)S(1)}, bf16[192,1280]{1,0:T(8,128)(2,1)S(1)}, u32[]{:S(2)}, u32[]{:S(2)}) collective-permute-start(bf16[192,1280]{1,0:T(8,128)(2,1)S(1)} %get-tuple-element.65), channel_id=1, source_target_pairs={{0,1},{1,0},{2,3},{3,2},{4,5},{5,4},{6,7},{7,6},{8,9},{9,8},{10,11... | collective-permute-start | bytes 1474568 | tf_op jit(solution)/shard_map/ppermute | solution.py:416
  22.8 5.5 %collective-permute-start.5 = (f32[24,256]{1,0:T(8,128)S(1)}, f32[24,256]{1,0:T(8,128)S(1)}, u32[]{:S(2)}, u32[]{:S(2)}) collective-permute-start(f32[24,256]{1,0:T(8,128)S(1)} %get-tuple-element.57.m.refs_3_), channel_id=1, source_target_pairs={{1,2},{2,1},{3,4},{4,3},{5,6},{6,5},{7,0},{0,7},{9,10},{10,9},{11,... | collective-permute-start | bytes 73736 | tf_op jit(solution)/shard_map/ppermute | solution.py:416
  28.9 11.2 %collective-permute-start.8 = (bf16[96,1280]{1,0:T(8,128)(2,1)S(1)}, bf16[96,1280]{1,0:T(8,128)(2,1)S(1)}, u32[]{:S(2)}, u32[]{:S(2)}) collective-permute-start(bf16[96,1280]{1,0:T(8,128)(2,1)S(1)} %get-tuple-element.66), channel_id=1, source_target_pairs={{1,2},{2,1},{3,4},{4,3},{5,6},{6,5},{7,0},{0,7},{9,10},{10,9},{11,... | collective-permute-start | bytes 737288 | tf_op jit(solution)/shard_map/ppermute | solution.py:416
  33.6 6.0 %collective-permute-start.7 = (f32[24,256]{1,0:T(8,128)S(1)}, f32[24,256]{1,0:T(8,128)S(1)}, u32[]{:S(2)}, u32[]{:S(2)}) collective-permute-start(f32[24,256]{1,0:T(8,128)S(1)} %get-tuple-element.68.m.refs_3_), channel_id=1, source_target_pairs={{0,1},{1,0},{2,3},{3,2},{4,5},{5,4},{6,7},{7,6},{8,9},{9,8},{10,11... | collective-permute-start | bytes 73736 | tf_op jit(solution)/shard_map/ppermute | solution.py:416
  40.1 7.1 %collective-permute-start.9 = (bf16[96,1280]{1,0:T(8,128)(2,1)S(1)}, bf16[96,1280]{1,0:T(8,128)(2,1)S(1)}, u32[]{:S(2)}, u32[]{:S(2)}) collective-permute-start(bf16[96,1280]{1,0:T(8,128)(2,1)S(1)} %get-tuple-element.78), channel_id=1, source_target_pairs={{0,1},{1,0},{2,3},{3,2},{4,5},{5,4},{6,7},{7,6},{8,9},{9,8},{10,11... | collective-permute-start | bytes 737288 | tf_op jit(solution)/shard_map/ppermute | solution.py:416
  42.1 10.3 %collective-permute-start.10 = (bf16[192,1280]{1,0:T(8,128)(2,1)S(1)}, bf16[192,1280]{1,0:T(8,128)(2,1)S(1)}, u32[]{:S(2)}, u32[]{:S(2)}) collective-permute-start(bf16[192,1280]{1,0:T(8,128)(2,1)S(1)} %get-tuple-element.81), channel_id=1, source_target_pairs={{8,16},{16,8},{9,17},{17,9},{10,18},{18,10},{11,19},{19,11},{12,20... | collective-permute-start | bytes 1474568 | tf_op jit(solution)/shard_map/ppermute | solution.py:416
  45.9 6.5 %collective-permute-start.11 = (bf16[192,1280]{1,0:T(8,128)(2,1)S(1)}, bf16[192,1280]{1,0:T(8,128)(2,1)S(1)}, u32[]{:S(2)}, u32[]{:S(2)}) collective-permute-start(bf16[192,1280]{1,0:T(8,128)(2,1)S(1)} %get-tuple-element.82), channel_id=1, source_target_pairs={{0,8},{8,0},{16,24},{24,16},{1,9},{9,1},{17,25},{25,17},{2,10},{10... | collective-permute-start | bytes 1474568 | tf_op jit(solution)/shard_map/ppermute | solution.py:416

commit v4 on v3

--- a/solution.py
+++ b/solution.py
@@ -464,14 +464,16 @@
     halo[first] = held(after(halo[first], own_stat))
     mine_a, theirs_a, s, d = stats(first)
     result, *lows_a = query_grad(first, mine_a, theirs_a, s, d)
-    back[first] = held(swap_lon(first, result))
-    halo[second] = held(after(halo[second], result))
+    result_a = result
+    halo[second] = held(after(halo[second], result_a))
     mine_b, theirs_b, s, d = stats(second)
+    back[first] = swap_lon(first, after(result_a, mine_b))
     dq[first], key_part, value_part = first_grads(first, operands(first, mine_a, theirs_a, *lows_a), *size)
-    result, *lows_b = query_grad(second, mine_b, after(theirs_b, key_part), s, d)
+    theirs_b = held(after(theirs_b, key_part))
+    result, *lows_b = query_grad(second, mine_b, theirs_b, s, d)
     back[second] = swap_lon(second, result)
     dq[second], dk, dv, *lat_back = second_grads(
-        second, operands(second, mine_b, theirs_b, *lows_b), after(key_part, back[first]), value_part, *size
+        second, operands(second, mine_b, theirs_b, *lows_b), key_part, value_part, *size
     )
     lat_back = [swap_lat(slot, send) for slot, send in enumerate(lat_back)]
     grad_query = finish_queries(dq, back, *size)

time: 54.4 us -> 51.9 us (0.954)
  waiting for transfers between devices: 22.2 us -> 17.6 us
  starting transfers between devices: 17.8 us -> 19.9 us
    ppermute x12, waiting for transfers between devices: 22.2 us -> 17.6 us  [swap(): return lax.ppermute(array, axis, pairs)]
    ppermute x12, starting transfers between devices: 17.8 us -> 19.9 us  [swap(): return lax.ppermute(array, axis, pairs)]
  transfers between devices with their start and end apart: 12 -> 12, of which waited for: 7 -> 6; matrix products, arithmetic and copies ran while one was open for 0% -> 0% of each run, Pallas kernels for 18% -> 17%
where the time goes in v4:
time: 51.9 us; the launch traced here: 51.7 us
  starting transfers between devices  19.9 us (38%)
  waiting for transfers between devices  17.6 us (34%)
  Pallas kernels  13.4 us (26%)
  between operations  0.79 us (2%)
    ppermute x12, starting transfers between devices, swap(): return lax.ppermute(array, axis, pairs)  19.9 us
    ppermute x12, waiting for transfers between devices, swap(): return lax.ppermute(array, axis, pairs)  17.6 us
    pallas_call x14, Pallas kernels, call(): pl.pallas_call(kernel, name=name, in_specs=ins or [VMEM_SPEC] * len(opera...  13.4 us
  transfers between devices with their start and end apart: 12, of which 6 were waited for; matrix products, arithmetic and copies ran while one was open for 0% of the time, Pallas kernels for 17%

profile of v4, /device:TPU:1, one launch (start us, length us, event | category | flops | bytes accessed | tf_op | source)
XLA Modules:
  0.0 51.7 jit_solution(7912128240917321881)
XLA Ops:
  0.6 1.9 %pack_queries.1 = (bf16[256,1280]{1,0:T(8,128)(2,1)S(1)}, bf16[256,1280]{1,0:T(8,128)(2,1)S(1)}, bf16[192,1280]{1,0:T(8,128)(2,1)S(1)}, bf16[192,1280]{1,0:T(8,1...) custom-call(bf16[256,1280]{1,0:T(8,128)(2,1)} %bitcast.7, bf16[256,1280]{1,0:T(8,128)(2,1)} %bitcast.8, ...), custom_call_target="tpu_custom_call" | custom-call | tf_op jit(solution)/shard_map/pack_queries/pallas_call | solution.py:92
  2.5 5.2 %collective-permute-start = (bf16[192,1280]{1,0:T(8,128)(2,1)S(1)}, bf16[192,1280]{1,0:T(8,128)(2,1)S(1)}, u32[]{:S(2)}, u32[]{:S(2)}) collective-permute-start(bf16[192,1280]{1,0:T(8,128)(2,1)S(1)} %get-tuple-element.46), channel_id=1, source_target_pairs={{1,2},{2,1},{3,4},{4,3},{5,6},{6,5},{7,0},{0,7},{9,10},{10,9},{11,... | collective-permute-start | bytes 1474568 | tf_op jit(solution)/shard_map/ppermute | solution.py:416
  7.7 0.5 %pack_keys.1 = (bf16[256,1280]{1,0:T(8,128)(2,1)S(1)}, bf16[256,1280]{1,0:T(8,128)(2,1)S(1)}, bf16[96,1280]{1,0:T(8,128)(2,1)S(1)}, bf16[96,1280]{1,0:T(8,128)(2...) custom-call(bf16[256,1280]{1,0:T(8,128)(2,1)S(1)} %get-tuple-element.47.k_ref, ...), custom_call_target="tpu_custom_call" | custom-call | tf_op jit(solution)/shard_map/pack_keys/pallas_call | solution.py:92
  8.2 4.0 %collective-permute-start.1 = (bf16[96,1280]{1,0:T(8,128)(2,1)S(1)}, bf16[96,1280]{1,0:T(8,128)(2,1)S(1)}, u32[]{:S(2)}, u32[]{:S(2)}) collective-permute-start(bf16[96,1280]{1,0:T(8,128)(2,1)S(1)} %get-tuple-element.51), channel_id=1, source_target_pairs={{8,16},{16,8},{9,17},{17,9},{10,18},{18,10},{11,19},{19,11},{12,20... | collective-permute-start | bytes 737288 | tf_op jit(solution)/shard_map/ppermute | solution.py:416
  12.2 0.1 collective-permute-start.2
  12.3 1.9 %collective-permute-start.3 = (bf16[96,1280]{1,0:T(8,128)(2,1)S(1)}, bf16[96,1280]{1,0:T(8,128)(2,1)S(1)}, u32[]{:S(2)}, u32[]{:S(2)}) collective-permute-start(bf16[96,1280]{1,0:T(8,128)(2,1)S(1)} %get-tuple-element.53), channel_id=1, source_target_pairs={{8,16},{16,8},{9,17},{17,9},{10,18},{18,10},{11,19},{19,11},{12,20... | collective-permute-start | bytes 737288 | tf_op jit(solution)/shard_map/ppermute | solution.py:416
  14.2 0.1 collective-permute-start.4
  14.3 2.1 %collective-permute-done.1.k_0.lat_0.refs_10_ = bf16[96,1280]{1,0:T(8,128)(2,1)S(1)} collective-permute-done((bf16[96,1280]{1,0:T(8,128)(2,1)S(1)}, bf16[96,1280]{1,0:T(8,128)(2,1)S(1)}, u32[]{:S(2)}, u32[]{:S(2)}) %collective-permute-start.1) | collective-permute-done | bytes 245792 | tf_op jit(solution)/shard_map/ppermute | solution.py:416
  16.4 0.0 collective-permute-start.6
  16.4 0.0 collective-permute-done.2.k_1.lat_1.refs_11_
  16.4 3.7 %collective-permute-done.3.v_0 = bf16[96,1280]{1,0:T(8,128)(2,1)S(1)} collective-permute-done((bf16[96,1280]{1,0:T(8,128)(2,1)S(1)}, bf16[96,1280]{1,0:T(8,128)(2,1)S(1)}, u32[]{:S(2)}, u32[]{:S(2)}) %collective-permute-start.3) | collective-permute-done | bytes 245792 | tf_op jit(solution)/shard_map/ppermute | solution.py:416
  20.1 0.0 collective-permute-done.4.v_1
  20.1 2.0 %own_stats.1 = (f32[24,256]{1,0:T(8,128)S(1)}, f32[10,448,256]{2,1,0:T(8,128)S(1)}, f32[10,448,256]{2,1,0:T(8,128)S(1)}) custom-call(bf16[256,1280]{1,0:T(8,128)(2,1)S(1)} %get-tuple-element.44.q_ref.refs_0_, bf16[256,1280]{1,0:T(8,128)(2,1)S(1)} %get-tuple-element.45.g_ref.refs_1_, bf16[256,1280]{1,0:T(8,128)(2,1)S(1)} %get-tuple-element.49.k_ref.refs_9_, ...), custom_call_target="tpu_custom_call" | custom-call | tf_op jit(solution)/shard_map/own_stats/pallas_call | solution.py:92
  22.1 0.0 collective-permute-done.src
  22.1 0.7 %halo_stats_0.1 = (f32[24,256]{1,0:T(8,128)S(1)}, f32[10,288,128]{2,1,0:T(8,128)S(1)}, f32[10,288,128]{2,1,0:T(8,128)S(1)}) custom-call(bf16[192,1280]{1,0:T(8,128)(2,1)S(1)} %held.3.halo_ref.refs_2_, f32[24,256]{1,0:T(8,128)S(1)} %get-tuple-element.55.stat, bf16[256,1280]{1,0:T(8,128)(2,1)S(1)} %get-tuple-element.49.k_ref.refs_9_, ...), custom_call_target="tpu_custom_call" | custom-call | tf_op jit(solution)/shard_map/halo_stats_0/pallas_call | solution.py:92
  22.8 0.4 collective-permute-start.5
  23.2 5.2 %collective-permute-done.5.t.refs_4_ = f32[24,256]{1,0:T(8,128)S(1)} collective-permute-done((f32[24,256]{1,0:T(8,128)S(1)}, f32[24,256]{1,0:T(8,128)S(1)}, u32[]{:S(2)}, u32[]{:S(2)}) %collective-permute-start.5) | collective-permute-done | bytes 24608 | tf_op jit(solution)/shard_map/ppermute | solution.py:416
  28.4 0.5 %halo_query_grad_0.1 = (bf16[96,1280]{1,0:T(8,128)(2,1)S(1)}, bf16[10,288,128]{2,1,0:T(8,128)(2,1)S(1)}, bf16[10,288,128]{2,1,0:T(8,128)(2,1)S(1)}) custom-call(f32[24,256]{1,0:T(8,128)S(1)} %get-tuple-element.57.m.refs_3_, f32[24,256]{1,0:T(8,128)S(1)} %collective-permute-done.5.t.refs_4_, f32[10,288,128]{2,1,0:T(8,128)S(1)} %get-tuple-element.60.s_ref, ...), custom_call_target="tpu_custom_call" | custom-call | tf_op jit(solution)/shard_map/halo_query_grad_0/pallas_call | solution.py:92
  28.9 1.5 %collective-permute-done.6.src = bf16[192,1280]{1,0:T(8,128)(2,1)S(1)} collective-permute-done((bf16[192,1280]{1,0:T(8,128)(2,1)S(1)}, bf16[192,1280]{1,0:T(8,128)(2,1)S(1)}, u32[]{:S(2)}, u32[]{:S(2)}) %collective-permute-start.6) | collective-permute-done | bytes 491552 | tf_op jit(solution)/shard_map/ppermute | solution.py:416
  30.4 0.7 %halo_stats_1.1 = (f32[24,256]{1,0:T(8,128)S(1)}, f32[10,288,128]{2,1,0:T(8,128)S(1)}, f32[10,288,128]{2,1,0:T(8,128)S(1)}) custom-call(bf16[192,1280]{1,0:T(8,128)(2,1)S(1)} %held.4.halo_ref.refs_2_, f32[24,256]{1,0:T(8,128)S(1)} %get-tuple-element.55.stat, bf16[256,1280]{1,0:T(8,128)(2,1)S(1)} %get-tuple-element.49.k_ref.refs_9_, ...), custom_call_target="tpu_custom_call" | custom-call | tf_op jit(solution)/shard_map/halo_stats_1/pallas_call | solution.py:92
  31.1 0.1 collective-permute-start.7
  31.2 4.2 %collective-permute-start.8 = (bf16[96,1280]{1,0:T(8,128)(2,1)S(1)}, bf16[96,1280]{1,0:T(8,128)(2,1)S(1)}, u32[]{:S(2)}, u32[]{:S(2)}) collective-permute-start(bf16[96,1280]{1,0:T(8,128)(2,1)S(1)} %get-tuple-element.77), channel_id=1, source_target_pairs={{1,2},{2,1},{3,4},{4,3},{5,6},{6,5},{7,0},{0,7},{9,10},{10,9},{11,... | collective-permute-start | bytes 737288 | tf_op jit(solution)/shard_map/ppermute | solution.py:416
  35.4 1.6 %first_grads.1 = (f32[128,1280]{1,0:T(8,128)S(1)}, f32[448,1280]{1,0:T(8,128)S(1)}, f32[448,1280]{1,0:T(8,128)S(1)}) custom-call(bf16[256,1280]{1,0:T(8,128)(2,1)S(1)} %get-tuple-element.44.q_ref.refs_0_, bf16[256,1280]{1,0:T(8,128)(2,1)S(1)} %get-tuple-element.45.g_ref.refs_1_, bf16[192,1280]{1,0:T(8,128)(2,1)S(1)} %held.3.halo_ref.refs_2_, ...), custom_call_target="tpu_custom_call" | custom-call | tf_op jit(solution)/shard_map/first_grads/pallas_call | solution.py:92
  37.0 0.0 collective-permute-done.7.src
  37.0 0.5 halo_query_grad_1.1
  37.6 0.1 collective-permute-start.9
  37.6 1.9 %second_grads.1 = (f32[128,1280]{1,0:T(8,128)S(1)}, f32[256,1280]{1,0:T(8,128)S(1)}, f32[256,1280]{1,0:T(8,128)S(1)}, bf16[192,1280]{1,0:T(8,128)(2,1)S(1)}, bf16[192,1280]{1,0:T(8,128)(2,1)S(1)}) custom-call(bf16[256,1280]{1,0:T(8,128)(2,1)S(1)} %get-tuple-element.44.q_ref.refs_0_, bf16[256,1280]{1,0:T(8,128)(2,1)S(1)} %get-tuple-element.45.g_ref.refs_1_, ...), custom_call_target="tpu_custom_call" | custom-call | tf_op jit(solution)/shard_map/second_grads/pallas_call | solution.py:92
  39.5 3.8 %collective-permute-start.10 = (bf16[192,1280]{1,0:T(8,128)(2,1)S(1)}, bf16[192,1280]{1,0:T(8,128)(2,1)S(1)}, u32[]{:S(2)}, u32[]{:S(2)}) collective-permute-start(bf16[192,1280]{1,0:T(8,128)(2,1)S(1)} %get-tuple-element.81), channel_id=1, source_target_pairs={{8,16},{16,8},{9,17},{17,9},{10,18},{18,10},{11,19},{19,11},{12,20... | collective-permute-start | bytes 1474568 | tf_op jit(solution)/shard_map/ppermute | solution.py:416
  43.4 0.1 collective-permute-start.11
  43.4 0.0 collective-permute-done.8.b_0
  43.4 3.7 %collective-permute-done.9.b_1 = bf16[96,1280]{1,0:T(8,128)(2,1)S(1)} collective-permute-done((bf16[96,1280]{1,0:T(8,128)(2,1)S(1)}, bf16[96,1280]{1,0:T(8,128)(2,1)S(1)}, u32[]{:S(2)}, u32[]{:S(2)}) %collective-permute-start.9) | collective-permute-done | bytes 245792 | tf_op jit(solution)/shard_map/ppermute | solution.py:416
  47.1 1.2 %finish_queries.1 = bf16[256,1280]{1,0:T(8,128)(2,1)} custom-call(f32[128,1280]{1,0:T(8,128)S(1)} %get-tuple-element.64.g_0, f32[128,1280]{1,0:T(8,128)S(1)} %get-tuple-element.76.g_1, bf16[96,1280]{1,0:T(8,128)(2,1)S(1)} %collective-permute-done.8.b_0, bf16[96,1280]{1,0:T(8,128)(2,1)S(1)} %collective-permute-done.9.b_1), custom_call_target="tpu_custom_call" | custom-call | flops 68719476736 | tf_op jit(solution)/shard_map/finish_queries/pallas_call | solution.py:92
  48.3 1.6 %collective-permute-done.10.b_0 = bf16[192,1280]{1,0:T(8,128)(2,1)S(1)} collective-permute-done((bf16[192,1280]{1,0:T(8,128)(2,1)S(1)}, bf16[192,1280]{1,0:T(8,128)(2,1)S(1)}, u32[]{:S(2)}, u32[]{:S(2)}) %collective-permute-start.10) | collective-permute-done | bytes 491552 | tf_op jit(solution)/shard_map/ppermute | solution.py:416
  49.9 0.0 collective-permute-done.11.b_1
  49.9 1.9 %finish_keys.1 = (bf16[256,1280]{1,0:T(8,128)(2,1)}, bf16[256,1280]{1,0:T(8,128)(2,1)}) custom-call(f32[256,1280]{1,0:T(8,128)S(1)} %get-tuple-element.79.dk_ref, f32[256,1280]{1,0:T(8,128)S(1)} %get-tuple-element.80.dv_ref, bf16[192,1280]{1,0:T(8,128)(2,1)S(1)} %collective-permute-done.10.b_0, bf16[192,1280]{1,0:T(8,128)(2,1)S(1)} %collective-permute-done.11.b_1), custom_call_target="tpu_custom_call" | custom-call | tf_op jit(solution)/shard_map/finish_keys/pallas_call | solution.py:92
  (3 shorter events, 0.0 us)
Async XLA Ops:
  2.5 19.6 %collective-permute-start = (bf16[192,1280]{1,0:T(8,128)(2,1)S(1)}, bf16[192,1280]{1,0:T(8,128)(2,1)S(1)}, u32[]{:S(2)}, u32[]{:S(2)}) collective-permute-start(bf16[192,1280]{1,0:T(8,128)(2,1)S(1)} %get-tuple-element.46), channel_id=1, source_target_pairs={{1,2},{2,1},{3,4},{4,3},{5,6},{6,5},{7,0},{0,7},{9,10},{10,9},{11,... | collective-permute-start | bytes 1474568 | tf_op jit(solution)/shard_map/ppermute | solution.py:416
  8.2 8.1 %collective-permute-start.1 = (bf16[96,1280]{1,0:T(8,128)(2,1)S(1)}, bf16[96,1280]{1,0:T(8,128)(2,1)S(1)}, u32[]{:S(2)}, u32[]{:S(2)}) collective-permute-start(bf16[96,1280]{1,0:T(8,128)(2,1)S(1)} %get-tuple-element.51), channel_id=1, source_target_pairs={{8,16},{16,8},{9,17},{17,9},{10,18},{18,10},{11,19},{19,11},{12,20... | collective-permute-start | bytes 737288 | tf_op jit(solution)/shard_map/ppermute | solution.py:416
  12.2 4.2 %collective-permute-start.2 = (bf16[96,1280]{1,0:T(8,128)(2,1)S(1)}, bf16[96,1280]{1,0:T(8,128)(2,1)S(1)}, u32[]{:S(2)}, u32[]{:S(2)}) collective-permute-start(bf16[96,1280]{1,0:T(8,128)(2,1)S(1)} %get-tuple-element.52), channel_id=1, source_target_pairs={{0,8},{8,0},{16,24},{24,16},{1,9},{9,1},{17,25},{25,17},{2,10},{10... | collective-permute-start | bytes 737288 | tf_op jit(solution)/shard_map/ppermute | solution.py:416
  12.3 7.8 %collective-permute-start.3 = (bf16[96,1280]{1,0:T(8,128)(2,1)S(1)}, bf16[96,1280]{1,0:T(8,128)(2,1)S(1)}, u32[]{:S(2)}, u32[]{:S(2)}) collective-permute-start(bf16[96,1280]{1,0:T(8,128)(2,1)S(1)} %get-tuple-element.53), channel_id=1, source_target_pairs={{8,16},{16,8},{9,17},{17,9},{10,18},{18,10},{11,19},{19,11},{12,20... | collective-permute-start | bytes 737288 | tf_op jit(solution)/shard_map/ppermute | solution.py:416
  14.2 5.9 %collective-permute-start.4 = (bf16[96,1280]{1,0:T(8,128)(2,1)S(1)}, bf16[96,1280]{1,0:T(8,128)(2,1)S(1)}, u32[]{:S(2)}, u32[]{:S(2)}) collective-permute-start(bf16[96,1280]{1,0:T(8,128)(2,1)S(1)} %get-tuple-element.54), channel_id=1, source_target_pairs={{0,8},{8,0},{16,24},{24,16},{1,9},{9,1},{17,25},{25,17},{2,10},{10... | collective-permute-start | bytes 737288 | tf_op jit(solution)/shard_map/ppermute | solution.py:416
  16.4 14.1 %collective-permute-start.6 = (bf16[192,1280]{1,0:T(8,128)(2,1)S(1)}, bf16[192,1280]{1,0:T(8,128)(2,1)S(1)}, u32[]{:S(2)}, u32[]{:S(2)}) collective-permute-start(bf16[192,1280]{1,0:T(8,128)(2,1)S(1)} %get-tuple-element.65), channel_id=1, source_target_pairs={{0,1},{1,0},{2,3},{3,2},{4,5},{5,4},{6,7},{7,6},{8,9},{9,8},{10,11... | collective-permute-start | bytes 1474568 | tf_op jit(solution)/shard_map/ppermute | solution.py:416
  22.8 5.5 %collective-permute-start.5 = (f32[24,256]{1,0:T(8,128)S(1)}, f32[24,256]{1,0:T(8,128)S(1)}, u32[]{:S(2)}, u32[]{:S(2)}) collective-permute-start(f32[24,256]{1,0:T(8,128)S(1)} %get-tuple-element.57.m.refs_3_), channel_id=1, source_target_pairs={{1,2},{2,1},{3,4},{4,3},{5,6},{6,5},{7,0},{0,7},{9,10},{10,9},{11,... | collective-permute-start | bytes 73736 | tf_op jit(solution)/shard_map/ppermute | solution.py:416
  31.1 5.9 %collective-permute-start.7 = (f32[24,256]{1,0:T(8,128)S(1)}, f32[24,256]{1,0:T(8,128)S(1)}, u32[]{:S(2)}, u32[]{:S(2)}) collective-permute-start(f32[24,256]{1,0:T(8,128)S(1)} %get-tuple-element.68.m.refs_3_), channel_id=1, source_target_pairs={{0,1},{1,0},{2,3},{3,2},{4,5},{5,4},{6,7},{7,6},{8,9},{9,8},{10,11... | collective-permute-start | bytes 73736 | tf_op jit(solution)/shard_map/ppermute | solution.py:416
  31.2 12.2 %collective-permute-start.8 = (bf16[96,1280]{1,0:T(8,128)(2,1)S(1)}, bf16[96,1280]{1,0:T(8,128)(2,1)S(1)}, u32[]{:S(2)}, u32[]{:S(2)}) collective-permute-start(bf16[96,1280]{1,0:T(8,128)(2,1)S(1)} %get-tuple-element.77), channel_id=1, source_target_pairs={{1,2},{2,1},{3,4},{4,3},{5,6},{6,5},{7,0},{0,7},{9,10},{10,9},{11,... | collective-permute-start | bytes 737288 | tf_op jit(solution)/shard_map/ppermute | solution.py:416
  37.6 9.5 %collective-permute-start.9 = (bf16[96,1280]{1,0:T(8,128)(2,1)S(1)}, bf16[96,1280]{1,0:T(8,128)(2,1)S(1)}, u32[]{:S(2)}, u32[]{:S(2)}) collective-permute-start(bf16[96,1280]{1,0:T(8,128)(2,1)S(1)} %get-tuple-element.78), channel_id=1, source_target_pairs={{0,1},{1,0},{2,3},{3,2},{4,5},{5,4},{6,7},{7,6},{8,9},{9,8},{10,11... | collective-permute-start | bytes 737288 | tf_op jit(solution)/shard_map/ppermute | solution.py:416
  39.5 10.3 %collective-permute-start.10 = (bf16[192,1280]{1,0:T(8,128)(2,1)S(1)}, bf16[192,1280]{1,0:T(8,128)(2,1)S(1)}, u32[]{:S(2)}, u32[]{:S(2)}) collective-permute-start(bf16[192,1280]{1,0:T(8,128)(2,1)S(1)} %get-tuple-element.81), channel_id=1, source_target_pairs={{8,16},{16,8},{9,17},{17,9},{10,18},{18,10},{11,19},{19,11},{12,20... | collective-permute-start | bytes 1474568 | tf_op jit(solution)/shard_map/ppermute | solution.py:416
  43.4 6.5 %collective-permute-start.11 = (bf16[192,1280]{1,0:T(8,128)(2,1)S(1)}, bf16[192,1280]{1,0:T(8,128)(2,1)S(1)}, u32[]{:S(2)}, u32[]{:S(2)}) collective-permute-start(bf16[192,1280]{1,0:T(8,128)(2,1)S(1)} %get-tuple-element.82), channel_id=1, source_target_pairs={{0,8},{8,0},{16,24},{24,16},{1,9},{9,1},{17,25},{25,17},{2,10},{10... | collective-permute-start | bytes 1474568 | tf_op jit(solution)/shard_map/ppermute | solution.py:416

commit v5 on v3

v5 whole, which is shorter than its diff:
```python
import math

import jax
import jax.numpy as jnp
from jax import lax
from jax.experimental import pallas as pl
from jax.experimental.pallas import tpu as pltpu
from jax.sharding import PartitionSpec as P

HEAD_DIM = 128
WINDOW = 13
RADIUS = WINDOW // 2
LANES = 128
MASKED = -1e30
LOG2E = math.log2(math.e)
VMEM_BYTES = 16 * 1024 * 1024


def split(index, width):
    if width & (width - 1) == 0:
        whole = index >> (width.bit_length() - 1)
    else:
        whole = (index * ((1 << 12) // width + 1)) >> 12
    return whole, index - whole * width


def odd(axis):
    return lax.axis_index(axis) & 1


def slot_side(axis, slot):
    parity = odd(axis)
    return parity if slot == (0 if axis == "lon" else 1) else 1 - parity


def own_query_cell(position, rows, cols):
    edge = rows * RADIUS
    group = position >> 7
    place = position & (LANES - 1)
    side = jnp.where(group == 0, slot_side("lon", 0), slot_side("lon", 1))
    row_a, col_a = split(place, RADIUS)
    inner = cols - 2 * RADIUS
    row_b, col_b = split(place - edge + (LANES - edge) * group, inner)
    at_edge = place < edge
    row = jnp.where(at_edge, row_a, row_b)
    col = jnp.where(at_edge, side * (cols - RADIUS) + col_a, RADIUS + col_b)
    return row, col


def halo_query_cell(position, rows, cols):
    edge = rows * RADIUS
    group = position >> 7
    place = position & (LANES - 1)
    side = jnp.where(group == 0, slot_side("lon", 0), slot_side("lon", 1))
    row, col = split(place, RADIUS)
    col = jnp.where(side == 1, cols, -RADIUS) + col
    col = jnp.where(place < edge, col, 1 << 12)
    return row, col


def lat_key_cell(slot, position, rows, cols):
    row, col = split(position, cols)
    return row + jnp.where(slot_side("lat", slot) == 1, rows, -RADIUS), col


def bias_of(key_cells, query_cells, rows):
    total_rows = rows * lax.axis_size("lat")
    first = rows * lax.axis_index("lat")
    key_row, key_col = key_cells
    query_row, query_col = query_cells
    start = jnp.clip(first + query_row - RADIUS, 0, total_rows - WINDOW)
    from_start = first + key_row - start
    inside = (from_start >= 0) & (from_start < WINDOW)
    inside = inside & (jnp.abs(key_col - query_col) <= RADIUS)
    return jnp.where(inside, 0.0, MASKED)


def down(count):
    return lax.broadcasted_iota(jnp.int32, (count, 1), 0)


def across(count, start=0):
    return lax.broadcasted_iota(jnp.int32, (1, count), 1) + start


def dot(a, b, contract):
    return lax.dot_general(a, b, ((contract[:1], contract[1:]), ((), ())), preferred_element_type=jnp.float32)


def call(kernel, name, operands, out_shapes, scratch=(), flops=0, aliases=None, outs=None, ins=None):
    return pl.pallas_call(
        kernel,
        name=name,
        in_specs=ins or [VMEM_SPEC] * len(operands),
        out_specs=outs or [VMEM_SPEC] * len(out_shapes),
        out_shape=out_shapes,
        scratch_shapes=scratch,
        input_output_aliases=aliases or {},
        compiler_params=pltpu.CompilerParams(vmem_limit_bytes=VMEM_BYTES),
        cost_estimate=pl.CostEstimate(flops=flops, bytes_accessed=0, transcendentals=0),
    )(*operands)


def low(*shape):
    return jax.ShapeDtypeStruct(shape, jnp.bfloat16)


def full(*shape):
    return jax.ShapeDtypeStruct(shape, jnp.float32)


def lanes_of(head, count=1):
    return slice(head * HEAD_DIM, (head + count) * HEAD_DIM)


def selection(row, col, rows, cols):
    source = across(rows * cols)
    return jnp.where(source == row * cols + col, 1.0, 0.0).astype(jnp.bfloat16)


HBM_SPEC, VMEM_SPEC = pl.BlockSpec(memory_space=pltpu.HBM), pl.BlockSpec(memory_space=pltpu.VMEM)
BLOCK = 2 * HEAD_DIM


def pack_queries(queries, out_grad, key_field, value_field, rows, cols, count):
    own, edge, width = rows * cols, rows * RADIUS, count * HEAD_DIM
    lat_edge = RADIUS * cols

    def kernel(
        q_hbm, g_hbm, k_hbm, v_hbm, qp_ref, gp_ref, send_0, send_1, k_ref, v_ref, k_0, k_1, v_0, v_1, q_ref, g_ref, sems
    ):
        copies = [
            pltpu.make_async_copy(src, dst, sems.at[i])
            for i, (src, dst) in enumerate(
                ((q_hbm, q_ref), (g_hbm, g_ref), (k_hbm, k_ref), (v_hbm, v_ref))
            )
        ]
        for copy in copies:
            copy.start()
        order = selection(*own_query_cell(down(own), rows, cols), rows, cols)
        for place, (src, dst) in enumerate(((q_ref, qp_ref), (g_ref, gp_ref))):
            copies[place].wait()
            for at in range(0, width, BLOCK):
                here = slice(at, at + BLOCK)
                moved = dot(order, src[:, here], (1, 0)).astype(jnp.bfloat16)
                dst[:, here] = moved
                for group, send in enumerate((send_0, send_1)):
                    send[place * edge : (place + 1) * edge, here] = moved[group * LANES : group * LANES + edge]
        for copy, src, sends in zip(copies[2:], (k_ref, v_ref), ((k_0, k_1), (v_0, v_1))):
            copy.wait()
            for slot, send in enumerate(sends):
                start = pl.multiple_of(slot_side("lat", slot) * (own - lat_edge), 16)
                send[...] = src[pl.ds(start, lat_edge), :]

    operands = [
        pltpu.with_memory_space_constraint(x, pltpu.HBM) for x in (queries, out_grad, key_field, value_field)
    ]
    return call(
        kernel, "pack_queries", operands,
        [low(own, width)] * 2 + [low(2 * edge, width)] * 2 + [low(own, width)] * 2 + [low(lat_edge, width)] * 4,
        [pltpu.VMEM((own, width), jnp.bfloat16)] * 2 + [pltpu.SemaphoreType.DMA((4,))],
        ins=[HBM_SPEC] * 4,
    )


def own_scores(qp, gp, key_field, value_field, rows, cols, count):
    own, width = rows * cols, key_field.shape[1]

    def kernel(q_ref, g_ref, k_ref, v_ref, kp_ref, vp_ref, out_0, out_1, s_ref, d_ref, bias):
        order = selection(*own_query_cell(down(own), rows, cols), rows, cols)
        for src, dst in ((k_ref, kp_ref), (v_ref, vp_ref)):
            for at in range(0, width, BLOCK):
                here = slice(at, at + BLOCK)
                dst[:, here] = dot(order, src[:, here], (1, 0)).astype(jnp.bfloat16)
        bias[...] = bias_of(
            own_query_cell(down(own), rows, cols), own_query_cell(across(own), rows, cols), rows
        )
        for out in (out_0, out_1):
            out[...] = jnp.zeros_like(out)
        for head in range(count):
            lanes = lanes_of(head)
            s_ref[head] = dot(kp_ref[:, lanes], q_ref[:, lanes], (1, 1)) * (SCORE_SCALE * LOG2E) + bias[...]
            d_ref[head] = dot(vp_ref[:, lanes], g_ref[:, lanes], (1, 1))
            put_stats((out_0, out_1), head, part_stats(s_ref[head], d_ref[head]), count)

    return call(
        kernel, "own_scores", (qp, gp, key_field, value_field),
        [low(own, width)] * 2 + [full(stat_rows(count), LANES)] * 2 + [full(count, own, own)] * 2,
        [pltpu.VMEM((own, own), jnp.float32)],
    )


def put_stats(outs, head, stats, count):
    for out, half in zip(outs, (LOW, HIGH)):
        for at, stat in zip((head, count + head), stats):
            out[at : at + 1, :] = stat[:, half]


def halo_head(ref, edge, part, head):
    rows = ref[part * edge : (part + 1) * edge, lanes_of(head)]
    return jnp.concatenate([rows, jnp.zeros((LANES - edge, HEAD_DIM), jnp.bfloat16)], axis=0)


def near_keys(group, own_ref, lat_refs, head):
    lanes, edge = lanes_of(head), lat_refs[0].shape[0]
    pieces = [own_ref[group * LANES : group * LANES + edge, lanes]]
    return jnp.concatenate(pieces + [ref[:, lanes] for ref in lat_refs], axis=0)


def every_key(own_ref, lat_refs, head):
    lanes = lanes_of(head)
    return jnp.concatenate([ref[:, lanes] for ref in (own_ref, *lat_refs)], axis=0)


def fill_bias(bias, own_position, queries, rows, cols):
    at, edge = own_position.shape[0], RADIUS * cols
    bias[:at, :] = bias_of(own_query_cell(own_position, rows, cols), queries, rows)
    for slot in (0, 1):
        here = slice(at + slot * edge, at + (slot + 1) * edge)
        bias[here, :] = bias_of(lat_key_cell(slot, down(edge), rows, cols), queries, rows)


LOW, HIGH = slice(0, LANES), slice(LANES, 2 * LANES)
SCORE_SCALE = 1.0 / math.sqrt(HEAD_DIM)


def part_stats(scores, weight_grad):
    peak = jnp.max(scores, axis=0, keepdims=True)
    weights = jnp.exp2(scores - peak)
    total = jnp.sum(weights, axis=0, keepdims=True)
    dotted = jnp.sum(weights * weight_grad, axis=0, keepdims=True)
    return peak + jnp.log(total) * LOG2E, dotted / total


def stat_rows(count):
    return -(-2 * count // 8) * 8


def lat_scores(qp, gp, lat, stats, rows, cols, count):
    own, lat_edge = rows * cols, RADIUS * cols

    def kernel(q_ref, g_ref, k_0, k_1, v_0, v_1, before_0, before_1, out_0, out_1, s_ref, d_ref, bias, part_0, part_1):
        queries = own_query_cell(across(own), rows, cols)
        for slot in (0, 1):
            cells = lat_key_cell(slot, down(lat_edge), rows, cols)
            bias[slot * lat_edge : (slot + 1) * lat_edge, :] = bias_of(cells, queries, rows)
        for head in range(count):
            lanes = lanes_of(head)
            key, value = (
                jnp.concatenate([ref[:, lanes] for ref in pair], axis=0) for pair in ((k_0, k_1), (v_0, v_1))
            )
            s_ref[head] = dot(key, q_ref[:, lanes], (1, 1)) * (SCORE_SCALE * LOG2E) + bias[...]
            d_ref[head] = dot(value, g_ref[:, lanes], (1, 1))
            put_stats((part_0, part_1), head, part_stats(s_ref[head], d_ref[head]), count)
        for out, part, before in ((out_0, part_0, before_0), (out_1, part_1, before_1)):
            out[...] = jnp.zeros_like(out)
            out[:count, :], out[count : 2 * count, :] = stats_of(part, before, count)

    return call(
        kernel, "lat_scores", (qp, gp, *lat, *stats),
        [full(stat_rows(count), LANES)] * 2 + [full(count, 2 * lat_edge, own)] * 2,
        [pltpu.VMEM((2 * lat_edge, own), jnp.float32)] + [pltpu.VMEM((stat_rows(count), LANES), jnp.float32)] * 2,
    )


def combined(mine, theirs):
    (a, delta_a), (b, delta_b) = mine, theirs
    peak = jnp.maximum(a, b)
    part_a, part_b = jnp.exp2(a - peak), jnp.exp2(b - peak)
    total = part_a + part_b
    return peak + jnp.log(total) * LOG2E, (part_a * delta_a + part_b * delta_b) / total


def halo_grads(group, halo, theirs, kp, vp, lat, rows, cols, count, pad=0):
    edge = RADIUS * rows
    near = edge + 2 * RADIUS * cols

    def kernel(halo_ref, stat, k_ref, v_ref, k_0, k_1, v_0, v_1, out, mine, p_ref, g_ref, bias, s_ref, d_ref):
        queries = halo_query_cell(across(LANES, group * LANES), rows, cols)
        fill_bias(bias, down(edge) + group * LANES, queries, rows, cols)
        mine[...] = jnp.zeros_like(mine)
        for head in range(count):
            key = near_keys(group, k_ref, (k_0, k_1), head)
            value = near_keys(group, v_ref, (v_0, v_1), head)
            s_ref[head] = dot(key, halo_head(halo_ref, edge, 0, head), (1, 1)) * (SCORE_SCALE * LOG2E) + bias[...]
            d_ref[head] = dot(value, halo_head(halo_ref, edge, 1, head), (1, 1))
            log_total, delta = part_stats(s_ref[head], d_ref[head])
            mine[head : head + 1, :] = log_total
            mine[count + head : count + head + 1, :] = delta
        log_total, delta = combined(*((x[:count, :], x[count : 2 * count, :]) for x in (mine, stat)))
        for head in range(count):
            row = slice(head, head + 1)
            p_ref[head], grad = gradients(s_ref[head], d_ref[head], log_total[row], delta[row])
            g_ref[head] = grad
            query_grad = dot(grad, near_keys(group, k_ref, (k_0, k_1), head), (0, 0)) * SCORE_SCALE
            out[:, lanes_of(head)] = query_grad[:edge].astype(jnp.bfloat16)

    return call(
        kernel, f"halo_grads_{group}", (halo, theirs, kp, vp, *lat),
        [pltpu.VMEM((edge, count * HEAD_DIM), jnp.bfloat16), full(stat_rows(count) + pad, LANES)]
        + [low(count, near, LANES)] * 2,
        [pltpu.VMEM((near, LANES), jnp.float32)] + [pltpu.VMEM((count, near, LANES), jnp.float32)] * 2,
    )


def halo_scores(group, halo, own_stat, kp, vp, lat, rows, cols, count):
    edge = RADIUS * rows
    near = edge + 2 * RADIUS * cols

    def kernel(halo_ref, stat, k_ref, v_ref, k_0, k_1, v_0, v_1, out, s_ref, d_ref, bias):
        queries = halo_query_cell(across(LANES, group * LANES), rows, cols)
        fill_bias(bias, down(edge) + group * LANES, queries, rows, cols)
        out[:, LOW] = stat[...]
        out[:, HIGH] = jnp.zeros((out.shape[0], LANES), jnp.float32)
        for head in range(count):
            key = near_keys(group, k_ref, (k_0, k_1), head)
            value = near_keys(group, v_ref, (v_0, v_1), head)
            s_ref[head] = dot(key, halo_head(halo_ref, edge, 0, head), (1, 1)) * (SCORE_SCALE * LOG2E) + bias[...]
            d_ref[head] = dot(value, halo_head(halo_ref, edge, 1, head), (1, 1))
            log_total, delta = part_stats(s_ref[head], d_ref[head])
            out[head : head + 1, HIGH] = log_total
            out[count + head : count + head + 1, HIGH] = delta

    return call(
        kernel, f"halo_scores_{group}", (halo, own_stat, kp, vp, *lat),
        [full(stat_rows(count), 2 * LANES)] + [full(count, near, LANES)] * 2,
        [pltpu.VMEM((near, LANES), jnp.float32)],
    )


def halo_finish(group, mine, theirs, scores, weight_grad, kp, lat, rows, cols, count):
    edge = RADIUS * rows

    def kernel(m, t, s_ref, d_ref, k_ref, k_0, k_1, out, final, p_ref, g_ref):
        final[...] = jnp.zeros_like(final)
        logs, deltas = combined(*((x[:count, half], x[count : 2 * count, half]) for x, half in ((m, LOW), (t, HIGH))))
        final[:count, :] = logs
        final[count : 2 * count, :] = deltas
        logs, deltas = combined(*((x[:count, half], x[count : 2 * count, half]) for x, half in ((m, HIGH), (t, LOW))))
        for head in range(count):
            row = slice(head, head + 1)
            p_ref[head], grad = gradients(s_ref[head], d_ref[head], logs[row], deltas[row])
            g_ref[head] = grad
            query_grad = dot(grad, near_keys(group, k_ref, (k_0, k_1), head), (0, 0)) * SCORE_SCALE
            out[:, lanes_of(head)] = query_grad[:edge].astype(jnp.bfloat16)

    return call(
        kernel, f"halo_finish_{group}", (mine, theirs, scores, weight_grad, kp, *lat),
        [low(edge, count * HEAD_DIM), full(stat_rows(count), LANES)] + [low(count, *scores.shape[1:])] * 2,
    )


def gradients(scores, weight_grad, log_total, delta):
    weights = jnp.exp2(scores - log_total)
    return weights.astype(jnp.bfloat16), (weights * (weight_grad - delta)).astype(jnp.bfloat16)


def stats_of(mine, theirs, count):
    return combined(*((x[:count, :], x[count : 2 * count, :]) for x in (mine, theirs)))


def first_grads(qp, gp, halo, stats, scores, weight_grad, lows, kp, lat, rows, cols, count):
    own, width, edge = rows * cols, count * HEAD_DIM, RADIUS * rows
    keys = own + 2 * RADIUS * cols

    def kernel(
        q_ref, g_ref, h_ref, stat, s_own, s_lat, d_own, d_lat, p_ref, l_ref, k_ref, k_0, k_1, dq_ref, dk_ref, dv_ref
    ):
        for head in range(count):
            row, lanes = slice(head, head + 1), lanes_of(head)
            logs, deltas = stat[row, :], stat[count + head : count + head + 1, :]
            own_p, own_l = gradients(s_own[head, :, LOW], d_own[head, :, LOW], logs, deltas)
            lat_p, lat_l = gradients(s_lat[head, :, LOW], d_lat[head, :, LOW], logs, deltas)
            every = jnp.concatenate([own_l, lat_l], axis=0)
            dq_ref[:, lanes] = dot(every, every_key(k_ref, (k_0, k_1), head), (0, 0)) * SCORE_SCALE
            sides = ((own_l, lat_l, l_ref, q_ref, dk_ref), (own_p, lat_p, p_ref, g_ref, dv_ref))
            for part, (low_own, low_lat, low_halo, own_ref, result) in enumerate(sides):
                own_rows = own_ref[LOW, lanes]
                both = jnp.concatenate([own_rows, halo_head(h_ref, edge, part, head)], axis=0)
                met = jnp.concatenate([low_own[:edge], low_lat], axis=0)
                met = dot(jnp.concatenate([met, low_halo[head]], axis=1), both, (1, 0))
                result[:edge, lanes] = met[:edge]
                result[own:, lanes] = met[edge:]
                result[edge:own, lanes] = dot(low_own[edge:own], own_rows, (1, 0))

    return call(
        kernel, "first_grads", (qp, gp, halo, stats, *scores, *weight_grad, *lows, kp, *lat),
        [full(LANES, width)] + [full(keys, width)] * 2,
    )


def lat_grads(qp, gp, halo, mine, theirs, scores, weight_grad, lows, key_part, value_part, rows, cols, count):
    own, width, edge, lat_edge = rows * cols, count * HEAD_DIM, RADIUS * rows, RADIUS * cols

    def kernel(q_ref, g_ref, h_ref, m, t, s_ref, d_ref, p_ref, l_ref, kpart, vpart, out_0, out_1, final, lat_low):
        logs, deltas = stats_of(m, t, count)
        final[...] = jnp.zeros_like(final)
        final[:count, :], final[count : 2 * count, :] = logs, deltas
        for head in range(count):
            row, lanes = slice(head, head + 1), lanes_of(head)
            weights, grad = gradients(s_ref[head, :, HIGH], d_ref[head, :, HIGH], logs[row], deltas[row])
            lat_low[head] = grad
            sides = ((grad, l_ref, q_ref, kpart, SCORE_SCALE), (weights, p_ref, g_ref, vpart, 1.0))
            for part, (low_lat, low_halo, own_ref, before, scale) in enumerate(sides):
                both = jnp.concatenate([own_ref[HIGH, lanes], halo_head(h_ref, edge, part, head)], axis=0)
                met = jnp.concatenate([low_lat, low_halo[head, edge:, :]], axis=1)
                outside = ((dot(met, both, (1, 0)) + before[own:, lanes]) * scale).astype(jnp.bfloat16)
                for slot, out in enumerate((out_0, out_1)):
                    out[part * lat_edge : (part + 1) * lat_edge, lanes] = outside[
                        slot * lat_edge : (slot + 1) * lat_edge
                    ]

    return call(
        kernel, "lat_grads", (qp, gp, halo, mine, theirs, scores, weight_grad, *lows, key_part, value_part),
        [low(2 * lat_edge, width)] * 2 + [full(stat_rows(count), LANES), low(count, 2 * lat_edge, LANES)],
    )


def second_grads(qp, gp, halo, stats, lat_low, scores, weight_grad, lows, kp, lat, parts, rows, cols, count):
    own, width, edge = rows * cols, count * HEAD_DIM, RADIUS * rows

    def kernel(
        q_ref, g_ref, h_ref, stat, lat_ref, s_ref, d_ref, p_ref, l_ref, k_ref, k_0, k_1, dq_0, kpart, vpart,
        dq_ref, dk_ref, dv_ref, sums,
    ):
        near = slice(LANES, LANES + edge)
        order = restore(rows, cols)
        twice = jnp.concatenate([order, order], axis=1)

        for head in range(count):
            row, lanes = slice(head, head + 1), lanes_of(head)
            logs, deltas = stat[row, :], stat[count + head : count + head + 1, :]
            own_p, own_l = gradients(s_ref[head, :, HIGH], d_ref[head, :, HIGH], logs, deltas)
            every = jnp.concatenate([own_l, lat_ref[head]], axis=0)
            dq_1 = dot(every, every_key(k_ref, (k_0, k_1), head), (0, 0)) * SCORE_SCALE
            sums[0, :LANES, lanes], sums[0, LANES:, lanes] = dq_0[:, lanes], dq_1
            sides = ((own_l, l_ref, q_ref, kpart, SCORE_SCALE), (own_p, p_ref, g_ref, vpart, 1.0))
            for part, (low_own, low_halo, own_ref, before, scale) in enumerate(sides):
                own_rows = own_ref[HIGH, lanes]
                both = jnp.concatenate([own_rows, halo_head(h_ref, edge, part, head)], axis=0)
                met = jnp.concatenate([low_own[near], low_halo[head, :edge, :]], axis=1)
                pieces = (
                    (slice(0, LANES), dot(low_own[:LANES], own_rows, (1, 0))),
                    (near, dot(met, both, (1, 0))),
                    (slice(near.stop, own), dot(low_own[near.stop : own], own_rows, (1, 0))),
                )
                for here, piece in pieces:
                    sums[1 + part, here, lanes] = (piece + before[here, lanes]) * scale
        for place, result in enumerate((dq_ref, dk_ref, dv_ref)):
            for at in range(0, width, BLOCK):
                value = sums[place, :, at : at + BLOCK]
                high = value.astype(jnp.bfloat16)
                rest = (value - high.astype(jnp.float32)).astype(jnp.bfloat16)
                result[:, at : at + BLOCK] = dot(twice, jnp.concatenate([high, rest], axis=0), (1, 0))

    return call(
        kernel, "second_grads", (qp, gp, halo, stats, lat_low, scores, weight_grad, *lows, kp, *lat, *parts),
        [full(own, width)] * 3, [pltpu.VMEM((3, own, width), jnp.float32)],
    )


def restore(rows, cols):
    own = rows * cols
    row, col = own_query_cell(across(own), rows, cols)
    return jnp.where(down(own) == row * cols + col, 1.0, 0.0).astype(jnp.bfloat16)


def finish(query_grad, back, key_grad, value_grad, lat_back, rows, cols, count):
    own, width, edge, lat_edge = rows * cols, count * HEAD_DIM, RADIUS * rows, RADIUS * cols

    def kernel(dq_ref, b_0, b_1, dk_ref, dv_ref, a_1, a_0, out_q, out_k, out_v, done_q, done_k, done_v, sems):
        copies = []

        def write(done, out):
            copies.append(pltpu.make_async_copy(done, out, sems.at[len(copies)]))
            copies[-1].start()

        middle = slice(lat_edge, own - lat_edge)
        for part, (grad, done, out) in enumerate(((dk_ref, done_k, out_k), (dv_ref, done_v, out_v))):
            done[middle, :] = grad[middle, :].astype(jnp.bfloat16)
            for slot, arrived in enumerate((a_0, a_1)):
                start = pl.multiple_of(slot_side("lat", slot) * (own - lat_edge), 16)
                added = arrived[part * lat_edge : (part + 1) * lat_edge, :].astype(jnp.float32)
                done[pl.ds(start, lat_edge), :] = (grad[pl.ds(start, lat_edge), :] + added).astype(jnp.bfloat16)
            write(done, out)
        position = across(2 * edge)
        place = jnp.where(position < edge, position, position - edge + LANES)
        row, col = own_query_cell(place, rows, cols)
        spread = jnp.where(down(own) == row * cols + col, 1.0, 0.0).astype(jnp.bfloat16)
        for at in range(0, width, BLOCK):
            lanes = slice(at, at + BLOCK)
            arrived = jnp.concatenate([b_0[:, lanes], b_1[:, lanes]], axis=0)
            done_q[:, lanes] = (dq_ref[:, lanes] + dot(spread, arrived, (1, 0))).astype(jnp.bfloat16)
        write(done_q, out_q)
        for copy in copies:
            copy.wait()

    return call(
        kernel, "finish", (query_grad, *back, key_grad, value_grad, *lat_back), [low(own, width)] * 3,
        [pltpu.VMEM((own, width), jnp.bfloat16)] * 3 + [pltpu.SemaphoreType.DMA((3,))],
        outs=[HBM_SPEC] * 3,
    )


def swap(axis, slot, wrap, array):
    count = lax.axis_size(axis)
    pairs = []
    for lower in range(slot, count if wrap else count - 1, 2):
        upper = (lower + 1) % count
        pairs += [(lower, upper), (upper, lower)]
    return lax.ppermute(array, axis, pairs)


def swap_lon(slot, array):
    return swap("lon", 1 - slot, True, array)


def swap_lat(slot, array):
    return swap("lat", slot, False, array)


def after(value, *earlier):
    return lax.optimization_barrier((value, *earlier))[0]


def held(value, *earlier, flops=1 << 33):
    spec = pl.BlockSpec(memory_space=pl.ANY)
    return call(
        lambda *refs: None, "held", (value, *earlier), [jax.ShapeDtypeStruct(value.shape, value.dtype)],
        flops=flops, aliases={0: 0}, ins=[spec] * (1 + len(earlier)), outs=[spec],
    )[0]


def shards(queries, key_field, value_field, out_grad):
    rows, cols, width = queries.shape
    own = rows * cols
    flat = lambda x: x.reshape(own, width)
    queries, key_field, value_field, out_grad = map(flat, (queries, key_field, value_field, out_grad))
    size = (rows, cols, width // HEAD_DIM)

    qp, gp, *sends = pack_queries(queries, out_grad, key_field, value_field, *size)
    sends, (key_field, value_field), edges = sends[:2], sends[2:4], sends[4:]
    halo = [swap_lon(slot, send) for slot, send in enumerate(sends)]
    lat = [swap_lat(place & 1, edge) for place, edge in enumerate(edges)]
    kp, vp, *stats, own_s, own_d = own_scores(qp, gp, key_field, value_field, *size)
    *own_stat, lat_s, lat_d = lat_scores(qp, gp, lat, stats, *size)
    theirs_1 = swap_lon(1, own_stat[1])

    mine_0, *scores_0 = halo_scores(0, halo[0], own_stat[0], kp, vp, lat, *size)
    theirs_0 = swap_lon(0, mine_0)
    result_0, stats_0, *lows_0 = halo_finish(0, mine_0, theirs_0, *scores_0, kp, lat[:2], *size)
    dq_0, *parts = first_grads(
        qp, gp, halo[0], stats_0, (own_s, lat_s), (own_d, lat_d), lows_0, kp, lat[:2], *size
    )
    halo[1] = after(halo[1], parts[0])
    result_1, part_1, *lows_1 = halo_grads(1, halo[1], theirs_1, kp, vp, lat, *size)
    other_1 = swap_lon(1, part_1)
    result_1 = held(result_1, part_1, flops=1 << 29)
    result_0 = held(result_0, result_1, flops=1 << 29)
    back = [swap_lon(0, result_0), swap_lon(1, result_1)]
    other_1 = held(other_1)
    *lat_back, stats_1, lat_low = lat_grads(
        qp, gp, halo[1], own_stat[1], other_1, lat_s, lat_d, lows_1, *parts, *size
    )
    dq, dk, dv = second_grads(
        qp, gp, halo[1], stats_1, lat_low, own_s, own_d, lows_1, kp, lat[:2], (dq_0, *parts), *size
    )
    lat_back = [swap_lat(slot, lat_back[slot]) for slot in (1, 0)]
    outs = finish(dq, back, held(dk), dv, lat_back, *size)
    shape = (rows, cols, width)
    return tuple(x.reshape(shape) for x in outs)


def solution(mesh):
    spec = P("lat", "lon", None)
    return jax.shard_map(
        shards, mesh=mesh, in_specs=(spec,) * 4, out_specs=(spec,) * 3, check_vma=False
    )
```

time: 54.4 us -> 50.7 us (0.932)
  waiting for transfers between devices: 22.2 us -> 12.1 us
  starting transfers between devices: 17.8 us -> 23.5 us
    ppermute x12 -> x13, waiting for transfers between devices: 22.2 us -> 12.1 us  [swap(): return lax.ppermute(array, axis, pairs)]
    ppermute x12 -> x13, starting transfers between devices: 17.8 us -> 23.5 us  [swap(): return lax.ppermute(array, axis, pairs)]
  transfers between devices with their start and end apart: 12 -> 13, of which waited for: 7 -> 7; matrix products, arithmetic and copies ran while one was open for 0% -> 0% of each run, Pallas kernels for 18% -> 18%
where the time goes in v5:
time: 50.7 us; the launch traced here: 50.6 us
  starting transfers between devices  23.5 us (46%)
  Pallas kernels  13.9 us (27%)
  waiting for transfers between devices  12.1 us (24%)
  between operations  0.95 us (2%)
    ppermute x13, starting transfers between devices, swap(): return lax.ppermute(array, axis, pairs)  23.5 us
    pallas_call x14, Pallas kernels, call(): pl.pallas_call(kernel, name=name, in_specs=ins or [VMEM_SPEC] * len(opera...  13.9 us
    ppermute x13, waiting for transfers between devices, swap(): return lax.ppermute(array, axis, pairs)  12.1 us
  transfers between devices with their start and end apart: 13, of which 7 were waited for; matrix products, arithmetic and copies ran while one was open for 0% of the time, Pallas kernels for 18%

profile of v5, /device:TPU:1, one launch (start us, length us, event | category | flops | bytes accessed | tf_op | source)
XLA Modules:
  0.0 50.6 jit_solution(9406293066792183701)
XLA Ops:
  0.6 1.9 %pack_queries.1 = (bf16[256,1280]{1,0:T(8,128)(2,1)S(1)}, bf16[256,1280]{1,0:T(8,128)(2,1)S(1)}, bf16[192,1280]{1,0:T(8,128)(2,1)S(1)}, bf16[192,1280]{1,0:T(8,1...) custom-call(bf16[256,1280]{1,0:T(8,128)(2,1)} %bitcast.7, ...), custom_call_target="tpu_custom_call" | custom-call | tf_op jit(solution)/shard_map/pack_queries/pallas_call | solution.py:91
  2.6 0.1 collective-permute-start.2
  2.7 5.7 %collective-permute-start.1 = (bf16[192,1280]{1,0:T(8,128)(2,1)S(1)}, bf16[192,1280]{1,0:T(8,128)(2,1)S(1)}, u32[]{:S(2)}, u32[]{:S(2)}) collective-permute-start(bf16[192,1280]{1,0:T(8,128)(2,1)S(1)} %get-tuple-element.51), channel_id=1, source_target_pairs={{1,2},{2,1},{3,4},{4,3},{5,6},{6,5},{7,0},{0,7},{9,10},{10,9},{11,... | collective-permute-start | bytes 1474568 | tf_op jit(solution)/shard_map/ppermute | solution.py:511
  8.4 0.0 collective-permute-start
  8.4 3.3 %collective-permute-start.3 = (bf16[96,1280]{1,0:T(8,128)(2,1)S(1)}, bf16[96,1280]{1,0:T(8,128)(2,1)S(1)}, u32[]{:S(2)}, u32[]{:S(2)}) collective-permute-start(bf16[96,1280]{1,0:T(8,128)(2,1)S(1)} %get-tuple-element.53), channel_id=1, source_target_pairs={{8,16},{16,8},{9,17},{17,9},{10,18},{18,10},{11,19},{19,11},{12,20... | collective-permute-start | bytes 737288 | tf_op jit(solution)/shard_map/ppermute | solution.py:511
  11.8 0.1 collective-permute-start.4
  11.9 0.0 collective-permute-done.2.k_0
  11.9 2.2 %collective-permute-start.5 = (bf16[96,1280]{1,0:T(8,128)(2,1)S(1)}, bf16[96,1280]{1,0:T(8,128)(2,1)S(1)}, u32[]{:S(2)}, u32[]{:S(2)}) collective-permute-start(bf16[96,1280]{1,0:T(8,128)(2,1)S(1)} %get-tuple-element.55), channel_id=1, source_target_pairs={{8,16},{16,8},{9,17},{17,9},{10,18},{18,10},{11,19},{19,11},{12,20... | collective-permute-start | bytes 737288 | tf_op jit(solution)/shard_map/ppermute | solution.py:511
  14.1 1.6 %own_scores.1 = (bf16[256,1280]{1,0:T(8,128)(2,1)S(1)}, bf16[256,1280]{1,0:T(8,128)(2,1)S(1)}, f32[24,128]{1,0:T(8,128)S(1)}, f32[24,128]{1,0:T(8,128)S(1)}, f32...) custom-call(bf16[256,1280]{1,0:T(8,128)(2,1)S(1)} %get-tuple-element.48.q_ref, ...), custom_call_target="tpu_custom_call" | custom-call | tf_op jit(solution)/shard_map/own_scores/pallas_call | solution.py:91
  15.7 0.6 %collective-permute-done.3.k_1 = bf16[96,1280]{1,0:T(8,128)(2,1)S(1)} collective-permute-done((bf16[96,1280]{1,0:T(8,128)(2,1)S(1)}, bf16[96,1280]{1,0:T(8,128)(2,1)S(1)}, u32[]{:S(2)}, u32[]{:S(2)}) %collective-permute-start.3) | collective-permute-done | bytes 245792 | tf_op jit(solution)/shard_map/ppermute | solution.py:511
  16.2 0.0 collective-permute-done.4.v_0
  16.2 3.4 %collective-permute-done.5.v_1 = bf16[96,1280]{1,0:T(8,128)(2,1)S(1)} collective-permute-done((bf16[96,1280]{1,0:T(8,128)(2,1)S(1)}, bf16[96,1280]{1,0:T(8,128)(2,1)S(1)}, u32[]{:S(2)}, u32[]{:S(2)}) %collective-permute-start.5) | collective-permute-done | bytes 245792 | tf_op jit(solution)/shard_map/ppermute | solution.py:511
  19.7 1.0 %lat_scores.1 = (f32[24,128]{1,0:T(8,128)S(1)}, f32[24,128]{1,0:T(8,128)S(1)}, f32[10,192,256]{2,1,0:T(8,128)S(1)}, f32[10,192,256]{2,1,0:T(8,128)S(1)}) custom-call(bf16[256,1280]{1,0:T(8,128)(2,1)S(1)} %get-tuple-element.48.q_ref, bf16[256,1280]{1,0:T(8,128)(2,1)S(1)} %get-tuple-element.49.g_ref, bf16[96,1280]{1,0:T(8,128)(2,1)S(1)} %collective-permute-done.2.k_0, ...), custom_call_target="tpu_custom_call" | custom-call | tf_op jit(solution)/shard_map/lat_scores/pallas_call | solution.py:91
  20.6 0.0 collective-permute-done.1.halo_ref.h_ref
  20.7 0.8 %halo_scores_0.1 = (f32[24,256]{1,0:T(8,128)S(1)}, f32[10,288,128]{2,1,0:T(8,128)S(1)}, f32[10,288,128]{2,1,0:T(8,128)S(1)}) custom-call(bf16[192,1280]{1,0:T(8,128)(2,1)S(1)} %collective-permute-done.1.halo_ref.h_ref, f32[24,128]{1,0:T(8,128)S(1)} %get-tuple-element.60.stat, bf16[256,1280]{1,0:T(8,128)(2,1)S(1)} %get-tuple-element.61.k_ref, ...), custom_call_target="tpu_custom_call" | custom-call | tf_op jit(solution)/shard_map/halo_scores_0/pallas_call | solution.py:91
  21.4 3.3 %collective-permute-start.6 = (f32[24,256]{1,0:T(8,128)S(1)}, f32[24,256]{1,0:T(8,128)S(1)}, u32[]{:S(2)}, u32[]{:S(2)}) collective-permute-start(f32[24,256]{1,0:T(8,128)S(1)} %get-tuple-element.63.m), channel_id=1, source_target_pairs={{1,2},{2,1},{3,4},{4,3},{5,6},{6,5},{7,0},{0,7},{9,10},{10,9},{11,... | collective-permute-start | bytes 73736 | tf_op jit(solution)/shard_map/ppermute | solution.py:511
  24.7 0.0 collective-permute-start.7
  24.7 2.2 %collective-permute-done.6.t = f32[24,256]{1,0:T(8,128)S(1)} collective-permute-done((f32[24,256]{1,0:T(8,128)S(1)}, f32[24,256]{1,0:T(8,128)S(1)}, u32[]{:S(2)}, u32[]{:S(2)}) %collective-permute-start.6) | collective-permute-done | bytes 24608 | tf_op jit(solution)/shard_map/ppermute | solution.py:511
  27.0 0.5 %halo_finish_0.1 = (bf16[96,1280]{1,0:T(8,128)(2,1)S(1)}, f32[24,128]{1,0:T(8,128)S(1)}, bf16[10,288,128]{2,1,0:T(8,128)(2,1)S(1)}, bf16[10,288,128]{2,1,0:T(8,128)(2,1)S(1)}) custom-call(f32[24,256]{1,0:T(8,128)S(1)} %get-tuple-element.63.m, f32[24,256]{1,0:T(8,128)S(1)} %collective-permute-done.6.t, f32[10,288,128]{2,1,0:T(8,128)S(1)} %get-tuple-element.64.s_ref, ...), custom_call_target="tpu_custom_call" | custom-call | tf_op jit(solution)/shard_map/halo_finish_0/pallas_call | solution.py:91
  27.5 1.7 %first_grads.1 = (f32[128,1280]{1,0:T(8,128)S(1)}, f32[448,1280]{1,0:T(8,128)S(1)}, f32[448,1280]{1,0:T(8,128)S(1)}) custom-call(bf16[256,1280]{1,0:T(8,128)(2,1)S(1)} %get-tuple-element.48.q_ref, bf16[256,1280]{1,0:T(8,128)(2,1)S(1)} %get-tuple-element.49.g_ref, bf16[192,1280]{1,0:T(8,128)(2,1)S(1)} %collective-permute-done.1.halo_ref.h_ref, ...), custom_call_target="tpu_custom_call" | custom-call | tf_op jit(solution)/shard_map/first_grads/pallas_call | solution.py:91
  29.2 2.0 %collective-permute-done.halo_ref.h_ref = bf16[192,1280]{1,0:T(8,128)(2,1)S(1)} collective-permute-done((bf16[192,1280]{1,0:T(8,128)(2,1)S(1)}, bf16[192,1280]{1,0:T(8,128)(2,1)S(1)}, u32[]{:S(2)}, u32[]{:S(2)}) %collective-permute-start) | collective-permute-done | bytes 491552 | tf_op jit(solution)/shard_map/ppermute | solution.py:511
  31.2 0.3 collective-permute-done.7.stat
  31.4 1.4 %halo_grads_1.1 = (bf16[96,1280]{1,0:T(8,128)(2,1)S(1)}, f32[24,128]{1,0:T(8,128)S(1)}, bf16[10,288,128]{2,1,0:T(8,128)(2,1)S(1)}, bf16[10,288,128]{2,1,0:T(8,128)(2,1)S(1)}) custom-call(bf16[192,1280]{1,0:T(8,128)(2,1)S(1)} %collective-permute-done.halo_ref.h_ref, f32[24,128]{1,0:T(8,128)S(1)} %collective-permute-done.7.stat, ...), custom_call_target="tpu_custom_call" | custom-call | tf_op jit(solution)/shard_map/halo_grads_1/pallas_call | solution.py:91
  32.8 0.1 collective-permute-start.8
  32.9 1.4 %collective-permute-start.10 = (bf16[96,1280]{1,0:T(8,128)(2,1)S(1)}, bf16[96,1280]{1,0:T(8,128)(2,1)S(1)}, u32[]{:S(2)}, u32[]{:S(2)}) collective-permute-start(bf16[96,1280]{1,0:T(8,128)(2,1)S(1)} %held.5.refs_1_), channel_id=1, source_target_pairs={{0,1},{1,0},{2,3},{3,2},{4,5},{5,4},{6,7},{7,6},{8,9},{9,8},{10,11... | collective-permute-start | bytes 737288 | tf_op jit(solution)/shard_map/ppermute | solution.py:511
  34.4 1.2 %collective-permute-start.9 = (bf16[96,1280]{1,0:T(8,128)(2,1)S(1)}, bf16[96,1280]{1,0:T(8,128)(2,1)S(1)}, u32[]{:S(2)}, u32[]{:S(2)}) collective-permute-start(bf16[96,1280]{1,0:T(8,128)(2,1)S(1)} %held.6), channel_id=1, source_target_pairs={{1,2},{2,1},{3,4},{4,3},{5,6},{6,5},{7,0},{0,7},{9,10},{10,9},{11,... | collective-permute-start | bytes 737288 | tf_op jit(solution)/shard_map/ppermute | solution.py:511
  35.6 0.0 collective-permute-done.8.refs_0_
  35.6 0.8 %lat_grads.1 = (bf16[192,1280]{1,0:T(8,128)(2,1)S(1)}, bf16[192,1280]{1,0:T(8,128)(2,1)S(1)}, f32[24,128]{1,0:T(8,128)S(1)}, bf16[10,192,128]{2,1,0:T(8,128)(2,1)S(1)}) custom-call(bf16[256,1280]{1,0:T(8,128)(2,1)S(1)} %get-tuple-element.48.q_ref, bf16[256,1280]{1,0:T(8,128)(2,1)S(1)} %get-tuple-element.49.g_ref, ...), custom_call_target="tpu_custom_call" | custom-call | tf_op jit(solution)/shard_map/lat_grads/pallas_call | solution.py:91
  36.4 5.9 %collective-permute-start.11 = (bf16[192,1280]{1,0:T(8,128)(2,1)S(1)}, bf16[192,1280]{1,0:T(8,128)(2,1)S(1)}, u32[]{:S(2)}, u32[]{:S(2)}) collective-permute-start(bf16[192,1280]{1,0:T(8,128)(2,1)S(1)} %get-tuple-element.88), channel_id=1, source_target_pairs={{8,16},{16,8},{9,17},{17,9},{10,18},{18,10},{11,19},{19,11},{12,20... | collective-permute-start | bytes 1474568 | tf_op jit(solution)/shard_map/ppermute | solution.py:511
  42.3 0.1 collective-permute-start.12
  42.4 2.6 %second_grads.1 = (f32[256,1280]{1,0:T(8,128)S(1)}, f32[256,1280]{1,0:T(8,128)S(1)}, f32[256,1280]{1,0:T(8,128)S(1)}) custom-call(bf16[256,1280]{1,0:T(8,128)(2,1)S(1)} %get-tuple-element.48.q_ref, bf16[256,1280]{1,0:T(8,128)(2,1)S(1)} %get-tuple-element.49.g_ref, bf16[192,1280]{1,0:T(8,128)(2,1)S(1)} %collective-permute-done.halo_ref.h_ref, ...), custom_call_target="tpu_custom_call" | custom-call | tf_op jit(solution)/shard_map/second_grads/pallas_call | solution.py:91
  45.0 0.0 collective-permute-done.9.b_0
  45.0 0.5 collective-permute-done.10.b_1
  45.5 3.1 %collective-permute-done.11.a_1 = bf16[192,1280]{1,0:T(8,128)(2,1)S(1)} collective-permute-done((bf16[192,1280]{1,0:T(8,128)(2,1)S(1)}, bf16[192,1280]{1,0:T(8,128)(2,1)S(1)}, u32[]{:S(2)}, u32[]{:S(2)}) %collective-permute-start.11) | collective-permute-done | bytes 491552 | tf_op jit(solution)/shard_map/ppermute | solution.py:511
  48.6 0.0 collective-permute-done.12.a_0
  48.6 1.7 %finish.1 = (bf16[256,1280]{1,0:T(8,128)(2,1)}, bf16[256,1280]{1,0:T(8,128)(2,1)}, bf16[256,1280]{1,0:T(8,128)(2,1)}) custom-call(f32[256,1280]{1,0:T(8,128)S(1)} %get-tuple-element.83.dq_ref, bf16[96,1280]{1,0:T(8,128)(2,1)S(1)} %collective-permute-done.9.b_0, bf16[96,1280]{1,0:T(8,128)(2,1)S(1)} %collective-permute-done.10.b_1, ...), custom_call_target="tpu_custom_call" | custom-call | tf_op jit(solution)/shard_map/finish/pallas_call | solution.py:91
  (4 shorter events, 0.0 us)
Async XLA Ops:
  2.6 9.3 %collective-permute-start.2 = (bf16[96,1280]{1,0:T(8,128)(2,1)S(1)}, bf16[96,1280]{1,0:T(8,128)(2,1)S(1)}, u32[]{:S(2)}, u32[]{:S(2)}) collective-permute-start(bf16[96,1280]{1,0:T(8,128)(2,1)S(1)} %get-tuple-element.52), channel_id=1, source_target_pairs={{0,8},{8,0},{16,24},{24,16},{1,9},{9,1},{17,25},{25,17},{2,10},{10... | collective-permute-start | bytes 737288 | tf_op jit(solution)/shard_map/ppermute | solution.py:511
  2.7 18.0 %collective-permute-start.1 = (bf16[192,1280]{1,0:T(8,128)(2,1)S(1)}, bf16[192,1280]{1,0:T(8,128)(2,1)S(1)}, u32[]{:S(2)}, u32[]{:S(2)}) collective-permute-start(bf16[192,1280]{1,0:T(8,128)(2,1)S(1)} %get-tuple-element.51), channel_id=1, source_target_pairs={{1,2},{2,1},{3,4},{4,3},{5,6},{6,5},{7,0},{0,7},{9,10},{10,9},{11,... | collective-permute-start | bytes 1474568 | tf_op jit(solution)/shard_map/ppermute | solution.py:511
  8.4 22.7 %collective-permute-start = (bf16[192,1280]{1,0:T(8,128)(2,1)S(1)}, bf16[192,1280]{1,0:T(8,128)(2,1)S(1)}, u32[]{:S(2)}, u32[]{:S(2)}) collective-permute-start(bf16[192,1280]{1,0:T(8,128)(2,1)S(1)} %get-tuple-element.50), channel_id=1, source_target_pairs={{0,1},{1,0},{2,3},{3,2},{4,5},{5,4},{6,7},{7,6},{8,9},{9,8},{10,11... | collective-permute-start | bytes 1474568 | tf_op jit(solution)/shard_map/ppermute | solution.py:511
  8.4 7.8 %collective-permute-start.3 = (bf16[96,1280]{1,0:T(8,128)(2,1)S(1)}, bf16[96,1280]{1,0:T(8,128)(2,1)S(1)}, u32[]{:S(2)}, u32[]{:S(2)}) collective-permute-start(bf16[96,1280]{1,0:T(8,128)(2,1)S(1)} %get-tuple-element.53), channel_id=1, source_target_pairs={{8,16},{16,8},{9,17},{17,9},{10,18},{18,10},{11,19},{19,11},{12,20... | collective-permute-start | bytes 737288 | tf_op jit(solution)/shard_map/ppermute | solution.py:511
  11.8 4.5 %collective-permute-start.4 = (bf16[96,1280]{1,0:T(8,128)(2,1)S(1)}, bf16[96,1280]{1,0:T(8,128)(2,1)S(1)}, u32[]{:S(2)}, u32[]{:S(2)}) collective-permute-start(bf16[96,1280]{1,0:T(8,128)(2,1)S(1)} %get-tuple-element.54), channel_id=1, source_target_pairs={{0,8},{8,0},{16,24},{24,16},{1,9},{9,1},{17,25},{25,17},{2,10},{10... | collective-permute-start | bytes 737288 | tf_op jit(solution)/shard_map/ppermute | solution.py:511
  11.9 7.8 %collective-permute-start.5 = (bf16[96,1280]{1,0:T(8,128)(2,1)S(1)}, bf16[96,1280]{1,0:T(8,128)(2,1)S(1)}, u32[]{:S(2)}, u32[]{:S(2)}) collective-permute-start(bf16[96,1280]{1,0:T(8,128)(2,1)S(1)} %get-tuple-element.55), channel_id=1, source_target_pairs={{8,16},{16,8},{9,17},{17,9},{10,18},{18,10},{11,19},{19,11},{12,20... | collective-permute-start | bytes 737288 | tf_op jit(solution)/shard_map/ppermute | solution.py:511
  21.4 5.5 %collective-permute-start.6 = (f32[24,256]{1,0:T(8,128)S(1)}, f32[24,256]{1,0:T(8,128)S(1)}, u32[]{:S(2)}, u32[]{:S(2)}) collective-permute-start(f32[24,256]{1,0:T(8,128)S(1)} %get-tuple-element.63.m), channel_id=1, source_target_pairs={{1,2},{2,1},{3,4},{4,3},{5,6},{6,5},{7,0},{0,7},{9,10},{10,9},{11,... | collective-permute-start | bytes 73736 | tf_op jit(solution)/shard_map/ppermute | solution.py:511
  24.7 6.7 %collective-permute-start.7 = (f32[24,128]{1,0:T(8,128)S(1)}, f32[24,128]{1,0:T(8,128)S(1)}, u32[]{:S(2)}, u32[]{:S(2)}) collective-permute-start(f32[24,128]{1,0:T(8,128)S(1)} %get-tuple-element.75.m), channel_id=1, source_target_pairs={{0,1},{1,0},{2,3},{3,2},{4,5},{5,4},{6,7},{7,6},{8,9},{9,8},{10,11... | collective-permute-start | bytes 36872 | tf_op jit(solution)/shard_map/ppermute | solution.py:511
  32.8 2.8 %collective-permute-start.8 = (f32[24,128]{1,0:T(8,128)S(1)}, f32[24,128]{1,0:T(8,128)S(1)}, u32[]{:S(2)}, u32[]{:S(2)}) collective-permute-start(f32[24,128]{1,0:T(8,128)S(1)} %get-tuple-element.76.refs_1_), channel_id=1, source_target_pairs={{0,1},{1,0},{2,3},{3,2},{4,5},{5,4},{6,7},{7,6},{8,9},{9,8},{10,11... | collective-permute-start | bytes 36872 | tf_op jit(solution)/shard_map/ppermute | solution.py:511
  32.9 12.6 %collective-permute-start.10 = (bf16[96,1280]{1,0:T(8,128)(2,1)S(1)}, bf16[96,1280]{1,0:T(8,128)(2,1)S(1)}, u32[]{:S(2)}, u32[]{:S(2)}) collective-permute-start(bf16[96,1280]{1,0:T(8,128)(2,1)S(1)} %held.5.refs_1_), channel_id=1, source_target_pairs={{0,1},{1,0},{2,3},{3,2},{4,5},{5,4},{6,7},{7,6},{8,9},{9,8},{10,11... | collective-permute-start | bytes 737288 | tf_op jit(solution)/shard_map/ppermute | solution.py:511
  34.4 10.6 %collective-permute-start.9 = (bf16[96,1280]{1,0:T(8,128)(2,1)S(1)}, bf16[96,1280]{1,0:T(8,128)(2,1)S(1)}, u32[]{:S(2)}, u32[]{:S(2)}) collective-permute-start(bf16[96,1280]{1,0:T(8,128)(2,1)S(1)} %held.6), channel_id=1, source_target_pairs={{1,2},{2,1},{3,4},{4,3},{5,6},{6,5},{7,0},{0,7},{9,10},{10,9},{11,... | collective-permute-start | bytes 737288 | tf_op jit(solution)/shard_map/ppermute | solution.py:511
  36.4 12.3 %collective-permute-start.11 = (bf16[192,1280]{1,0:T(8,128)(2,1)S(1)}, bf16[192,1280]{1,0:T(8,128)(2,1)S(1)}, u32[]{:S(2)}, u32[]{:S(2)}) collective-permute-start(bf16[192,1280]{1,0:T(8,128)(2,1)S(1)} %get-tuple-element.88), channel_id=1, source_target_pairs={{8,16},{16,8},{9,17},{17,9},{10,18},{18,10},{11,19},{19,11},{12,20... | collective-permute-start | bytes 1474568 | tf_op jit(solution)/shard_map/ppermute | solution.py:511
  42.3 6.3 %collective-permute-start.12 = (bf16[192,1280]{1,0:T(8,128)(2,1)S(1)}, bf16[192,1280]{1,0:T(8,128)(2,1)S(1)}, u32[]{:S(2)}, u32[]{:S(2)}) collective-permute-start(bf16[192,1280]{1,0:T(8,128)(2,1)S(1)} %get-tuple-element.89), channel_id=1, source_target_pairs={{0,8},{8,0},{16,24},{24,16},{1,9},{9,1},{17,25},{25,17},{2,10},{10... | collective-permute-start | bytes 1474568 | tf_op jit(solution)/shard_map/ppermute | solution.py:511

commit v6 on v5

--- a/solution.py
+++ b/solution.py
@@ -359,93 +359,63 @@
     return combined(*((x[:count, :], x[count : 2 * count, :]) for x in (mine, theirs)))
 
 
-def first_grads(qp, gp, halo, stats, scores, weight_grad, lows, kp, lat, rows, cols, count):
-    own, width, edge = rows * cols, count * HEAD_DIM, RADIUS * rows
-    keys = own + 2 * RADIUS * cols
+def lat_grads(qp, gp, halo, stats_0, mine, theirs, scores, weight_grad, lows, rows, cols, count):
+    own, width, edge, lat_edge = rows * cols, count * HEAD_DIM, RADIUS * rows, RADIUS * cols
 
     def kernel(
-        q_ref, g_ref, h_ref, stat, s_own, s_lat, d_own, d_lat, p_ref, l_ref, k_ref, k_0, k_1, dq_ref, dk_ref, dv_ref
+        q_ref, g_ref, h_0, h_1, stat, m, t, s_ref, d_ref, p_0, l_0, p_1, l_1, out_0, out_1, final, lat_low
     ):
-        for head in range(count):
-            row, lanes = slice(head, head + 1), lanes_of(head)
-            logs, deltas = stat[row, :], stat[count + head : count + head + 1, :]
-            own_p, own_l = gradients(s_own[head, :, LOW], d_own[head, :, LOW], logs, deltas)
-            lat_p, lat_l = gradients(s_lat[head, :, LOW], d_lat[head, :, LOW], logs, deltas)
-            every = jnp.concatenate([own_l, lat_l], axis=0)
-            dq_ref[:, lanes] = dot(every, every_key(k_ref, (k_0, k_1), head), (0, 0)) * SCORE_SCALE
-            sides = ((own_l, lat_l, l_ref, q_ref, dk_ref), (own_p, lat_p, p_ref, g_ref, dv_ref))
-            for part, (low_own, low_lat, low_halo, own_ref, result) in enumerate(sides):
-                own_rows = own_ref[LOW, lanes]
-                both = jnp.concatenate([own_rows, halo_head(h_ref, edge, part, head)], axis=0)
-                met = jnp.concatenate([low_own[:edge], low_lat], axis=0)
-                met = dot(jnp.concatenate([met, low_halo[head]], axis=1), both, (1, 0))
-                result[:edge, lanes] = met[:edge]
-                result[own:, lanes] = met[edge:]
-                result[edge:own, lanes] = dot(low_own[edge:own], own_rows, (1, 0))
-
-    return call(
-        kernel, "first_grads", (qp, gp, halo, stats, *scores, *weight_grad, *lows, kp, *lat),
-        [full(LANES, width)] + [full(keys, width)] * 2,
-    )
-
-
-def lat_grads(qp, gp, halo, mine, theirs, scores, weight_grad, lows, key_part, value_part, rows, cols, count):
-    own, width, edge, lat_edge = rows * cols, count * HEAD_DIM, RADIUS * rows, RADIUS * cols
-
-    def kernel(q_ref, g_ref, h_ref, m, t, s_ref, d_ref, p_ref, l_ref, kpart, vpart, out_0, out_1, final, lat_low):
-        logs, deltas = stats_of(m, t, count)
         final[...] = jnp.zeros_like(final)
-        final[:count, :], final[count : 2 * count, :] = logs, deltas
-        for head in range(count):
-            row, lanes = slice(head, head + 1), lanes_of(head)
-            weights, grad = gradients(s_ref[head, :, HIGH], d_ref[head, :, HIGH], logs[row], deltas[row])
+        final[:count, :], final[count : 2 * count, :] = stats_of(m, t, count)
+        for head in range(count):
+            lanes = lanes_of(head)
+            logs, deltas = (
+                jnp.concatenate([ref[at : at + 1, :] for ref in (stat, final)], axis=1) for at in (head, count + head)
+            )
+            weights, grad = gradients(s_ref[head], d_ref[head], logs, deltas)
             lat_low[head] = grad
-            sides = ((grad, l_ref, q_ref, kpart, SCORE_SCALE), (weights, p_ref, g_ref, vpart, 1.0))
-            for part, (low_lat, low_halo, own_ref, before, scale) in enumerate(sides):
-                both = jnp.concatenate([own_ref[HIGH, lanes], halo_head(h_ref, edge, part, head)], axis=0)
-                met = jnp.concatenate([low_lat, low_halo[head, edge:, :]], axis=1)
-                outside = ((dot(met, both, (1, 0)) + before[own:, lanes]) * scale).astype(jnp.bfloat16)
+            sides = ((grad, (l_0, l_1), q_ref, SCORE_SCALE), (weights, (p_0, p_1), g_ref, 1.0))
+            for part, (low_lat, low_halo, own_ref, scale) in enumerate(sides):
+                every = [own_ref[:, lanes]] + [halo_head(h, edge, part, head) for h in (h_0, h_1)]
+                met = jnp.concatenate([low_lat] + [x[head, edge:, :] for x in low_halo], axis=1)
+                outside = (dot(met, jnp.concatenate(every, axis=0), (1, 0)) * scale).astype(jnp.bfloat16)
                 for slot, out in enumerate((out_0, out_1)):
                     out[part * lat_edge : (part + 1) * lat_edge, lanes] = outside[
                         slot * lat_edge : (slot + 1) * lat_edge
                     ]
 
     return call(
-        kernel, "lat_grads", (qp, gp, halo, mine, theirs, scores, weight_grad, *lows, key_part, value_part),
-        [low(2 * lat_edge, width)] * 2 + [full(stat_rows(count), LANES), low(count, 2 * lat_edge, LANES)],
-    )
-
-
-def second_grads(qp, gp, halo, stats, lat_low, scores, weight_grad, lows, kp, lat, parts, rows, cols, count):
+        kernel, "lat_grads", (qp, gp, *halo, stats_0, mine, theirs, scores, weight_grad, *lows[0], *lows[1]),
+        [low(2 * lat_edge, width)] * 2 + [full(stat_rows(count), LANES), low(count, 2 * lat_edge, own)],
+    )
+
+
+def own_grads(qp, gp, halo, stats, lat_low, scores, weight_grad, lows, kp, lat, rows, cols, count):
     own, width, edge = rows * cols, count * HEAD_DIM, RADIUS * rows
 
     def kernel(
-        q_ref, g_ref, h_ref, stat, lat_ref, s_ref, d_ref, p_ref, l_ref, k_ref, k_0, k_1, dq_0, kpart, vpart,
+        q_ref, g_ref, h_0, h_1, stat_0, stat_1, lat_ref, s_ref, d_ref, p_0, l_0, p_1, l_1, k_ref, k_0, k_1,
         dq_ref, dk_ref, dv_ref, sums,
     ):
-        near = slice(LANES, LANES + edge)
+        for head in range(count):
+            lanes = lanes_of(head)
+            logs, deltas = (
+                jnp.concatenate([ref[at : at + 1, :] for ref in (stat_0, stat_1)], axis=1)
+                for at in (head, count + head)
+            )
+            own_p, own_l = gradients(s_ref[head], d_ref[head], logs, deltas)
+            every = jnp.concatenate([own_l, lat_ref[head]], axis=0)
+            sums[0, :, lanes] = dot(every, every_key(k_ref, (k_0, k_1), head), (0, 0)) * SCORE_SCALE
+            sides = ((own_l, (l_0, l_1), q_ref, SCORE_SCALE), (own_p, (p_0, p_1), g_ref, 1.0))
+            for part, (low_own, low_halo, own_ref, scale) in enumerate(sides):
+                inside = dot(low_own, own_ref[:, lanes], (1, 0))
+                for group, (x, h) in enumerate(zip(low_halo, (h_0, h_1))):
+                    at = group * LANES
+                    near = inside[at : at + edge] + dot(x[head, :edge, :], halo_head(h, edge, part, head), (1, 0))
+                    sums[1 + part, at : at + edge, lanes] = near * scale
+                    sums[1 + part, at + edge : at + LANES, lanes] = inside[at + edge : at + LANES] * scale
         order = restore(rows, cols)
         twice = jnp.concatenate([order, order], axis=1)
-
-        for head in range(count):
-            row, lanes = slice(head, head + 1), lanes_of(head)
-            logs, deltas = stat[row, :], stat[count + head : count + head + 1, :]
-            own_p, own_l = gradients(s_ref[head, :, HIGH], d_ref[head, :, HIGH], logs, deltas)
-            every = jnp.concatenate([own_l, lat_ref[head]], axis=0)
-            dq_1 = dot(every, every_key(k_ref, (k_0, k_1), head), (0, 0)) * SCORE_SCALE
-            sums[0, :LANES, lanes], sums[0, LANES:, lanes] = dq_0[:, lanes], dq_1
-            sides = ((own_l, l_ref, q_ref, kpart, SCORE_SCALE), (own_p, p_ref, g_ref, vpart, 1.0))
-            for part, (low_own, low_halo, own_ref, before, scale) in enumerate(sides):
-                own_rows = own_ref[HIGH, lanes]
-                both = jnp.concatenate([own_rows, halo_head(h_ref, edge, part, head)], axis=0)
-                met = jnp.concatenate([low_own[near], low_halo[head, :edge, :]], axis=1)
-                pieces = (
-                    (slice(0, LANES), dot(low_own[:LANES], own_rows, (1, 0))),
-                    (near, dot(met, both, (1, 0))),
-                    (slice(near.stop, own), dot(low_own[near.stop : own], own_rows, (1, 0))),
-                )
-                for here, piece in pieces:
-                    sums[1 + part, here, lanes] = (piece + before[here, lanes]) * scale
         for place, result in enumerate((dq_ref, dk_ref, dv_ref)):
             for at in range(0, width, BLOCK):
                 value = sums[place, :, at : at + BLOCK]
@@ -454,7 +424,8 @@
                 result[:, at : at + BLOCK] = dot(twice, jnp.concatenate([high, rest], axis=0), (1, 0))
 
     return call(
-        kernel, "second_grads", (qp, gp, halo, stats, lat_low, scores, weight_grad, *lows, kp, *lat, *parts),
+        kernel, "own_grads",
+        (qp, gp, *halo, *stats, lat_low, scores, weight_grad, *lows[0], *lows[1], kp, *lat),
         [full(own, width)] * 3, [pltpu.VMEM((3, own, width), jnp.float32)],
     )
 
@@ -549,21 +520,17 @@
     mine_0, *scores_0 = halo_scores(0, halo[0], own_stat[0], kp, vp, lat, *size)
     theirs_0 = swap_lon(0, mine_0)
     result_0, stats_0, *lows_0 = halo_finish(0, mine_0, theirs_0, *scores_0, kp, lat[:2], *size)
-    dq_0, *parts = first_grads(
-        qp, gp, halo[0], stats_0, (own_s, lat_s), (own_d, lat_d), lows_0, kp, lat[:2], *size
-    )
-    halo[1] = after(halo[1], parts[0])
+    halo[1] = after(halo[1], result_0)
     result_1, part_1, *lows_1 = halo_grads(1, halo[1], theirs_1, kp, vp, lat, *size)
-    other_1 = swap_lon(1, part_1)
+    other_1 = held(swap_lon(1, part_1))
     result_1 = held(result_1, part_1, flops=1 << 29)
     result_0 = held(result_0, result_1, flops=1 << 29)
     back = [swap_lon(0, result_0), swap_lon(1, result_1)]
-    other_1 = held(other_1)
     *lat_back, stats_1, lat_low = lat_grads(
-        qp, gp, halo[1], own_stat[1], other_1, lat_s, lat_d, lows_1, *parts, *size
-    )
-    dq, dk, dv = second_grads(
-        qp, gp, halo[1], stats_1, lat_low, own_s, own_d, lows_1, kp, lat[:2], (dq_0, *parts), *size
+        qp, gp, halo, stats_0, own_stat[1], other_1, lat_s, lat_d, (lows_0, lows_1), *size
+    )
+    dq, dk, dv = own_grads(
+        qp, gp, halo, (stats_0, stats_1), lat_low, own_s, own_d, (lows_0, lows_1), kp, lat[:2], *size
     )
     lat_back = [swap_lat(slot, lat_back[slot]) for slot in (1, 0)]
     outs = finish(dq, back, held(dk), dv, lat_back, *size)

time: 50.7 us -> 50 us (0.986)
  starting transfers between devices: 23.5 us -> 22.2 us
  waiting for transfers between devices: 12.1 us -> 13.4 us
    ppermute x13, starting transfers between devices: 23.5 us -> 22.2 us  [swap(): return lax.ppermute(array, axis, pairs)]
    ppermute x13, waiting for transfers between devices: 12.1 us -> 13.4 us  [swap(): return lax.ppermute(array, axis, pairs)]
    pallas_call x14 -> x13, Pallas kernels: 13.9 us -> 13.4 us  [call(): pl.pallas_call(kernel, name=name, in_specs=ins or [VMEM_SPEC] * len(opera...]
  transfers between devices with their start and end apart: 13 -> 13, of which waited for: 7 -> 7; matrix products, arithmetic and copies ran while one was open for 0% -> 0% of each run, Pallas kernels for 18% -> 17%
where the time goes in v6:
time: 50 us; the launch traced here: 49.8 us
  starting transfers between devices  22.2 us (44%)
  Pallas kernels  13.4 us (27%)
  waiting for transfers between devices  13.4 us (27%)
  between operations  0.78 us (2%)
    ppermute x13, starting transfers between devices, swap(): return lax.ppermute(array, axis, pairs)  22.2 us
    ppermute x13, waiting for transfers between devices, swap(): return lax.ppermute(array, axis, pairs)  13.4 us
    pallas_call x13, Pallas kernels, call(): pl.pallas_call(kernel, name=name, in_specs=ins or [VMEM_SPEC] * len(opera...  13.4 us
  transfers between devices with their start and end apart: 13, of which 7 were waited for; matrix products, arithmetic and copies ran while one was open for 0% of the time, Pallas kernels for 17%

profile of v6, /device:TPU:1, one launch (start us, length us, event | category | flops | bytes accessed | tf_op | source)
XLA Modules:
  0.0 49.8 jit_solution(16803518896058785682)
XLA Ops:
  0.6 1.9 %pack_queries.1 = (bf16[256,1280]{1,0:T(8,128)(2,1)S(1)}, bf16[256,1280]{1,0:T(8,128)(2,1)S(1)}, bf16[192,1280]{1,0:T(8,128)(2,1)S(1)}, bf16[192,1280]{1,0:T(8,1...) custom-call(bf16[256,1280]{1,0:T(8,128)(2,1)} %bitcast.7, ...), custom_call_target="tpu_custom_call" | custom-call | tf_op jit(solution)/shard_map/pack_queries/pallas_call | solution.py:91
  2.6 0.1 collective-permute-start.2
  2.7 5.7 %collective-permute-start = (bf16[192,1280]{1,0:T(8,128)(2,1)S(1)}, bf16[192,1280]{1,0:T(8,128)(2,1)S(1)}, u32[]{:S(2)}, u32[]{:S(2)}) collective-permute-start(bf16[192,1280]{1,0:T(8,128)(2,1)S(1)} %get-tuple-element.47), channel_id=1, source_target_pairs={{1,2},{2,1},{3,4},{4,3},{5,6},{6,5},{7,0},{0,7},{9,10},{10,9},{11,... | collective-permute-start | bytes 1474568 | tf_op jit(solution)/shard_map/ppermute | solution.py:482
  8.4 0.0 collective-permute-start.1
  8.4 3.3 %collective-permute-start.3 = (bf16[96,1280]{1,0:T(8,128)(2,1)S(1)}, bf16[96,1280]{1,0:T(8,128)(2,1)S(1)}, u32[]{:S(2)}, u32[]{:S(2)}) collective-permute-start(bf16[96,1280]{1,0:T(8,128)(2,1)S(1)} %get-tuple-element.50), channel_id=1, source_target_pairs={{8,16},{16,8},{9,17},{17,9},{10,18},{18,10},{11,19},{19,11},{12,20... | collective-permute-start | bytes 737288 | tf_op jit(solution)/shard_map/ppermute | solution.py:482
  11.8 0.1 collective-permute-start.4
  11.9 0.0 collective-permute-done.2.k_0
  11.9 2.2 %collective-permute-start.5 = (bf16[96,1280]{1,0:T(8,128)(2,1)S(1)}, bf16[96,1280]{1,0:T(8,128)(2,1)S(1)}, u32[]{:S(2)}, u32[]{:S(2)}) collective-permute-start(bf16[96,1280]{1,0:T(8,128)(2,1)S(1)} %get-tuple-element.52), channel_id=1, source_target_pairs={{8,16},{16,8},{9,17},{17,9},{10,18},{18,10},{11,19},{19,11},{12,20... | collective-permute-start | bytes 737288 | tf_op jit(solution)/shard_map/ppermute | solution.py:482
  14.1 1.6 %own_scores.1 = (bf16[256,1280]{1,0:T(8,128)(2,1)S(1)}, bf16[256,1280]{1,0:T(8,128)(2,1)S(1)}, f32[24,128]{1,0:T(8,128)S(1)}, f32[24,128]{1,0:T(8,128)S(1)}, f32...) custom-call(bf16[256,1280]{1,0:T(8,128)(2,1)S(1)} %get-tuple-element.45.q_ref, ...), custom_call_target="tpu_custom_call" | custom-call | tf_op jit(solution)/shard_map/own_scores/pallas_call | solution.py:91
  15.7 0.5 %collective-permute-done.3.k_1 = bf16[96,1280]{1,0:T(8,128)(2,1)S(1)} collective-permute-done((bf16[96,1280]{1,0:T(8,128)(2,1)S(1)}, bf16[96,1280]{1,0:T(8,128)(2,1)S(1)}, u32[]{:S(2)}, u32[]{:S(2)}) %collective-permute-start.3) | collective-permute-done | bytes 245792 | tf_op jit(solution)/shard_map/ppermute | solution.py:482
  16.2 0.0 collective-permute-done.4.v_0
  16.2 3.4 %collective-permute-done.5.v_1 = bf16[96,1280]{1,0:T(8,128)(2,1)S(1)} collective-permute-done((bf16[96,1280]{1,0:T(8,128)(2,1)S(1)}, bf16[96,1280]{1,0:T(8,128)(2,1)S(1)}, u32[]{:S(2)}, u32[]{:S(2)}) %collective-permute-start.5) | collective-permute-done | bytes 245792 | tf_op jit(solution)/shard_map/ppermute | solution.py:482
  19.7 0.9 %lat_scores.1 = (f32[24,128]{1,0:T(8,128)S(1)}, f32[24,128]{1,0:T(8,128)S(1)}, f32[10,192,256]{2,1,0:T(8,128)S(1)}, f32[10,192,256]{2,1,0:T(8,128)S(1)}) custom-call(bf16[256,1280]{1,0:T(8,128)(2,1)S(1)} %get-tuple-element.45.q_ref, bf16[256,1280]{1,0:T(8,128)(2,1)S(1)} %get-tuple-element.46.g_ref, bf16[96,1280]{1,0:T(8,128)(2,1)S(1)} %collective-permute-done.2.k_0, ...), custom_call_target="tpu_custom_call" | custom-call | tf_op jit(solution)/shard_map/lat_scores/pallas_call | solution.py:91
  20.6 0.0 collective-permute-done.halo_ref.h_0
  20.6 0.8 %halo_scores_0.1 = (f32[24,256]{1,0:T(8,128)S(1)}, f32[10,288,128]{2,1,0:T(8,128)S(1)}, f32[10,288,128]{2,1,0:T(8,128)S(1)}) custom-call(bf16[192,1280]{1,0:T(8,128)(2,1)S(1)} %collective-permute-done.halo_ref.h_0, f32[24,128]{1,0:T(8,128)S(1)} %get-tuple-element.57.stat, bf16[256,1280]{1,0:T(8,128)(2,1)S(1)} %get-tuple-element.58.k_ref, ...), custom_call_target="tpu_custom_call" | custom-call | tf_op jit(solution)/shard_map/halo_scores_0/pallas_call | solution.py:91
  21.4 3.3 %collective-permute-start.6 = (f32[24,256]{1,0:T(8,128)S(1)}, f32[24,256]{1,0:T(8,128)S(1)}, u32[]{:S(2)}, u32[]{:S(2)}) collective-permute-start(f32[24,256]{1,0:T(8,128)S(1)} %get-tuple-element.60.m), channel_id=1, source_target_pairs={{1,2},{2,1},{3,4},{4,3},{5,6},{6,5},{7,0},{0,7},{9,10},{10,9},{11,... | collective-permute-start | bytes 73736 | tf_op jit(solution)/shard_map/ppermute | solution.py:482
  24.7 0.0 collective-permute-start.7
  24.7 2.2 %collective-permute-done.6.t = f32[24,256]{1,0:T(8,128)S(1)} collective-permute-done((f32[24,256]{1,0:T(8,128)S(1)}, f32[24,256]{1,0:T(8,128)S(1)}, u32[]{:S(2)}, u32[]{:S(2)}) %collective-permute-start.6) | collective-permute-done | bytes 24608 | tf_op jit(solution)/shard_map/ppermute | solution.py:482
  26.9 0.6 %halo_finish_0.1 = (bf16[96,1280]{1,0:T(8,128)(2,1)S(1)}, f32[24,128]{1,0:T(8,128)S(1)}, bf16[10,288,128]{2,1,0:T(8,128)(2,1)S(1)}, bf16[10,288,128]{2,1,0:T(8,128)(2,1)S(1)}) custom-call(f32[24,256]{1,0:T(8,128)S(1)} %get-tuple-element.60.m, f32[24,256]{1,0:T(8,128)S(1)} %collective-permute-done.6.t, f32[10,288,128]{2,1,0:T(8,128)S(1)} %get-tuple-element.61.s_ref, ...), custom_call_target="tpu_custom_call" | custom-call | tf_op jit(solution)/shard_map/halo_finish_0/pallas_call | solution.py:91
  27.5 3.7 %collective-permute-done.1.halo_ref.h_1 = bf16[192,1280]{1,0:T(8,128)(2,1)S(1)} collective-permute-done((bf16[192,1280]{1,0:T(8,128)(2,1)S(1)}, bf16[192,1280]{1,0:T(8,128)(2,1)S(1)}, u32[]{:S(2)}, u32[]{:S(2)}) %collective-permute-start.1) | collective-permute-done | bytes 491552 | tf_op jit(solution)/shard_map/ppermute | solution.py:482
  31.2 0.3 collective-permute-done.7.stat
  31.4 1.4 %halo_grads_1.1 = (bf16[96,1280]{1,0:T(8,128)(2,1)S(1)}, f32[24,128]{1,0:T(8,128)S(1)}, bf16[10,288,128]{2,1,0:T(8,128)(2,1)S(1)}, bf16[10,288,128]{2,1,0:T(8,128)(2,1)S(1)}) custom-call(bf16[192,1280]{1,0:T(8,128)(2,1)S(1)} %collective-permute-done.1.halo_ref.h_1, f32[24,128]{1,0:T(8,128)S(1)} %collective-permute-done.7.stat, ...), custom_call_target="tpu_custom_call" | custom-call | tf_op jit(solution)/shard_map/halo_grads_1/pallas_call | solution.py:91
  32.9 0.1 collective-permute-start.8
  33.0 1.4 %collective-permute-start.10 = (bf16[96,1280]{1,0:T(8,128)(2,1)S(1)}, bf16[96,1280]{1,0:T(8,128)(2,1)S(1)}, u32[]{:S(2)}, u32[]{:S(2)}) collective-permute-start(bf16[96,1280]{1,0:T(8,128)(2,1)S(1)} %held.5.refs_1_), channel_id=1, source_target_pairs={{0,1},{1,0},{2,3},{3,2},{4,5},{5,4},{6,7},{7,6},{8,9},{9,8},{10,11... | collective-permute-start | bytes 737288 | tf_op jit(solution)/shard_map/ppermute | solution.py:482
  34.4 1.2 %collective-permute-start.9 = (bf16[96,1280]{1,0:T(8,128)(2,1)S(1)}, bf16[96,1280]{1,0:T(8,128)(2,1)S(1)}, u32[]{:S(2)}, u32[]{:S(2)}) collective-permute-start(bf16[96,1280]{1,0:T(8,128)(2,1)S(1)} %held.6), channel_id=1, source_target_pairs={{1,2},{2,1},{3,4},{4,3},{5,6},{6,5},{7,0},{0,7},{9,10},{10,9},{11,... | collective-permute-start | bytes 737288 | tf_op jit(solution)/shard_map/ppermute | solution.py:482
  35.6 0.0 collective-permute-done.8.refs_0_
  35.6 1.3 %lat_grads.1 = (bf16[192,1280]{1,0:T(8,128)(2,1)S(1)}, bf16[192,1280]{1,0:T(8,128)(2,1)S(1)}, f32[24,128]{1,0:T(8,128)S(1)}, bf16[10,192,256]{2,1,0:T(8,128)(2,1)S(1)}) custom-call(bf16[256,1280]{1,0:T(8,128)(2,1)S(1)} %get-tuple-element.45.q_ref, bf16[256,1280]{1,0:T(8,128)(2,1)S(1)} %get-tuple-element.46.g_ref, ...), custom_call_target="tpu_custom_call" | custom-call | tf_op jit(solution)/shard_map/lat_grads/pallas_call | solution.py:91
  37.0 4.6 %collective-permute-start.11 = (bf16[192,1280]{1,0:T(8,128)(2,1)S(1)}, bf16[192,1280]{1,0:T(8,128)(2,1)S(1)}, u32[]{:S(2)}, u32[]{:S(2)}) collective-permute-start(bf16[192,1280]{1,0:T(8,128)(2,1)S(1)} %get-tuple-element.82), channel_id=1, source_target_pairs={{8,16},{16,8},{9,17},{17,9},{10,18},{18,10},{11,19},{19,11},{12,20... | collective-permute-start | bytes 1474568 | tf_op jit(solution)/shard_map/ppermute | solution.py:482
  41.6 0.1 collective-permute-start.12
  41.6 3.1 %own_grads.1 = (f32[256,1280]{1,0:T(8,128)S(1)}, f32[256,1280]{1,0:T(8,128)S(1)}, f32[256,1280]{1,0:T(8,128)S(1)}) custom-call(bf16[256,1280]{1,0:T(8,128)(2,1)S(1)} %get-tuple-element.45.q_ref, bf16[256,1280]{1,0:T(8,128)(2,1)S(1)} %get-tuple-element.46.g_ref, bf16[192,1280]{1,0:T(8,128)(2,1)S(1)} %collective-permute-done.halo_ref.h_0, ...), custom_call_target="tpu_custom_call" | custom-call | tf_op jit(solution)/shard_map/own_grads/pallas_call | solution.py:91
  44.7 0.0 collective-permute-done.9.b_0
  44.8 0.8 %collective-permute-done.10.b_1 = bf16[96,1280]{1,0:T(8,128)(2,1)S(1)} collective-permute-done((bf16[96,1280]{1,0:T(8,128)(2,1)S(1)}, bf16[96,1280]{1,0:T(8,128)(2,1)S(1)}, u32[]{:S(2)}, u32[]{:S(2)}) %collective-permute-start.10) | collective-permute-done | bytes 245792 | tf_op jit(solution)/shard_map/ppermute | solution.py:482
  45.5 2.5 %collective-permute-done.11.a_1 = bf16[192,1280]{1,0:T(8,128)(2,1)S(1)} collective-permute-done((bf16[192,1280]{1,0:T(8,128)(2,1)S(1)}, bf16[192,1280]{1,0:T(8,128)(2,1)S(1)}, u32[]{:S(2)}, u32[]{:S(2)}) %collective-permute-start.11) | collective-permute-done | bytes 491552 | tf_op jit(solution)/shard_map/ppermute | solution.py:482
  48.1 0.0 collective-permute-done.12.a_0
  48.1 1.8 %finish.1 = (bf16[256,1280]{1,0:T(8,128)(2,1)}, bf16[256,1280]{1,0:T(8,128)(2,1)}, bf16[256,1280]{1,0:T(8,128)(2,1)}) custom-call(f32[256,1280]{1,0:T(8,128)S(1)} %get-tuple-element.78.dq_ref, bf16[96,1280]{1,0:T(8,128)(2,1)S(1)} %collective-permute-done.9.b_0, bf16[96,1280]{1,0:T(8,128)(2,1)S(1)} %collective-permute-done.10.b_1, ...), custom_call_target="tpu_custom_call" | custom-call | tf_op jit(solution)/shard_map/finish/pallas_call | solution.py:91
  (4 shorter events, 0.0 us)
Async XLA Ops:
  2.6 9.3 %collective-permute-start.2 = (bf16[96,1280]{1,0:T(8,128)(2,1)S(1)}, bf16[96,1280]{1,0:T(8,128)(2,1)S(1)}, u32[]{:S(2)}, u32[]{:S(2)}) collective-permute-start(bf16[96,1280]{1,0:T(8,128)(2,1)S(1)} %get-tuple-element.49), channel_id=1, source_target_pairs={{0,8},{8,0},{16,24},{24,16},{1,9},{9,1},{17,25},{25,17},{2,10},{10... | collective-permute-start | bytes 737288 | tf_op jit(solution)/shard_map/ppermute | solution.py:482
  2.7 17.9 %collective-permute-start = (bf16[192,1280]{1,0:T(8,128)(2,1)S(1)}, bf16[192,1280]{1,0:T(8,128)(2,1)S(1)}, u32[]{:S(2)}, u32[]{:S(2)}) collective-permute-start(bf16[192,1280]{1,0:T(8,128)(2,1)S(1)} %get-tuple-element.47), channel_id=1, source_target_pairs={{1,2},{2,1},{3,4},{4,3},{5,6},{6,5},{7,0},{0,7},{9,10},{10,9},{11,... | collective-permute-start | bytes 1474568 | tf_op jit(solution)/shard_map/ppermute | solution.py:482
  8.4 22.7 %collective-permute-start.1 = (bf16[192,1280]{1,0:T(8,128)(2,1)S(1)}, bf16[192,1280]{1,0:T(8,128)(2,1)S(1)}, u32[]{:S(2)}, u32[]{:S(2)}) collective-permute-start(bf16[192,1280]{1,0:T(8,128)(2,1)S(1)} %get-tuple-element.48), channel_id=1, source_target_pairs={{0,1},{1,0},{2,3},{3,2},{4,5},{5,4},{6,7},{7,6},{8,9},{9,8},{10,11... | collective-permute-start | bytes 1474568 | tf_op jit(solution)/shard_map/ppermute | solution.py:482
  8.4 7.8 %collective-permute-start.3 = (bf16[96,1280]{1,0:T(8,128)(2,1)S(1)}, bf16[96,1280]{1,0:T(8,128)(2,1)S(1)}, u32[]{:S(2)}, u32[]{:S(2)}) collective-permute-start(bf16[96,1280]{1,0:T(8,128)(2,1)S(1)} %get-tuple-element.50), channel_id=1, source_target_pairs={{8,16},{16,8},{9,17},{17,9},{10,18},{18,10},{11,19},{19,11},{12,20... | collective-permute-start | bytes 737288 | tf_op jit(solution)/shard_map/ppermute | solution.py:482
  11.8 4.5 %collective-permute-start.4 = (bf16[96,1280]{1,0:T(8,128)(2,1)S(1)}, bf16[96,1280]{1,0:T(8,128)(2,1)S(1)}, u32[]{:S(2)}, u32[]{:S(2)}) collective-permute-start(bf16[96,1280]{1,0:T(8,128)(2,1)S(1)} %get-tuple-element.51), channel_id=1, source_target_pairs={{0,8},{8,0},{16,24},{24,16},{1,9},{9,1},{17,25},{25,17},{2,10},{10... | collective-permute-start | bytes 737288 | tf_op jit(solution)/shard_map/ppermute | solution.py:482
  11.9 7.8 %collective-permute-start.5 = (bf16[96,1280]{1,0:T(8,128)(2,1)S(1)}, bf16[96,1280]{1,0:T(8,128)(2,1)S(1)}, u32[]{:S(2)}, u32[]{:S(2)}) collective-permute-start(bf16[96,1280]{1,0:T(8,128)(2,1)S(1)} %get-tuple-element.52), channel_id=1, source_target_pairs={{8,16},{16,8},{9,17},{17,9},{10,18},{18,10},{11,19},{19,11},{12,20... | collective-permute-start | bytes 737288 | tf_op jit(solution)/shard_map/ppermute | solution.py:482
  21.4 5.5 %collective-permute-start.6 = (f32[24,256]{1,0:T(8,128)S(1)}, f32[24,256]{1,0:T(8,128)S(1)}, u32[]{:S(2)}, u32[]{:S(2)}) collective-permute-start(f32[24,256]{1,0:T(8,128)S(1)} %get-tuple-element.60.m), channel_id=1, source_target_pairs={{1,2},{2,1},{3,4},{4,3},{5,6},{6,5},{7,0},{0,7},{9,10},{10,9},{11,... | collective-permute-start | bytes 73736 | tf_op jit(solution)/shard_map/ppermute | solution.py:482
  24.7 6.7 %collective-permute-start.7 = (f32[24,128]{1,0:T(8,128)S(1)}, f32[24,128]{1,0:T(8,128)S(1)}, u32[]{:S(2)}, u32[]{:S(2)}) collective-permute-start(f32[24,128]{1,0:T(8,128)S(1)} %get-tuple-element.66.m), channel_id=1, source_target_pairs={{0,1},{1,0},{2,3},{3,2},{4,5},{5,4},{6,7},{7,6},{8,9},{9,8},{10,11... | collective-permute-start | bytes 36872 | tf_op jit(solution)/shard_map/ppermute | solution.py:482
  32.9 2.8 %collective-permute-start.8 = (f32[24,128]{1,0:T(8,128)S(1)}, f32[24,128]{1,0:T(8,128)S(1)}, u32[]{:S(2)}, u32[]{:S(2)}) collective-permute-start(f32[24,128]{1,0:T(8,128)S(1)} %get-tuple-element.67.refs_1_), channel_id=1, source_target_pairs={{0,1},{1,0},{2,3},{3,2},{4,5},{5,4},{6,7},{7,6},{8,9},{9,8},{10,11... | collective-permute-start | bytes 36872 | tf_op jit(solution)/shard_map/ppermute | solution.py:482
  33.0 12.6 %collective-permute-start.10 = (bf16[96,1280]{1,0:T(8,128)(2,1)S(1)}, bf16[96,1280]{1,0:T(8,128)(2,1)S(1)}, u32[]{:S(2)}, u32[]{:S(2)}) collective-permute-start(bf16[96,1280]{1,0:T(8,128)(2,1)S(1)} %held.5.refs_1_), channel_id=1, source_target_pairs={{0,1},{1,0},{2,3},{3,2},{4,5},{5,4},{6,7},{7,6},{8,9},{9,8},{10,11... | collective-permute-start | bytes 737288 | tf_op jit(solution)/shard_map/ppermute | solution.py:482
  34.4 10.3 %collective-permute-start.9 = (bf16[96,1280]{1,0:T(8,128)(2,1)S(1)}, bf16[96,1280]{1,0:T(8,128)(2,1)S(1)}, u32[]{:S(2)}, u32[]{:S(2)}) collective-permute-start(bf16[96,1280]{1,0:T(8,128)(2,1)S(1)} %held.6), channel_id=1, source_target_pairs={{1,2},{2,1},{3,4},{4,3},{5,6},{6,5},{7,0},{0,7},{9,10},{10,9},{11,... | collective-permute-start | bytes 737288 | tf_op jit(solution)/shard_map/ppermute | solution.py:482
  37.0 11.1 %collective-permute-start.11 = (bf16[192,1280]{1,0:T(8,128)(2,1)S(1)}, bf16[192,1280]{1,0:T(8,128)(2,1)S(1)}, u32[]{:S(2)}, u32[]{:S(2)}) collective-permute-start(bf16[192,1280]{1,0:T(8,128)(2,1)S(1)} %get-tuple-element.82), channel_id=1, source_target_pairs={{8,16},{16,8},{9,17},{17,9},{10,18},{18,10},{11,19},{19,11},{12,20... | collective-permute-start | bytes 1474568 | tf_op jit(solution)/shard_map/ppermute | solution.py:482
  41.6 6.5 %collective-permute-start.12 = (bf16[192,1280]{1,0:T(8,128)(2,1)S(1)}, bf16[192,1280]{1,0:T(8,128)(2,1)S(1)}, u32[]{:S(2)}, u32[]{:S(2)}) collective-permute-start(bf16[192,1280]{1,0:T(8,128)(2,1)S(1)} %get-tuple-element.83), channel_id=1, source_target_pairs={{0,8},{8,0},{16,24},{24,16},{1,9},{9,1},{17,25},{25,17},{2,10},{10... | collective-permute-start | bytes 1474568 | tf_op jit(solution)/shard_map/ppermute | solution.py:482

commit v7 on v6

--- a/solution.py
+++ b/solution.py
@@ -157,7 +157,7 @@
     ]
     return call(
         kernel, "pack_queries", operands,
-        [low(own, width)] * 2 + [low(2 * edge, width)] * 2 + [low(own, width)] * 2 + [low(lat_edge, width)] * 4,
+        [low(own, width)] * 2 + [low(2 * edge, width), low(2 * edge + 16, width)] + [low(own, width)] * 2 + [low(lat_edge, width)] * 4,
         [pltpu.VMEM((own, width), jnp.bfloat16)] * 2 + [pltpu.SemaphoreType.DMA((4,))],
         ins=[HBM_SPEC] * 4,
     )
@@ -271,35 +271,45 @@
     return peak + jnp.log(total) * LOG2E, (part_a * delta_a + part_b * delta_b) / total
 
 
-def halo_grads(group, halo, theirs, kp, vp, lat, rows, cols, count, pad=0):
+def halo_part(group, halo, kp, vp, lat, rows, cols, count):
     edge = RADIUS * rows
     near = edge + 2 * RADIUS * cols
 
-    def kernel(halo_ref, stat, k_ref, v_ref, k_0, k_1, v_0, v_1, out, mine, p_ref, g_ref, bias, s_ref, d_ref):
+    def kernel(halo_ref, k_ref, v_ref, k_0, k_1, v_0, v_1, out, s_ref, d_ref, bias):
         queries = halo_query_cell(across(LANES, group * LANES), rows, cols)
         fill_bias(bias, down(edge) + group * LANES, queries, rows, cols)
-        mine[...] = jnp.zeros_like(mine)
+        out[...] = jnp.zeros_like(out)
         for head in range(count):
             key = near_keys(group, k_ref, (k_0, k_1), head)
             value = near_keys(group, v_ref, (v_0, v_1), head)
             s_ref[head] = dot(key, halo_head(halo_ref, edge, 0, head), (1, 1)) * (SCORE_SCALE * LOG2E) + bias[...]
             d_ref[head] = dot(value, halo_head(halo_ref, edge, 1, head), (1, 1))
             log_total, delta = part_stats(s_ref[head], d_ref[head])
-            mine[head : head + 1, :] = log_total
-            mine[count + head : count + head + 1, :] = delta
-        log_total, delta = combined(*((x[:count, :], x[count : 2 * count, :]) for x in (mine, stat)))
+            out[head : head + 1, :] = log_total
+            out[count + head : count + head + 1, :] = delta
+
+    return call(
+        kernel, f"halo_part_{group}", (halo, kp, vp, *lat),
+        [full(stat_rows(count), LANES)] + [full(count, near, LANES)] * 2,
+        [pltpu.VMEM((near, LANES), jnp.float32)],
+    )
+
+
+def halo_rest(group, mine, theirs, scores, weight_grad, kp, lat, rows, cols, count):
+    edge = RADIUS * rows
+
+    def kernel(m, t, s_ref, d_ref, k_ref, k_0, k_1, out, p_ref, g_ref):
+        logs, deltas = stats_of(m, t, count)
         for head in range(count):
             row = slice(head, head + 1)
-            p_ref[head], grad = gradients(s_ref[head], d_ref[head], log_total[row], delta[row])
+            p_ref[head], grad = gradients(s_ref[head], d_ref[head], logs[row], deltas[row])
             g_ref[head] = grad
             query_grad = dot(grad, near_keys(group, k_ref, (k_0, k_1), head), (0, 0)) * SCORE_SCALE
             out[:, lanes_of(head)] = query_grad[:edge].astype(jnp.bfloat16)
 
     return call(
-        kernel, f"halo_grads_{group}", (halo, theirs, kp, vp, *lat),
-        [pltpu.VMEM((edge, count * HEAD_DIM), jnp.bfloat16), full(stat_rows(count) + pad, LANES)]
-        + [low(count, near, LANES)] * 2,
-        [pltpu.VMEM((near, LANES), jnp.float32)] + [pltpu.VMEM((count, near, LANES), jnp.float32)] * 2,
+        kernel, f"halo_rest_{group}", (mine, theirs, scores, weight_grad, kp, *lat),
+        [low(edge, count * HEAD_DIM)] + [low(count, *scores.shape[1:])] * 2,
     )
 
 
@@ -519,12 +529,14 @@
 
     mine_0, *scores_0 = halo_scores(0, halo[0], own_stat[0], kp, vp, lat, *size)
     theirs_0 = swap_lon(0, mine_0)
+    part_1, *scores_1 = halo_part(1, after(halo[1], mine_0), kp, vp, lat, *size)
+    other_1 = held(swap_lon(1, part_1))
+    theirs_0 = held(theirs_0, part_1, flops=1 << 29)
     result_0, stats_0, *lows_0 = halo_finish(0, mine_0, theirs_0, *scores_0, kp, lat[:2], *size)
-    halo[1] = after(halo[1], result_0)
-    result_1, part_1, *lows_1 = halo_grads(1, halo[1], theirs_1, kp, vp, lat, *size)
-    other_1 = held(swap_lon(1, part_1))
-    result_1 = held(result_1, part_1, flops=1 << 29)
+    theirs_1 = held(theirs_1, result_0, flops=1 << 29)
+    result_1, *lows_1 = halo_rest(1, part_1, theirs_1, *scores_1, kp, lat[:2], *size)
     result_0 = held(result_0, result_1, flops=1 << 29)
+    result_1 = held(result_1, result_0, flops=1 << 29)
     back = [swap_lon(0, result_0), swap_lon(1, result_1)]
     *lat_back, stats_1, lat_low = lat_grads(
         qp, gp, halo, stats_0, own_stat[1], other_1, lat_s, lat_d, (lows_0, lows_1), *size

time: 50 us -> 49 us (0.980)
  waiting for transfers between devices: 13.4 us -> 9.21 us
  starting transfers between devices: 22.2 us -> 25.7 us
    ppermute x13, waiting for transfers between devices: 13.4 us -> 9.21 us  [swap(): return lax.ppermute(array, axis, pairs)]
    ppermute x13, starting transfers between devices: 22.2 us -> 25.7 us  [swap(): return lax.ppermute(array, axis, pairs)]
    pallas_call x13 -> x16, Pallas kernels: 13.4 us -> 13.2 us  [call(): pl.pallas_call(kernel, name=name, in_specs=ins or [VMEM_SPEC] * len(opera...]
  transfers between devices with their start and end apart: 13 -> 13, of which waited for: 7 -> 6; matrix products, arithmetic and copies ran while one was open for 0% -> 0% of each run, Pallas kernels for 17% -> 20%
where the time goes in v7:
time: 49 us; the launch traced here: 48.9 us
  starting transfers between devices  25.7 us (52%)
  Pallas kernels  13.2 us (27%)
  waiting for transfers between devices  9.21 us (19%)
  between operations  0.78 us (2%)
    ppermute x13, starting transfers between devices, swap(): return lax.ppermute(array, axis, pairs)  25.7 us
    pallas_call x16, Pallas kernels, call(): pl.pallas_call(kernel, name=name, in_specs=ins or [VMEM_SPEC] * len(opera...  13.2 us
    ppermute x13, waiting for transfers between devices, swap(): return lax.ppermute(array, axis, pairs)  9.21 us
  transfers between devices with their start and end apart: 13, of which 6 were waited for; matrix products, arithmetic and copies ran while one was open for 0% of the time, Pallas kernels for 20%

profile of v7, /device:TPU:1, one launch (start us, length us, event | category | flops | bytes accessed | tf_op | source)
XLA Modules:
  0.0 48.9 jit_solution(6808152161005203777)
XLA Ops:
  0.6 1.9 %pack_queries.1 = (bf16[256,1280]{1,0:T(8,128)(2,1)S(1)}, bf16[256,1280]{1,0:T(8,128)(2,1)S(1)}, bf16[192,1280]{1,0:T(8,128)(2,1)S(1)}, bf16[208,1280]{1,0:T(8,1...) custom-call(bf16[256,1280]{1,0:T(8,128)(2,1)} %bitcast.7, ...), custom_call_target="tpu_custom_call" | custom-call | tf_op jit(solution)/shard_map/pack_queries/pallas_call | solution.py:91
  2.6 2.1 %collective-permute-start.1 = (bf16[208,1280]{1,0:T(8,128)(2,1)S(1)}, bf16[208,1280]{1,0:T(8,128)(2,1)S(1)}, u32[]{:S(2)}, u32[]{:S(2)}) collective-permute-start(bf16[208,1280]{1,0:T(8,128)(2,1)S(1)} %get-tuple-element.50), channel_id=1, source_target_pairs={{0,1},{1,0},{2,3},{3,2},{4,5},{5,4},{6,7},{7,6},{8,9},{9,8},{10,11... | collective-permute-start | bytes 1597448 | tf_op jit(solution)/shard_map/ppermute | solution.py:492
  4.7 1.0 %collective-permute-start.2 = (bf16[96,1280]{1,0:T(8,128)(2,1)S(1)}, bf16[96,1280]{1,0:T(8,128)(2,1)S(1)}, u32[]{:S(2)}, u32[]{:S(2)}) collective-permute-start(bf16[96,1280]{1,0:T(8,128)(2,1)S(1)} %get-tuple-element.51), channel_id=1, source_target_pairs={{0,8},{8,0},{16,24},{24,16},{1,9},{9,1},{17,25},{25,17},{2,10},{10... | collective-permute-start | bytes 737288 | tf_op jit(solution)/shard_map/ppermute | solution.py:492
  5.7 3.3 %collective-permute-start = (bf16[192,1280]{1,0:T(8,128)(2,1)S(1)}, bf16[192,1280]{1,0:T(8,128)(2,1)S(1)}, u32[]{:S(2)}, u32[]{:S(2)}) collective-permute-start(bf16[192,1280]{1,0:T(8,128)(2,1)S(1)} %get-tuple-element.49), channel_id=1, source_target_pairs={{1,2},{2,1},{3,4},{4,3},{5,6},{6,5},{7,0},{0,7},{9,10},{10,9},{11,... | collective-permute-start | bytes 1474568 | tf_op jit(solution)/shard_map/ppermute | solution.py:492
  8.9 3.3 %collective-permute-start.3 = (bf16[96,1280]{1,0:T(8,128)(2,1)S(1)}, bf16[96,1280]{1,0:T(8,128)(2,1)S(1)}, u32[]{:S(2)}, u32[]{:S(2)}) collective-permute-start(bf16[96,1280]{1,0:T(8,128)(2,1)S(1)} %get-tuple-element.52), channel_id=1, source_target_pairs={{8,16},{16,8},{9,17},{17,9},{10,18},{18,10},{11,19},{19,11},{12,20... | collective-permute-start | bytes 737288 | tf_op jit(solution)/shard_map/ppermute | solution.py:492
  12.2 0.1 collective-permute-start.4
  12.3 0.0 collective-permute-done.2.k_0
  12.3 2.3 %collective-permute-start.5 = (bf16[96,1280]{1,0:T(8,128)(2,1)S(1)}, bf16[96,1280]{1,0:T(8,128)(2,1)S(1)}, u32[]{:S(2)}, u32[]{:S(2)}) collective-permute-start(bf16[96,1280]{1,0:T(8,128)(2,1)S(1)} %get-tuple-element.54), channel_id=1, source_target_pairs={{8,16},{16,8},{9,17},{17,9},{10,18},{18,10},{11,19},{19,11},{12,20... | collective-permute-start | bytes 737288 | tf_op jit(solution)/shard_map/ppermute | solution.py:492
  14.6 1.6 %own_scores.1 = (bf16[256,1280]{1,0:T(8,128)(2,1)S(1)}, bf16[256,1280]{1,0:T(8,128)(2,1)S(1)}, f32[24,128]{1,0:T(8,128)S(1)}, f32[24,128]{1,0:T(8,128)S(1)}, f32...) custom-call(bf16[256,1280]{1,0:T(8,128)(2,1)S(1)} %get-tuple-element.47.q_ref, ...), custom_call_target="tpu_custom_call" | custom-call | tf_op jit(solution)/shard_map/own_scores/pallas_call | solution.py:91
  16.2 0.5 %collective-permute-done.3.k_1 = bf16[96,1280]{1,0:T(8,128)(2,1)S(1)} collective-permute-done((bf16[96,1280]{1,0:T(8,128)(2,1)S(1)}, bf16[96,1280]{1,0:T(8,128)(2,1)S(1)}, u32[]{:S(2)}, u32[]{:S(2)}) %collective-permute-start.3) | collective-permute-done | bytes 245792 | tf_op jit(solution)/shard_map/ppermute | solution.py:492
  16.7 0.0 collective-permute-done.4.v_0
  16.7 3.4 %collective-permute-done.5.v_1 = bf16[96,1280]{1,0:T(8,128)(2,1)S(1)} collective-permute-done((bf16[96,1280]{1,0:T(8,128)(2,1)S(1)}, bf16[96,1280]{1,0:T(8,128)(2,1)S(1)}, u32[]{:S(2)}, u32[]{:S(2)}) %collective-permute-start.5) | collective-permute-done | bytes 245792 | tf_op jit(solution)/shard_map/ppermute | solution.py:492
  20.1 1.0 %lat_scores.1 = (f32[24,128]{1,0:T(8,128)S(1)}, f32[24,128]{1,0:T(8,128)S(1)}, f32[10,192,256]{2,1,0:T(8,128)S(1)}, f32[10,192,256]{2,1,0:T(8,128)S(1)}) custom-call(bf16[256,1280]{1,0:T(8,128)(2,1)S(1)} %get-tuple-element.47.q_ref, bf16[256,1280]{1,0:T(8,128)(2,1)S(1)} %get-tuple-element.48.g_ref, bf16[96,1280]{1,0:T(8,128)(2,1)S(1)} %collective-permute-done.2.k_0, ...), custom_call_target="tpu_custom_call" | custom-call | tf_op jit(solution)/shard_map/lat_scores/pallas_call | solution.py:91
  21.1 0.1 collective-permute-done.halo_ref.h_0
  21.2 0.8 %halo_scores_0.1 = (f32[24,256]{1,0:T(8,128)S(1)}, f32[10,288,128]{2,1,0:T(8,128)S(1)}, f32[10,288,128]{2,1,0:T(8,128)S(1)}) custom-call(bf16[192,1280]{1,0:T(8,128)(2,1)S(1)} %collective-permute-done.halo_ref.h_0, f32[24,128]{1,0:T(8,128)S(1)} %get-tuple-element.59.stat, bf16[256,1280]{1,0:T(8,128)(2,1)S(1)} %get-tuple-element.60.k_ref, ...), custom_call_target="tpu_custom_call" | custom-call | tf_op jit(solution)/shard_map/halo_scores_0/pallas_call | solution.py:91
  22.0 3.3 %collective-permute-start.6 = (f32[24,256]{1,0:T(8,128)S(1)}, f32[24,256]{1,0:T(8,128)S(1)}, u32[]{:S(2)}, u32[]{:S(2)}) collective-permute-start(f32[24,256]{1,0:T(8,128)S(1)} %get-tuple-element.62.m), channel_id=1, source_target_pairs={{1,2},{2,1},{3,4},{4,3},{5,6},{6,5},{7,0},{0,7},{9,10},{10,9},{11,... | collective-permute-start | bytes 73736 | tf_op jit(solution)/shard_map/ppermute | solution.py:492
  25.3 0.0 collective-permute-start.8
  25.3 1.8 %collective-permute-done.1.halo_ref.h_1 = bf16[208,1280]{1,0:T(8,128)(2,1)S(1)} collective-permute-done((bf16[208,1280]{1,0:T(8,128)(2,1)S(1)}, bf16[208,1280]{1,0:T(8,128)(2,1)S(1)}, u32[]{:S(2)}, u32[]{:S(2)}) %collective-permute-start.1) | collective-permute-done | bytes 532512 | tf_op jit(solution)/shard_map/ppermute | solution.py:492
  27.1 0.8 %halo_part_1.1 = (f32[24,128]{1,0:T(8,128)S(1)}, f32[10,288,128]{2,1,0:T(8,128)S(1)}, f32[10,288,128]{2,1,0:T(8,128)S(1)}) custom-call(bf16[208,1280]{1,0:T(8,128)(2,1)S(1)} %collective-permute-done.1.halo_ref.h_1, bf16[256,1280]{1,0:T(8,128)(2,1)S(1)} %get-tuple-element.60.k_ref, bf16[256,1280]{1,0:T(8,128)(2,1)S(1)} %get-tuple-element.61.v_ref, ...), custom_call_target="tpu_custom_call" | custom-call | tf_op jit(solution)/shard_map/halo_part_1/pallas_call | solution.py:91
  27.8 1.7 %collective-permute-start.7 = (f32[24,128]{1,0:T(8,128)S(1)}, f32[24,128]{1,0:T(8,128)S(1)}, u32[]{:S(2)}, u32[]{:S(2)}) collective-permute-start(f32[24,128]{1,0:T(8,128)S(1)} %get-tuple-element.64.refs_1_.m), channel_id=1, source_target_pairs={{0,1},{1,0},{2,3},{3,2},{4,5},{5,4},{6,7},{7,6},{8,9},{9,8},{10,11... | collective-permute-start | bytes 36872 | tf_op jit(solution)/shard_map/ppermute | solution.py:492
  29.6 0.0 collective-permute-done.6.refs_0_
  29.6 0.5 %halo_finish_0.1 = (bf16[96,1280]{1,0:T(8,128)(2,1)S(1)}, f32[24,128]{1,0:T(8,128)S(1)}, bf16[10,288,128]{2,1,0:T(8,128)(2,1)S(1)}, bf16[10,288,128]{2,1,0:T(8,128)(2,1)S(1)}) custom-call(f32[24,256]{1,0:T(8,128)S(1)} %get-tuple-element.62.m, f32[24,256]{1,0:T(8,128)S(1)} %held.6.t, f32[10,288,128]{2,1,0:T(8,128)S(1)} %get-tuple-element.65.s_ref, ...), custom_call_target="tpu_custom_call" | custom-call | tf_op jit(solution)/shard_map/halo_finish_0/pallas_call | solution.py:91
  30.1 0.0 collective-permute-done.8.refs_0_
  30.1 0.6 %halo_rest_1.1 = (bf16[96,1280]{1,0:T(8,128)(2,1)S(1)}, bf16[10,288,128]{2,1,0:T(8,128)(2,1)S(1)}, bf16[10,288,128]{2,1,0:T(8,128)(2,1)S(1)}) custom-call(f32[24,128]{1,0:T(8,128)S(1)} %get-tuple-element.64.refs_1_.m, f32[24,128]{1,0:T(8,128)S(1)} %held.8.t, f32[10,288,128]{2,1,0:T(8,128)S(1)} %get-tuple-element.74.s_ref, ...), custom_call_target="tpu_custom_call" | custom-call | tf_op jit(solution)/shard_map/halo_rest_1/pallas_call | solution.py:91
  30.7 3.3 %collective-permute-start.9 = (bf16[96,1280]{1,0:T(8,128)(2,1)S(1)}, bf16[96,1280]{1,0:T(8,128)(2,1)S(1)}, u32[]{:S(2)}, u32[]{:S(2)}) collective-permute-start(bf16[96,1280]{1,0:T(8,128)(2,1)S(1)} %held.9.refs_1_), channel_id=1, source_target_pairs={{1,2},{2,1},{3,4},{4,3},{5,6},{6,5},{7,0},{0,7},{9,10},{10,9},{11,... | collective-permute-start | bytes 737288 | tf_op jit(solution)/shard_map/ppermute | solution.py:492
  34.0 0.0 collective-permute-start.10
  34.0 0.0 collective-permute-done.7.refs_0_
  34.0 1.3 %lat_grads.1 = (bf16[192,1280]{1,0:T(8,128)(2,1)S(1)}, bf16[192,1280]{1,0:T(8,128)(2,1)S(1)}, f32[24,128]{1,0:T(8,128)S(1)}, bf16[10,192,256]{2,1,0:T(8,128)(2,1)S(1)}) custom-call(bf16[256,1280]{1,0:T(8,128)(2,1)S(1)} %get-tuple-element.47.q_ref, bf16[256,1280]{1,0:T(8,128)(2,1)S(1)} %get-tuple-element.48.g_ref, ...), custom_call_target="tpu_custom_call" | custom-call | tf_op jit(solution)/shard_map/lat_grads/pallas_call | solution.py:91
  35.4 5.2 %collective-permute-start.11 = (bf16[192,1280]{1,0:T(8,128)(2,1)S(1)}, bf16[192,1280]{1,0:T(8,128)(2,1)S(1)}, u32[]{:S(2)}, u32[]{:S(2)}) collective-permute-start(bf16[192,1280]{1,0:T(8,128)(2,1)S(1)} %get-tuple-element.86), channel_id=1, source_target_pairs={{8,16},{16,8},{9,17},{17,9},{10,18},{18,10},{11,19},{19,11},{12,20... | collective-permute-start | bytes 1474568 | tf_op jit(solution)/shard_map/ppermute | solution.py:492
  40.6 0.1 collective-permute-start.12
  40.7 3.0 %own_grads.1 = (f32[256,1280]{1,0:T(8,128)S(1)}, f32[256,1280]{1,0:T(8,128)S(1)}, f32[256,1280]{1,0:T(8,128)S(1)}) custom-call(bf16[256,1280]{1,0:T(8,128)(2,1)S(1)} %get-tuple-element.47.q_ref, bf16[256,1280]{1,0:T(8,128)(2,1)S(1)} %get-tuple-element.48.g_ref, bf16[192,1280]{1,0:T(8,128)(2,1)S(1)} %collective-permute-done.halo_ref.h_0, ...), custom_call_target="tpu_custom_call" | custom-call | tf_op jit(solution)/shard_map/own_grads/pallas_call | solution.py:91
  43.8 2.8 %collective-permute-done.10.b_1 = bf16[96,1280]{1,0:T(8,128)(2,1)S(1)} collective-permute-done((bf16[96,1280]{1,0:T(8,128)(2,1)S(1)}, bf16[96,1280]{1,0:T(8,128)(2,1)S(1)}, u32[]{:S(2)}, u32[]{:S(2)}) %collective-permute-start.10) | collective-permute-done | bytes 245792 | tf_op jit(solution)/shard_map/ppermute | solution.py:492
  46.6 0.0 collective-permute-done.9.b_0
  46.6 0.5 %collective-permute-done.11.a_1 = bf16[192,1280]{1,0:T(8,128)(2,1)S(1)} collective-permute-done((bf16[192,1280]{1,0:T(8,128)(2,1)S(1)}, bf16[192,1280]{1,0:T(8,128)(2,1)S(1)}, u32[]{:S(2)}, u32[]{:S(2)}) %collective-permute-start.11) | collective-permute-done | bytes 491552 | tf_op jit(solution)/shard_map/ppermute | solution.py:492
  47.1 0.0 collective-permute-done.12.a_0
  47.1 1.7 %finish.1 = (bf16[256,1280]{1,0:T(8,128)(2,1)}, bf16[256,1280]{1,0:T(8,128)(2,1)}, bf16[256,1280]{1,0:T(8,128)(2,1)}) custom-call(f32[256,1280]{1,0:T(8,128)S(1)} %get-tuple-element.82.dq_ref, bf16[96,1280]{1,0:T(8,128)(2,1)S(1)} %collective-permute-done.9.b_0, bf16[96,1280]{1,0:T(8,128)(2,1)S(1)} %collective-permute-done.10.b_1, ...), custom_call_target="tpu_custom_call" | custom-call | tf_op jit(solution)/shard_map/finish/pallas_call | solution.py:91
  (6 shorter events, 0.0 us)
Async XLA Ops:
  2.6 24.5 %collective-permute-start.1 = (bf16[208,1280]{1,0:T(8,128)(2,1)S(1)}, bf16[208,1280]{1,0:T(8,128)(2,1)S(1)}, u32[]{:S(2)}, u32[]{:S(2)}) collective-permute-start(bf16[208,1280]{1,0:T(8,128)(2,1)S(1)} %get-tuple-element.50), channel_id=1, source_target_pairs={{0,1},{1,0},{2,3},{3,2},{4,5},{5,4},{6,7},{7,6},{8,9},{9,8},{10,11... | collective-permute-start | bytes 1597448 | tf_op jit(solution)/shard_map/ppermute | solution.py:492
  4.7 7.6 %collective-permute-start.2 = (bf16[96,1280]{1,0:T(8,128)(2,1)S(1)}, bf16[96,1280]{1,0:T(8,128)(2,1)S(1)}, u32[]{:S(2)}, u32[]{:S(2)}) collective-permute-start(bf16[96,1280]{1,0:T(8,128)(2,1)S(1)} %get-tuple-element.51), channel_id=1, source_target_pairs={{0,8},{8,0},{16,24},{24,16},{1,9},{9,1},{17,25},{25,17},{2,10},{10... | collective-permute-start | bytes 737288 | tf_op jit(solution)/shard_map/ppermute | solution.py:492
  5.7 15.5 %collective-permute-start = (bf16[192,1280]{1,0:T(8,128)(2,1)S(1)}, bf16[192,1280]{1,0:T(8,128)(2,1)S(1)}, u32[]{:S(2)}, u32[]{:S(2)}) collective-permute-start(bf16[192,1280]{1,0:T(8,128)(2,1)S(1)} %get-tuple-element.49), channel_id=1, source_target_pairs={{1,2},{2,1},{3,4},{4,3},{5,6},{6,5},{7,0},{0,7},{9,10},{10,9},{11,... | collective-permute-start | bytes 1474568 | tf_op jit(solution)/shard_map/ppermute | solution.py:492
  8.9 7.8 %collective-permute-start.3 = (bf16[96,1280]{1,0:T(8,128)(2,1)S(1)}, bf16[96,1280]{1,0:T(8,128)(2,1)S(1)}, u32[]{:S(2)}, u32[]{:S(2)}) collective-permute-start(bf16[96,1280]{1,0:T(8,128)(2,1)S(1)} %get-tuple-element.52), channel_id=1, source_target_pairs={{8,16},{16,8},{9,17},{17,9},{10,18},{18,10},{11,19},{19,11},{12,20... | collective-permute-start | bytes 737288 | tf_op jit(solution)/shard_map/ppermute | solution.py:492
  12.2 4.5 %collective-permute-start.4 = (bf16[96,1280]{1,0:T(8,128)(2,1)S(1)}, bf16[96,1280]{1,0:T(8,128)(2,1)S(1)}, u32[]{:S(2)}, u32[]{:S(2)}) collective-permute-start(bf16[96,1280]{1,0:T(8,128)(2,1)S(1)} %get-tuple-element.53), channel_id=1, source_target_pairs={{0,8},{8,0},{16,24},{24,16},{1,9},{9,1},{17,25},{25,17},{2,10},{10... | collective-permute-start | bytes 737288 | tf_op jit(solution)/shard_map/ppermute | solution.py:492
  12.3 7.8 %collective-permute-start.5 = (bf16[96,1280]{1,0:T(8,128)(2,1)S(1)}, bf16[96,1280]{1,0:T(8,128)(2,1)S(1)}, u32[]{:S(2)}, u32[]{:S(2)}) collective-permute-start(bf16[96,1280]{1,0:T(8,128)(2,1)S(1)} %get-tuple-element.54), channel_id=1, source_target_pairs={{8,16},{16,8},{9,17},{17,9},{10,18},{18,10},{11,19},{19,11},{12,20... | collective-permute-start | bytes 737288 | tf_op jit(solution)/shard_map/ppermute | solution.py:492
  22.0 7.6 %collective-permute-start.6 = (f32[24,256]{1,0:T(8,128)S(1)}, f32[24,256]{1,0:T(8,128)S(1)}, u32[]{:S(2)}, u32[]{:S(2)}) collective-permute-start(f32[24,256]{1,0:T(8,128)S(1)} %get-tuple-element.62.m), channel_id=1, source_target_pairs={{1,2},{2,1},{3,4},{4,3},{5,6},{6,5},{7,0},{0,7},{9,10},{10,9},{11,... | collective-permute-start | bytes 73736 | tf_op jit(solution)/shard_map/ppermute | solution.py:492
  25.3 4.8 %collective-permute-start.8 = (f32[24,128]{1,0:T(8,128)S(1)}, f32[24,128]{1,0:T(8,128)S(1)}, u32[]{:S(2)}, u32[]{:S(2)}) collective-permute-start(f32[24,128]{1,0:T(8,128)S(1)} %get-tuple-element.68.m), channel_id=1, source_target_pairs={{0,1},{1,0},{2,3},{3,2},{4,5},{5,4},{6,7},{7,6},{8,9},{9,8},{10,11... | collective-permute-start | bytes 36872 | tf_op jit(solution)/shard_map/ppermute | solution.py:492
  27.8 6.2 %collective-permute-start.7 = (f32[24,128]{1,0:T(8,128)S(1)}, f32[24,128]{1,0:T(8,128)S(1)}, u32[]{:S(2)}, u32[]{:S(2)}) collective-permute-start(f32[24,128]{1,0:T(8,128)S(1)} %get-tuple-element.64.refs_1_.m), channel_id=1, source_target_pairs={{0,1},{1,0},{2,3},{3,2},{4,5},{5,4},{6,7},{7,6},{8,9},{9,8},{10,11... | collective-permute-start | bytes 36872 | tf_op jit(solution)/shard_map/ppermute | solution.py:492
  30.7 15.9 %collective-permute-start.9 = (bf16[96,1280]{1,0:T(8,128)(2,1)S(1)}, bf16[96,1280]{1,0:T(8,128)(2,1)S(1)}, u32[]{:S(2)}, u32[]{:S(2)}) collective-permute-start(bf16[96,1280]{1,0:T(8,128)(2,1)S(1)} %held.9.refs_1_), channel_id=1, source_target_pairs={{1,2},{2,1},{3,4},{4,3},{5,6},{6,5},{7,0},{0,7},{9,10},{10,9},{11,... | collective-permute-start | bytes 737288 | tf_op jit(solution)/shard_map/ppermute | solution.py:492
  34.0 12.6 %collective-permute-start.10 = (bf16[96,1280]{1,0:T(8,128)(2,1)S(1)}, bf16[96,1280]{1,0:T(8,128)(2,1)S(1)}, u32[]{:S(2)}, u32[]{:S(2)}) collective-permute-start(bf16[96,1280]{1,0:T(8,128)(2,1)S(1)} %held.10), channel_id=1, source_target_pairs={{0,1},{1,0},{2,3},{3,2},{4,5},{5,4},{6,7},{7,6},{8,9},{9,8},{10,11... | collective-permute-start | bytes 737288 | tf_op jit(solution)/shard_map/ppermute | solution.py:492
  35.4 11.8 %collective-permute-start.11 = (bf16[192,1280]{1,0:T(8,128)(2,1)S(1)}, bf16[192,1280]{1,0:T(8,128)(2,1)S(1)}, u32[]{:S(2)}, u32[]{:S(2)}) collective-permute-start(bf16[192,1280]{1,0:T(8,128)(2,1)S(1)} %get-tuple-element.86), channel_id=1, source_target_pairs={{8,16},{16,8},{9,17},{17,9},{10,18},{18,10},{11,19},{19,11},{12,20... | collective-permute-start | bytes 1474568 | tf_op jit(solution)/shard_map/ppermute | solution.py:492
  40.6 6.5 %collective-permute-start.12 = (bf16[192,1280]{1,0:T(8,128)(2,1)S(1)}, bf16[192,1280]{1,0:T(8,128)(2,1)S(1)}, u32[]{:S(2)}, u32[]{:S(2)}) collective-permute-start(bf16[192,1280]{1,0:T(8,128)(2,1)S(1)} %get-tuple-element.87), channel_id=1, source_target_pairs={{0,8},{8,0},{16,24},{24,16},{1,9},{9,1},{17,25},{25,17},{2,10},{10... | collective-permute-start | bytes 1474568 | tf_op jit(solution)/shard_map/ppermute | solution.py:492

commit v8 on v7

--- a/solution.py
+++ b/solution.py
@@ -535,15 +535,14 @@
     result_0, stats_0, *lows_0 = halo_finish(0, mine_0, theirs_0, *scores_0, kp, lat[:2], *size)
     theirs_1 = held(theirs_1, result_0, flops=1 << 29)
     result_1, *lows_1 = halo_rest(1, part_1, theirs_1, *scores_1, kp, lat[:2], *size)
-    result_0 = held(result_0, result_1, flops=1 << 29)
-    result_1 = held(result_1, result_0, flops=1 << 29)
-    back = [swap_lon(0, result_0), swap_lon(1, result_1)]
+    back_1 = swap_lon(1, result_1)
     *lat_back, stats_1, lat_low = lat_grads(
         qp, gp, halo, stats_0, own_stat[1], other_1, lat_s, lat_d, (lows_0, lows_1), *size
     )
     dq, dk, dv = own_grads(
         qp, gp, halo, (stats_0, stats_1), lat_low, own_s, own_d, (lows_0, lows_1), kp, lat[:2], *size
     )
+    back = [swap_lon(0, held(result_0, lat_back[1], flops=1 << 29)), back_1]
     lat_back = [swap_lat(slot, lat_back[slot]) for slot in (1, 0)]
     outs = finish(dq, back, held(dk), dv, lat_back, *size)
     shape = (rows, cols, width)

time: 49 us -> 48.5 us (0.990)
  waiting for transfers between devices: 9.21 us -> 6.87 us
  starting transfers between devices: 25.7 us -> 27.5 us
    ppermute x13, waiting for transfers between devices: 9.21 us -> 6.87 us  [swap(): return lax.ppermute(array, axis, pairs)]
    ppermute x13, starting transfers between devices: 25.7 us -> 27.5 us  [swap(): return lax.ppermute(array, axis, pairs)]
    pallas_call x16 -> x15, Pallas kernels: 13.2 us -> 13.2 us  [call(): pl.pallas_call(kernel, name=name, in_specs=ins or [VMEM_SPEC] * len(opera...]
  transfers between devices with their start and end apart: 13 -> 13, of which waited for: 6 -> 5; matrix products, arithmetic and copies ran while one was open for 0% -> 0% of each run, Pallas kernels for 20% -> 20%
where the time goes in v8:
time: 48.5 us; the launch traced here: 48.3 us
  starting transfers between devices  27.5 us (57%)
  Pallas kernels  13.2 us (27%)
  waiting for transfers between devices  6.87 us (14%)
  between operations  0.77 us (2%)
    ppermute x13, starting transfers between devices, swap(): return lax.ppermute(array, axis, pairs)  27.5 us
    pallas_call x15, Pallas kernels, call(): pl.pallas_call(kernel, name=name, in_specs=ins or [VMEM_SPEC] * len(opera...  13.2 us
    ppermute x13, waiting for transfers between devices, swap(): return lax.ppermute(array, axis, pairs)  6.87 us
  transfers between devices with their start and end apart: 13, of which 5 were waited for; matrix products, arithmetic and copies ran while one was open for 0% of the time, Pallas kernels for 20%

profile of v8, /device:TPU:1, one launch (start us, length us, event | category | flops | bytes accessed | tf_op | source)
XLA Modules:
  0.0 48.3 jit_solution(5499898995386886598)
XLA Ops:
  0.6 1.9 %pack_queries.1 = (bf16[256,1280]{1,0:T(8,128)(2,1)S(1)}, bf16[256,1280]{1,0:T(8,128)(2,1)S(1)}, bf16[192,1280]{1,0:T(8,128)(2,1)S(1)}, bf16[208,1280]{1,0:T(8,1...) custom-call(bf16[256,1280]{1,0:T(8,128)(2,1)} %bitcast.7, ...), custom_call_target="tpu_custom_call" | custom-call | tf_op jit(solution)/shard_map/pack_queries/pallas_call | solution.py:91
  2.6 2.1 %collective-permute-start.1 = (bf16[208,1280]{1,0:T(8,128)(2,1)S(1)}, bf16[208,1280]{1,0:T(8,128)(2,1)S(1)}, u32[]{:S(2)}, u32[]{:S(2)}) collective-permute-start(bf16[208,1280]{1,0:T(8,128)(2,1)S(1)} %get-tuple-element.50), channel_id=1, source_target_pairs={{0,1},{1,0},{2,3},{3,2},{4,5},{5,4},{6,7},{7,6},{8,9},{9,8},{10,11... | collective-permute-start | bytes 1597448 | tf_op jit(solution)/shard_map/ppermute | solution.py:492
  4.7 1.0 %collective-permute-start.2 = (bf16[96,1280]{1,0:T(8,128)(2,1)S(1)}, bf16[96,1280]{1,0:T(8,128)(2,1)S(1)}, u32[]{:S(2)}, u32[]{:S(2)}) collective-permute-start(bf16[96,1280]{1,0:T(8,128)(2,1)S(1)} %get-tuple-element.51), channel_id=1, source_target_pairs={{0,8},{8,0},{16,24},{24,16},{1,9},{9,1},{17,25},{25,17},{2,10},{10... | collective-permute-start | bytes 737288 | tf_op jit(solution)/shard_map/ppermute | solution.py:492
  5.7 3.3 %collective-permute-start = (bf16[192,1280]{1,0:T(8,128)(2,1)S(1)}, bf16[192,1280]{1,0:T(8,128)(2,1)S(1)}, u32[]{:S(2)}, u32[]{:S(2)}) collective-permute-start(bf16[192,1280]{1,0:T(8,128)(2,1)S(1)} %get-tuple-element.49), channel_id=1, source_target_pairs={{1,2},{2,1},{3,4},{4,3},{5,6},{6,5},{7,0},{0,7},{9,10},{10,9},{11,... | collective-permute-start | bytes 1474568 | tf_op jit(solution)/shard_map/ppermute | solution.py:492
  8.9 3.3 %collective-permute-start.3 = (bf16[96,1280]{1,0:T(8,128)(2,1)S(1)}, bf16[96,1280]{1,0:T(8,128)(2,1)S(1)}, u32[]{:S(2)}, u32[]{:S(2)}) collective-permute-start(bf16[96,1280]{1,0:T(8,128)(2,1)S(1)} %get-tuple-element.52), channel_id=1, source_target_pairs={{8,16},{16,8},{9,17},{17,9},{10,18},{18,10},{11,19},{19,11},{12,20... | collective-permute-start | bytes 737288 | tf_op jit(solution)/shard_map/ppermute | solution.py:492
  12.2 0.1 collective-permute-start.4
  12.3 0.0 collective-permute-done.2.k_0
  12.3 2.3 %collective-permute-start.5 = (bf16[96,1280]{1,0:T(8,128)(2,1)S(1)}, bf16[96,1280]{1,0:T(8,128)(2,1)S(1)}, u32[]{:S(2)}, u32[]{:S(2)}) collective-permute-start(bf16[96,1280]{1,0:T(8,128)(2,1)S(1)} %get-tuple-element.54), channel_id=1, source_target_pairs={{8,16},{16,8},{9,17},{17,9},{10,18},{18,10},{11,19},{19,11},{12,20... | collective-permute-start | bytes 737288 | tf_op jit(solution)/shard_map/ppermute | solution.py:492
  14.6 1.6 %own_scores.1 = (bf16[256,1280]{1,0:T(8,128)(2,1)S(1)}, bf16[256,1280]{1,0:T(8,128)(2,1)S(1)}, f32[24,128]{1,0:T(8,128)S(1)}, f32[24,128]{1,0:T(8,128)S(1)}, f32...) custom-call(bf16[256,1280]{1,0:T(8,128)(2,1)S(1)} %get-tuple-element.47.q_ref, ...), custom_call_target="tpu_custom_call" | custom-call | tf_op jit(solution)/shard_map/own_scores/pallas_call | solution.py:91
  16.2 0.5 %collective-permute-done.3.k_1 = bf16[96,1280]{1,0:T(8,128)(2,1)S(1)} collective-permute-done((bf16[96,1280]{1,0:T(8,128)(2,1)S(1)}, bf16[96,1280]{1,0:T(8,128)(2,1)S(1)}, u32[]{:S(2)}, u32[]{:S(2)}) %collective-permute-start.3) | collective-permute-done | bytes 245792 | tf_op jit(solution)/shard_map/ppermute | solution.py:492
  16.7 0.0 collective-permute-done.4.v_0
  16.7 3.4 %collective-permute-done.5.v_1 = bf16[96,1280]{1,0:T(8,128)(2,1)S(1)} collective-permute-done((bf16[96,1280]{1,0:T(8,128)(2,1)S(1)}, bf16[96,1280]{1,0:T(8,128)(2,1)S(1)}, u32[]{:S(2)}, u32[]{:S(2)}) %collective-permute-start.5) | collective-permute-done | bytes 245792 | tf_op jit(solution)/shard_map/ppermute | solution.py:492
  20.1 1.0 %lat_scores.1 = (f32[24,128]{1,0:T(8,128)S(1)}, f32[24,128]{1,0:T(8,128)S(1)}, f32[10,192,256]{2,1,0:T(8,128)S(1)}, f32[10,192,256]{2,1,0:T(8,128)S(1)}) custom-call(bf16[256,1280]{1,0:T(8,128)(2,1)S(1)} %get-tuple-element.47.q_ref, bf16[256,1280]{1,0:T(8,128)(2,1)S(1)} %get-tuple-element.48.g_ref, bf16[96,1280]{1,0:T(8,128)(2,1)S(1)} %collective-permute-done.2.k_0, ...), custom_call_target="tpu_custom_call" | custom-call | tf_op jit(solution)/shard_map/lat_scores/pallas_call | solution.py:91
  21.1 0.1 collective-permute-done.halo_ref.h_0
  21.2 0.8 %halo_scores_0.1 = (f32[24,256]{1,0:T(8,128)S(1)}, f32[10,288,128]{2,1,0:T(8,128)S(1)}, f32[10,288,128]{2,1,0:T(8,128)S(1)}) custom-call(bf16[192,1280]{1,0:T(8,128)(2,1)S(1)} %collective-permute-done.halo_ref.h_0, f32[24,128]{1,0:T(8,128)S(1)} %get-tuple-element.59.stat, bf16[256,1280]{1,0:T(8,128)(2,1)S(1)} %get-tuple-element.60.k_ref, ...), custom_call_target="tpu_custom_call" | custom-call | tf_op jit(solution)/shard_map/halo_scores_0/pallas_call | solution.py:91
  22.0 3.3 %collective-permute-start.6 = (f32[24,256]{1,0:T(8,128)S(1)}, f32[24,256]{1,0:T(8,128)S(1)}, u32[]{:S(2)}, u32[]{:S(2)}) collective-permute-start(f32[24,256]{1,0:T(8,128)S(1)} %get-tuple-element.62.m), channel_id=1, source_target_pairs={{1,2},{2,1},{3,4},{4,3},{5,6},{6,5},{7,0},{0,7},{9,10},{10,9},{11,... | collective-permute-start | bytes 73736 | tf_op jit(solution)/shard_map/ppermute | solution.py:492
  25.3 0.0 collective-permute-start.8
  25.3 1.8 %collective-permute-done.1.halo_ref.h_1 = bf16[208,1280]{1,0:T(8,128)(2,1)S(1)} collective-permute-done((bf16[208,1280]{1,0:T(8,128)(2,1)S(1)}, bf16[208,1280]{1,0:T(8,128)(2,1)S(1)}, u32[]{:S(2)}, u32[]{:S(2)}) %collective-permute-start.1) | collective-permute-done | bytes 532512 | tf_op jit(solution)/shard_map/ppermute | solution.py:492
  27.1 0.8 %halo_part_1.1 = (f32[24,128]{1,0:T(8,128)S(1)}, f32[10,288,128]{2,1,0:T(8,128)S(1)}, f32[10,288,128]{2,1,0:T(8,128)S(1)}) custom-call(bf16[208,1280]{1,0:T(8,128)(2,1)S(1)} %collective-permute-done.1.halo_ref.h_1, bf16[256,1280]{1,0:T(8,128)(2,1)S(1)} %get-tuple-element.60.k_ref, bf16[256,1280]{1,0:T(8,128)(2,1)S(1)} %get-tuple-element.61.v_ref, ...), custom_call_target="tpu_custom_call" | custom-call | tf_op jit(solution)/shard_map/halo_part_1/pallas_call | solution.py:91
  27.8 1.7 %collective-permute-start.7 = (f32[24,128]{1,0:T(8,128)S(1)}, f32[24,128]{1,0:T(8,128)S(1)}, u32[]{:S(2)}, u32[]{:S(2)}) collective-permute-start(f32[24,128]{1,0:T(8,128)S(1)} %get-tuple-element.64.refs_1_.m), channel_id=1, source_target_pairs={{0,1},{1,0},{2,3},{3,2},{4,5},{5,4},{6,7},{7,6},{8,9},{9,8},{10,11... | collective-permute-start | bytes 36872 | tf_op jit(solution)/shard_map/ppermute | solution.py:492
  29.6 0.0 collective-permute-done.6.refs_0_
  29.6 0.5 %halo_finish_0.1 = (bf16[96,1280]{1,0:T(8,128)(2,1)S(1)}, f32[24,128]{1,0:T(8,128)S(1)}, bf16[10,288,128]{2,1,0:T(8,128)(2,1)S(1)}, bf16[10,288,128]{2,1,0:T(8,128)(2,1)S(1)}) custom-call(f32[24,256]{1,0:T(8,128)S(1)} %get-tuple-element.62.m, f32[24,256]{1,0:T(8,128)S(1)} %held.5.t, f32[10,288,128]{2,1,0:T(8,128)S(1)} %get-tuple-element.65.s_ref, ...), custom_call_target="tpu_custom_call" | custom-call | tf_op jit(solution)/shard_map/halo_finish_0/pallas_call | solution.py:91
  30.1 0.0 collective-permute-done.8.refs_0_
  30.1 0.6 %halo_rest_1.1 = (bf16[96,1280]{1,0:T(8,128)(2,1)S(1)}, bf16[10,288,128]{2,1,0:T(8,128)(2,1)S(1)}, bf16[10,288,128]{2,1,0:T(8,128)(2,1)S(1)}) custom-call(f32[24,128]{1,0:T(8,128)S(1)} %get-tuple-element.64.refs_1_.m, f32[24,128]{1,0:T(8,128)S(1)} %held.7.t, f32[10,288,128]{2,1,0:T(8,128)S(1)} %get-tuple-element.74.s_ref, ...), custom_call_target="tpu_custom_call" | custom-call | tf_op jit(solution)/shard_map/halo_rest_1/pallas_call | solution.py:91
  30.7 0.1 collective-permute-start.10
  30.8 0.0 collective-permute-done.7.refs_0_
  30.8 1.3 %lat_grads.1 = (bf16[192,1280]{1,0:T(8,128)(2,1)S(1)}, bf16[192,1280]{1,0:T(8,128)(2,1)S(1)}, f32[24,128]{1,0:T(8,128)S(1)}, bf16[10,192,256]{2,1,0:T(8,128)(2,1)S(1)}) custom-call(bf16[256,1280]{1,0:T(8,128)(2,1)S(1)} %get-tuple-element.47.q_ref, bf16[256,1280]{1,0:T(8,128)(2,1)S(1)} %get-tuple-element.48.g_ref, ...), custom_call_target="tpu_custom_call" | custom-call | tf_op jit(solution)/shard_map/lat_grads/pallas_call | solution.py:91
  32.1 5.6 %collective-permute-start.11 = (bf16[192,1280]{1,0:T(8,128)(2,1)S(1)}, bf16[192,1280]{1,0:T(8,128)(2,1)S(1)}, u32[]{:S(2)}, u32[]{:S(2)}) collective-permute-start(bf16[192,1280]{1,0:T(8,128)(2,1)S(1)} %get-tuple-element.83.refs_1_), channel_id=1, source_target_pairs={{8,16},{16,8},{9,17},{17,9},{10,18},{18,10},{11,19},{19,11},{12,20... | collective-permute-start | bytes 1474568 | tf_op jit(solution)/shard_map/ppermute | solution.py:492
  37.8 4.7 %collective-permute-start.9 = (bf16[96,1280]{1,0:T(8,128)(2,1)S(1)}, bf16[96,1280]{1,0:T(8,128)(2,1)S(1)}, u32[]{:S(2)}, u32[]{:S(2)}) collective-permute-start(bf16[96,1280]{1,0:T(8,128)(2,1)S(1)} %held.8), channel_id=1, source_target_pairs={{1,2},{2,1},{3,4},{4,3},{5,6},{6,5},{7,0},{0,7},{9,10},{10,9},{11,... | collective-permute-start | bytes 737288 | tf_op jit(solution)/shard_map/ppermute | solution.py:492
  42.5 0.0 collective-permute-start.12
  42.5 3.0 %own_grads.1 = (f32[256,1280]{1,0:T(8,128)S(1)}, f32[256,1280]{1,0:T(8,128)S(1)}, f32[256,1280]{1,0:T(8,128)S(1)}) custom-call(bf16[256,1280]{1,0:T(8,128)(2,1)S(1)} %get-tuple-element.47.q_ref, bf16[256,1280]{1,0:T(8,128)(2,1)S(1)} %get-tuple-element.48.g_ref, bf16[192,1280]{1,0:T(8,128)(2,1)S(1)} %collective-permute-done.halo_ref.h_0, ...), custom_call_target="tpu_custom_call" | custom-call | tf_op jit(solution)/shard_map/own_grads/pallas_call | solution.py:91
  45.5 0.0 collective-permute-done.10.b_1
  45.5 1.0 %collective-permute-done.9.b_0 = bf16[96,1280]{1,0:T(8,128)(2,1)S(1)} collective-permute-done((bf16[96,1280]{1,0:T(8,128)(2,1)S(1)}, bf16[96,1280]{1,0:T(8,128)(2,1)S(1)}, u32[]{:S(2)}, u32[]{:S(2)}) %collective-permute-start.9) | collective-permute-done | bytes 245792 | tf_op jit(solution)/shard_map/ppermute | solution.py:492
  46.6 0.0 collective-permute-done.11.a_1
  46.6 0.0 collective-permute-done.12.a_0
  46.6 1.7 %finish.1 = (bf16[256,1280]{1,0:T(8,128)(2,1)}, bf16[256,1280]{1,0:T(8,128)(2,1)}, bf16[256,1280]{1,0:T(8,128)(2,1)}) custom-call(f32[256,1280]{1,0:T(8,128)S(1)} %get-tuple-element.82.dq_ref, bf16[96,1280]{1,0:T(8,128)(2,1)S(1)} %collective-permute-done.9.b_0, bf16[96,1280]{1,0:T(8,128)(2,1)S(1)} %collective-permute-done.10.b_1, ...), custom_call_target="tpu_custom_call" | custom-call | tf_op jit(solution)/shard_map/finish/pallas_call | solution.py:91
  (5 shorter events, 0.0 us)
Async XLA Ops:
  2.6 24.5 %collective-permute-start.1 = (bf16[208,1280]{1,0:T(8,128)(2,1)S(1)}, bf16[208,1280]{1,0:T(8,128)(2,1)S(1)}, u32[]{:S(2)}, u32[]{:S(2)}) collective-permute-start(bf16[208,1280]{1,0:T(8,128)(2,1)S(1)} %get-tuple-element.50), channel_id=1, source_target_pairs={{0,1},{1,0},{2,3},{3,2},{4,5},{5,4},{6,7},{7,6},{8,9},{9,8},{10,11... | collective-permute-start | bytes 1597448 | tf_op jit(solution)/shard_map/ppermute | solution.py:492
  4.7 7.6 %collective-permute-start.2 = (bf16[96,1280]{1,0:T(8,128)(2,1)S(1)}, bf16[96,1280]{1,0:T(8,128)(2,1)S(1)}, u32[]{:S(2)}, u32[]{:S(2)}) collective-permute-start(bf16[96,1280]{1,0:T(8,128)(2,1)S(1)} %get-tuple-element.51), channel_id=1, source_target_pairs={{0,8},{8,0},{16,24},{24,16},{1,9},{9,1},{17,25},{25,17},{2,10},{10... | collective-permute-start | bytes 737288 | tf_op jit(solution)/shard_map/ppermute | solution.py:492
  5.7 15.5 %collective-permute-start = (bf16[192,1280]{1,0:T(8,128)(2,1)S(1)}, bf16[192,1280]{1,0:T(8,128)(2,1)S(1)}, u32[]{:S(2)}, u32[]{:S(2)}) collective-permute-start(bf16[192,1280]{1,0:T(8,128)(2,1)S(1)} %get-tuple-element.49), channel_id=1, source_target_pairs={{1,2},{2,1},{3,4},{4,3},{5,6},{6,5},{7,0},{0,7},{9,10},{10,9},{11,... | collective-permute-start | bytes 1474568 | tf_op jit(solution)/shard_map/ppermute | solution.py:492
  8.9 7.8 %collective-permute-start.3 = (bf16[96,1280]{1,0:T(8,128)(2,1)S(1)}, bf16[96,1280]{1,0:T(8,128)(2,1)S(1)}, u32[]{:S(2)}, u32[]{:S(2)}) collective-permute-start(bf16[96,1280]{1,0:T(8,128)(2,1)S(1)} %get-tuple-element.52), channel_id=1, source_target_pairs={{8,16},{16,8},{9,17},{17,9},{10,18},{18,10},{11,19},{19,11},{12,20... | collective-permute-start | bytes 737288 | tf_op jit(solution)/shard_map/ppermute | solution.py:492
  12.2 4.5 %collective-permute-start.4 = (bf16[96,1280]{1,0:T(8,128)(2,1)S(1)}, bf16[96,1280]{1,0:T(8,128)(2,1)S(1)}, u32[]{:S(2)}, u32[]{:S(2)}) collective-permute-start(bf16[96,1280]{1,0:T(8,128)(2,1)S(1)} %get-tuple-element.53), channel_id=1, source_target_pairs={{0,8},{8,0},{16,24},{24,16},{1,9},{9,1},{17,25},{25,17},{2,10},{10... | collective-permute-start | bytes 737288 | tf_op jit(solution)/shard_map/ppermute | solution.py:492
  12.3 7.8 %collective-permute-start.5 = (bf16[96,1280]{1,0:T(8,128)(2,1)S(1)}, bf16[96,1280]{1,0:T(8,128)(2,1)S(1)}, u32[]{:S(2)}, u32[]{:S(2)}) collective-permute-start(bf16[96,1280]{1,0:T(8,128)(2,1)S(1)} %get-tuple-element.54), channel_id=1, source_target_pairs={{8,16},{16,8},{9,17},{17,9},{10,18},{18,10},{11,19},{19,11},{12,20... | collective-permute-start | bytes 737288 | tf_op jit(solution)/shard_map/ppermute | solution.py:492
  22.0 7.6 %collective-permute-start.6 = (f32[24,256]{1,0:T(8,128)S(1)}, f32[24,256]{1,0:T(8,128)S(1)}, u32[]{:S(2)}, u32[]{:S(2)}) collective-permute-start(f32[24,256]{1,0:T(8,128)S(1)} %get-tuple-element.62.m), channel_id=1, source_target_pairs={{1,2},{2,1},{3,4},{4,3},{5,6},{6,5},{7,0},{0,7},{9,10},{10,9},{11,... | collective-permute-start | bytes 73736 | tf_op jit(solution)/shard_map/ppermute | solution.py:492
  25.3 4.8 %collective-permute-start.8 = (f32[24,128]{1,0:T(8,128)S(1)}, f32[24,128]{1,0:T(8,128)S(1)}, u32[]{:S(2)}, u32[]{:S(2)}) collective-permute-start(f32[24,128]{1,0:T(8,128)S(1)} %get-tuple-element.68.m), channel_id=1, source_target_pairs={{0,1},{1,0},{2,3},{3,2},{4,5},{5,4},{6,7},{7,6},{8,9},{9,8},{10,11... | collective-permute-start | bytes 36872 | tf_op jit(solution)/shard_map/ppermute | solution.py:492
  27.8 3.0 %collective-permute-start.7 = (f32[24,128]{1,0:T(8,128)S(1)}, f32[24,128]{1,0:T(8,128)S(1)}, u32[]{:S(2)}, u32[]{:S(2)}) collective-permute-start(f32[24,128]{1,0:T(8,128)S(1)} %get-tuple-element.64.refs_1_.m), channel_id=1, source_target_pairs={{0,1},{1,0},{2,3},{3,2},{4,5},{5,4},{6,7},{7,6},{8,9},{9,8},{10,11... | collective-permute-start | bytes 36872 | tf_op jit(solution)/shard_map/ppermute | solution.py:492
  30.7 14.9 %collective-permute-start.10 = (bf16[96,1280]{1,0:T(8,128)(2,1)S(1)}, bf16[96,1280]{1,0:T(8,128)(2,1)S(1)}, u32[]{:S(2)}, u32[]{:S(2)}) collective-permute-start(bf16[96,1280]{1,0:T(8,128)(2,1)S(1)} %get-tuple-element.84), channel_id=1, source_target_pairs={{0,1},{1,0},{2,3},{3,2},{4,5},{5,4},{6,7},{7,6},{8,9},{9,8},{10,11... | collective-permute-start | bytes 737288 | tf_op jit(solution)/shard_map/ppermute | solution.py:492
  32.1 14.4 %collective-permute-start.11 = (bf16[192,1280]{1,0:T(8,128)(2,1)S(1)}, bf16[192,1280]{1,0:T(8,128)(2,1)S(1)}, u32[]{:S(2)}, u32[]{:S(2)}) collective-permute-start(bf16[192,1280]{1,0:T(8,128)(2,1)S(1)} %get-tuple-element.83.refs_1_), channel_id=1, source_target_pairs={{8,16},{16,8},{9,17},{17,9},{10,18},{18,10},{11,19},{19,11},{12,20... | collective-permute-start | bytes 1474568 | tf_op jit(solution)/shard_map/ppermute | solution.py:492
  37.8 8.8 %collective-permute-start.9 = (bf16[96,1280]{1,0:T(8,128)(2,1)S(1)}, bf16[96,1280]{1,0:T(8,128)(2,1)S(1)}, u32[]{:S(2)}, u32[]{:S(2)}) collective-permute-start(bf16[96,1280]{1,0:T(8,128)(2,1)S(1)} %held.8), channel_id=1, source_target_pairs={{1,2},{2,1},{3,4},{4,3},{5,6},{6,5},{7,0},{0,7},{9,10},{10,9},{11,... | collective-permute-start | bytes 737288 | tf_op jit(solution)/shard_map/ppermute | solution.py:492
  42.5 4.1 %collective-permute-start.12 = (bf16[192,1280]{1,0:T(8,128)(2,1)S(1)}, bf16[192,1280]{1,0:T(8,128)(2,1)S(1)}, u32[]{:S(2)}, u32[]{:S(2)}) collective-permute-start(bf16[192,1280]{1,0:T(8,128)(2,1)S(1)} %get-tuple-element.87), channel_id=1, source_target_pairs={{0,8},{8,0},{16,24},{24,16},{1,9},{9,1},{17,25},{25,17},{2,10},{10... | collective-permute-start | bytes 1474568 | tf_op jit(solution)/shard_map/ppermute | solution.py:492

commit v9 on v8

--- a/solution.py
+++ b/solution.py
@@ -271,13 +271,11 @@
     return peak + jnp.log(total) * LOG2E, (part_a * delta_a + part_b * delta_b) / total
 
 
-def halo_part(group, halo, kp, vp, lat, rows, cols, count):
+def halo_part(group, halo, mask, kp, vp, lat, rows, cols, count):
     edge = RADIUS * rows
     near = edge + 2 * RADIUS * cols
 
-    def kernel(halo_ref, k_ref, v_ref, k_0, k_1, v_0, v_1, out, s_ref, d_ref, bias):
-        queries = halo_query_cell(across(LANES, group * LANES), rows, cols)
-        fill_bias(bias, down(edge) + group * LANES, queries, rows, cols)
+    def kernel(halo_ref, bias, k_ref, v_ref, k_0, k_1, v_0, v_1, out, s_ref, d_ref):
         out[...] = jnp.zeros_like(out)
         for head in range(count):
             key = near_keys(group, k_ref, (k_0, k_1), head)
@@ -289,9 +287,8 @@
             out[count + head : count + head + 1, :] = delta
 
     return call(
-        kernel, f"halo_part_{group}", (halo, kp, vp, *lat),
+        kernel, f"halo_part_{group}", (halo, mask, kp, vp, *lat),
         [full(stat_rows(count), LANES)] + [full(count, near, LANES)] * 2,
-        [pltpu.VMEM((near, LANES), jnp.float32)],
     )
 
 
@@ -317,9 +314,11 @@
     edge = RADIUS * rows
     near = edge + 2 * RADIUS * cols
 
-    def kernel(halo_ref, stat, k_ref, v_ref, k_0, k_1, v_0, v_1, out, s_ref, d_ref, bias):
+    def kernel(halo_ref, stat, k_ref, v_ref, k_0, k_1, v_0, v_1, out, s_ref, d_ref, other, bias):
         queries = halo_query_cell(across(LANES, group * LANES), rows, cols)
         fill_bias(bias, down(edge) + group * LANES, queries, rows, cols)
+        queries = halo_query_cell(across(LANES, (1 - group) * LANES), rows, cols)
+        fill_bias(other, down(edge) + (1 - group) * LANES, queries, rows, cols)
         out[:, LOW] = stat[...]
         out[:, HIGH] = jnp.zeros((out.shape[0], LANES), jnp.float32)
         for head in range(count):
@@ -333,7 +332,7 @@
 
     return call(
         kernel, f"halo_scores_{group}", (halo, own_stat, kp, vp, *lat),
-        [full(stat_rows(count), 2 * LANES)] + [full(count, near, LANES)] * 2,
+        [full(stat_rows(count), 2 * LANES)] + [full(count, near, LANES)] * 2 + [full(near, LANES)],
         [pltpu.VMEM((near, LANES), jnp.float32)],
     )
 
@@ -527,9 +526,9 @@
     *own_stat, lat_s, lat_d = lat_scores(qp, gp, lat, stats, *size)
     theirs_1 = swap_lon(1, own_stat[1])
 
-    mine_0, *scores_0 = halo_scores(0, halo[0], own_stat[0], kp, vp, lat, *size)
+    mine_0, *scores_0, mask_1 = halo_scores(0, halo[0], own_stat[0], kp, vp, lat, *size)
     theirs_0 = swap_lon(0, mine_0)
-    part_1, *scores_1 = halo_part(1, after(halo[1], mine_0), kp, vp, lat, *size)
+    part_1, *scores_1 = halo_part(1, after(halo[1], mine_0), mask_1, kp, vp, lat, *size)
     other_1 = held(swap_lon(1, part_1))
     theirs_0 = held(theirs_0, part_1, flops=1 << 29)
     result_0, stats_0, *lows_0 = halo_finish(0, mine_0, theirs_0, *scores_0, kp, lat[:2], *size)

time: 48.5 us -> 48.5 us (level)
  no operation moved by 1% of the time
where the time goes in v9:
time: 48.5 us; the launch traced here: 48.3 us
  starting transfers between devices  27.5 us (57%)
  Pallas kernels  13.3 us (27%)
  waiting for transfers between devices  6.8 us (14%)
  between operations  0.77 us (2%)
    ppermute x13, starting transfers between devices, swap(): return lax.ppermute(array, axis, pairs)  27.5 us
    pallas_call x15, Pallas kernels, call(): pl.pallas_call(kernel, name=name, in_specs=ins or [VMEM_SPEC] * len(opera...  13.3 us
    ppermute x13, waiting for transfers between devices, swap(): return lax.ppermute(array, axis, pairs)  6.8 us
  transfers between devices with their start and end apart: 13, of which 5 were waited for; matrix products, arithmetic and copies ran while one was open for 0% of the time, Pallas kernels for 20%

profile of v9, /device:TPU:1, one launch (start us, length us, event | category | flops | bytes accessed | tf_op | source)
XLA Modules:
  0.0 48.3 jit_solution(9879214639246585402)
XLA Ops:
  0.6 1.9 %pack_queries.1 = (bf16[256,1280]{1,0:T(8,128)(2,1)S(1)}, bf16[256,1280]{1,0:T(8,128)(2,1)S(1)}, bf16[192,1280]{1,0:T(8,128)(2,1)S(1)}, bf16[208,1280]{1,0:T(8,1...) custom-call(bf16[256,1280]{1,0:T(8,128)(2,1)} %bitcast.7, ...), custom_call_target="tpu_custom_call" | custom-call | tf_op jit(solution)/shard_map/pack_queries/pallas_call | solution.py:91
  2.6 2.1 %collective-permute-start.1 = (bf16[208,1280]{1,0:T(8,128)(2,1)S(1)}, bf16[208,1280]{1,0:T(8,128)(2,1)S(1)}, u32[]{:S(2)}, u32[]{:S(2)}) collective-permute-start(bf16[208,1280]{1,0:T(8,128)(2,1)S(1)} %get-tuple-element.51), channel_id=1, source_target_pairs={{0,1},{1,0},{2,3},{3,2},{4,5},{5,4},{6,7},{7,6},{8,9},{9,8},{10,11... | collective-permute-start | bytes 1597448 | tf_op jit(solution)/shard_map/ppermute | solution.py:491
  4.7 1.0 %collective-permute-start.2 = (bf16[96,1280]{1,0:T(8,128)(2,1)S(1)}, bf16[96,1280]{1,0:T(8,128)(2,1)S(1)}, u32[]{:S(2)}, u32[]{:S(2)}) collective-permute-start(bf16[96,1280]{1,0:T(8,128)(2,1)S(1)} %get-tuple-element.52), channel_id=1, source_target_pairs={{0,8},{8,0},{16,24},{24,16},{1,9},{9,1},{17,25},{25,17},{2,10},{10... | collective-permute-start | bytes 737288 | tf_op jit(solution)/shard_map/ppermute | solution.py:491
  5.7 3.3 %collective-permute-start = (bf16[192,1280]{1,0:T(8,128)(2,1)S(1)}, bf16[192,1280]{1,0:T(8,128)(2,1)S(1)}, u32[]{:S(2)}, u32[]{:S(2)}) collective-permute-start(bf16[192,1280]{1,0:T(8,128)(2,1)S(1)} %get-tuple-element.50), channel_id=1, source_target_pairs={{1,2},{2,1},{3,4},{4,3},{5,6},{6,5},{7,0},{0,7},{9,10},{10,9},{11,... | collective-permute-start | bytes 1474568 | tf_op jit(solution)/shard_map/ppermute | solution.py:491
  8.9 3.3 %collective-permute-start.3 = (bf16[96,1280]{1,0:T(8,128)(2,1)S(1)}, bf16[96,1280]{1,0:T(8,128)(2,1)S(1)}, u32[]{:S(2)}, u32[]{:S(2)}) collective-permute-start(bf16[96,1280]{1,0:T(8,128)(2,1)S(1)} %get-tuple-element.53), channel_id=1, source_target_pairs={{8,16},{16,8},{9,17},{17,9},{10,18},{18,10},{11,19},{19,11},{12,20... | collective-permute-start | bytes 737288 | tf_op jit(solution)/shard_map/ppermute | solution.py:491
  12.2 0.1 collective-permute-start.4
  12.3 0.0 collective-permute-done.2.k_0
  12.3 2.3 %collective-permute-start.5 = (bf16[96,1280]{1,0:T(8,128)(2,1)S(1)}, bf16[96,1280]{1,0:T(8,128)(2,1)S(1)}, u32[]{:S(2)}, u32[]{:S(2)}) collective-permute-start(bf16[96,1280]{1,0:T(8,128)(2,1)S(1)} %get-tuple-element.55), channel_id=1, source_target_pairs={{8,16},{16,8},{9,17},{17,9},{10,18},{18,10},{11,19},{19,11},{12,20... | collective-permute-start | bytes 737288 | tf_op jit(solution)/shard_map/ppermute | solution.py:491
  14.6 1.6 %own_scores.1 = (bf16[256,1280]{1,0:T(8,128)(2,1)S(1)}, bf16[256,1280]{1,0:T(8,128)(2,1)S(1)}, f32[24,128]{1,0:T(8,128)S(1)}, f32[24,128]{1,0:T(8,128)S(1)}, f32...) custom-call(bf16[256,1280]{1,0:T(8,128)(2,1)S(1)} %get-tuple-element.48.q_ref, ...), custom_call_target="tpu_custom_call" | custom-call | tf_op jit(solution)/shard_map/own_scores/pallas_call | solution.py:91
  16.2 0.5 %collective-permute-done.3.k_1 = bf16[96,1280]{1,0:T(8,128)(2,1)S(1)} collective-permute-done((bf16[96,1280]{1,0:T(8,128)(2,1)S(1)}, bf16[96,1280]{1,0:T(8,128)(2,1)S(1)}, u32[]{:S(2)}, u32[]{:S(2)}) %collective-permute-start.3) | collective-permute-done | bytes 245792 | tf_op jit(solution)/shard_map/ppermute | solution.py:491
  16.7 0.0 collective-permute-done.4.v_0
  16.7 3.4 %collective-permute-done.5.v_1 = bf16[96,1280]{1,0:T(8,128)(2,1)S(1)} collective-permute-done((bf16[96,1280]{1,0:T(8,128)(2,1)S(1)}, bf16[96,1280]{1,0:T(8,128)(2,1)S(1)}, u32[]{:S(2)}, u32[]{:S(2)}) %collective-permute-start.5) | collective-permute-done | bytes 245792 | tf_op jit(solution)/shard_map/ppermute | solution.py:491
  20.1 1.0 %lat_scores.1 = (f32[24,128]{1,0:T(8,128)S(1)}, f32[24,128]{1,0:T(8,128)S(1)}, f32[10,192,256]{2,1,0:T(8,128)S(1)}, f32[10,192,256]{2,1,0:T(8,128)S(1)}) custom-call(bf16[256,1280]{1,0:T(8,128)(2,1)S(1)} %get-tuple-element.48.q_ref, bf16[256,1280]{1,0:T(8,128)(2,1)S(1)} %get-tuple-element.49.g_ref, bf16[96,1280]{1,0:T(8,128)(2,1)S(1)} %collective-permute-done.2.k_0, ...), custom_call_target="tpu_custom_call" | custom-call | tf_op jit(solution)/shard_map/lat_scores/pallas_call | solution.py:91
  21.1 0.1 collective-permute-done.halo_ref.h_0
  21.2 0.8 %halo_scores_0.1 = (f32[24,256]{1,0:T(8,128)S(1)}, f32[10,288,128]{2,1,0:T(8,128)S(1)}, f32[10,288,128]{2,1,0:T(8,128)S(1)}, f32[288,128]{1,0:T(8,128)S(1)}) custom-call(bf16[192,1280]{1,0:T(8,128)(2,1)S(1)} %collective-permute-done.halo_ref.h_0, f32[24,128]{1,0:T(8,128)S(1)} %get-tuple-element.60.stat, bf16[256,1280]{1,0:T(8,128)(2,1)S(1)} %get-tuple-element.61.k_ref, ...), custom_call_target="tpu_custom_call" | custom-call | tf_op jit(solution)/shard_map/halo_scores_0/pallas_call | solution.py:91
  22.0 3.3 %collective-permute-start.6 = (f32[24,256]{1,0:T(8,128)S(1)}, f32[24,256]{1,0:T(8,128)S(1)}, u32[]{:S(2)}, u32[]{:S(2)}) collective-permute-start(f32[24,256]{1,0:T(8,128)S(1)} %get-tuple-element.63.m), channel_id=1, source_target_pairs={{1,2},{2,1},{3,4},{4,3},{5,6},{6,5},{7,0},{0,7},{9,10},{10,9},{11,... | collective-permute-start | bytes 73736 | tf_op jit(solution)/shard_map/ppermute | solution.py:491
  25.4 0.0 collective-permute-start.8
  25.4 1.7 %collective-permute-done.1.halo_ref.h_1 = bf16[208,1280]{1,0:T(8,128)(2,1)S(1)} collective-permute-done((bf16[208,1280]{1,0:T(8,128)(2,1)S(1)}, bf16[208,1280]{1,0:T(8,128)(2,1)S(1)}, u32[]{:S(2)}, u32[]{:S(2)}) %collective-permute-start.1) | collective-permute-done | bytes 532512 | tf_op jit(solution)/shard_map/ppermute | solution.py:491
  27.1 0.8 %halo_part_1.1 = (f32[24,128]{1,0:T(8,128)S(1)}, f32[10,288,128]{2,1,0:T(8,128)S(1)}, f32[10,288,128]{2,1,0:T(8,128)S(1)}) custom-call(bf16[208,1280]{1,0:T(8,128)(2,1)S(1)} %collective-permute-done.1.halo_ref.h_1, f32[288,128]{1,0:T(8,128)S(1)} %get-tuple-element.65.bias, bf16[256,1280]{1,0:T(8,128)(2,1)S(1)} %get-tuple-element.61.k_ref, ...), custom_call_target="tpu_custom_call" | custom-call | tf_op jit(solution)/shard_map/halo_part_1/pallas_call | solution.py:91
  27.8 1.7 %collective-permute-start.7 = (f32[24,128]{1,0:T(8,128)S(1)}, f32[24,128]{1,0:T(8,128)S(1)}, u32[]{:S(2)}, u32[]{:S(2)}) collective-permute-start(f32[24,128]{1,0:T(8,128)S(1)} %get-tuple-element.66.refs_1_.m), channel_id=1, source_target_pairs={{0,1},{1,0},{2,3},{3,2},{4,5},{5,4},{6,7},{7,6},{8,9},{9,8},{10,11... | collective-permute-start | bytes 36872 | tf_op jit(solution)/shard_map/ppermute | solution.py:491
  29.6 0.0 collective-permute-done.6.refs_0_
  29.6 0.5 %halo_finish_0.1 = (bf16[96,1280]{1,0:T(8,128)(2,1)S(1)}, f32[24,128]{1,0:T(8,128)S(1)}, bf16[10,288,128]{2,1,0:T(8,128)(2,1)S(1)}, bf16[10,288,128]{2,1,0:T(8,128)(2,1)S(1)}) custom-call(f32[24,256]{1,0:T(8,128)S(1)} %get-tuple-element.63.m, f32[24,256]{1,0:T(8,128)S(1)} %held.5.t, f32[10,288,128]{2,1,0:T(8,128)S(1)} %get-tuple-element.67.s_ref, ...), custom_call_target="tpu_custom_call" | custom-call | tf_op jit(solution)/shard_map/halo_finish_0/pallas_call | solution.py:91
  30.1 0.0 collective-permute-done.8.refs_0_
  30.1 0.5 %halo_rest_1.1 = (bf16[96,1280]{1,0:T(8,128)(2,1)S(1)}, bf16[10,288,128]{2,1,0:T(8,128)(2,1)S(1)}, bf16[10,288,128]{2,1,0:T(8,128)(2,1)S(1)}) custom-call(f32[24,128]{1,0:T(8,128)S(1)} %get-tuple-element.66.refs_1_.m, f32[24,128]{1,0:T(8,128)S(1)} %held.7.t, f32[10,288,128]{2,1,0:T(8,128)S(1)} %get-tuple-element.76.s_ref, ...), custom_call_target="tpu_custom_call" | custom-call | tf_op jit(solution)/shard_map/halo_rest_1/pallas_call | solution.py:91
  30.7 0.1 collective-permute-start.10
  30.8 0.0 collective-permute-done.7.refs_0_
  30.8 1.3 %lat_grads.1 = (bf16[192,1280]{1,0:T(8,128)(2,1)S(1)}, bf16[192,1280]{1,0:T(8,128)(2,1)S(1)}, f32[24,128]{1,0:T(8,128)S(1)}, bf16[10,192,256]{2,1,0:T(8,128)(2,1)S(1)}) custom-call(bf16[256,1280]{1,0:T(8,128)(2,1)S(1)} %get-tuple-element.48.q_ref, bf16[256,1280]{1,0:T(8,128)(2,1)S(1)} %get-tuple-element.49.g_ref, ...), custom_call_target="tpu_custom_call" | custom-call | tf_op jit(solution)/shard_map/lat_grads/pallas_call | solution.py:91
  32.1 5.7 %collective-permute-start.11 = (bf16[192,1280]{1,0:T(8,128)(2,1)S(1)}, bf16[192,1280]{1,0:T(8,128)(2,1)S(1)}, u32[]{:S(2)}, u32[]{:S(2)}) collective-permute-start(bf16[192,1280]{1,0:T(8,128)(2,1)S(1)} %get-tuple-element.85.refs_1_), channel_id=1, source_target_pairs={{8,16},{16,8},{9,17},{17,9},{10,18},{18,10},{11,19},{19,11},{12,20... | collective-permute-start | bytes 1474568 | tf_op jit(solution)/shard_map/ppermute | solution.py:491
  37.8 4.7 %collective-permute-start.9 = (bf16[96,1280]{1,0:T(8,128)(2,1)S(1)}, bf16[96,1280]{1,0:T(8,128)(2,1)S(1)}, u32[]{:S(2)}, u32[]{:S(2)}) collective-permute-start(bf16[96,1280]{1,0:T(8,128)(2,1)S(1)} %held.8), channel_id=1, source_target_pairs={{1,2},{2,1},{3,4},{4,3},{5,6},{6,5},{7,0},{0,7},{9,10},{10,9},{11,... | collective-permute-start | bytes 737288 | tf_op jit(solution)/shard_map/ppermute | solution.py:491
  42.5 0.0 collective-permute-start.12
  42.5 3.0 %own_grads.1 = (f32[256,1280]{1,0:T(8,128)S(1)}, f32[256,1280]{1,0:T(8,128)S(1)}, f32[256,1280]{1,0:T(8,128)S(1)}) custom-call(bf16[256,1280]{1,0:T(8,128)(2,1)S(1)} %get-tuple-element.48.q_ref, bf16[256,1280]{1,0:T(8,128)(2,1)S(1)} %get-tuple-element.49.g_ref, bf16[192,1280]{1,0:T(8,128)(2,1)S(1)} %collective-permute-done.halo_ref.h_0, ...), custom_call_target="tpu_custom_call" | custom-call | tf_op jit(solution)/shard_map/own_grads/pallas_call | solution.py:91
  45.5 0.0 collective-permute-done.10.b_1
  45.6 1.0 %collective-permute-done.9.b_0 = bf16[96,1280]{1,0:T(8,128)(2,1)S(1)} collective-permute-done((bf16[96,1280]{1,0:T(8,128)(2,1)S(1)}, bf16[96,1280]{1,0:T(8,128)(2,1)S(1)}, u32[]{:S(2)}, u32[]{:S(2)}) %collective-permute-start.9) | collective-permute-done | bytes 245792 | tf_op jit(solution)/shard_map/ppermute | solution.py:491
  46.6 0.0 collective-permute-done.11.a_1
  46.6 0.0 collective-permute-done.12.a_0
  46.6 1.7 %finish.1 = (bf16[256,1280]{1,0:T(8,128)(2,1)}, bf16[256,1280]{1,0:T(8,128)(2,1)}, bf16[256,1280]{1,0:T(8,128)(2,1)}) custom-call(f32[256,1280]{1,0:T(8,128)S(1)} %get-tuple-element.84.dq_ref, bf16[96,1280]{1,0:T(8,128)(2,1)S(1)} %collective-permute-done.9.b_0, bf16[96,1280]{1,0:T(8,128)(2,1)S(1)} %collective-permute-done.10.b_1, ...), custom_call_target="tpu_custom_call" | custom-call | tf_op jit(solution)/shard_map/finish/pallas_call | solution.py:91
  (5 shorter events, 0.0 us)
Async XLA Ops:
  2.6 24.5 %collective-permute-start.1 = (bf16[208,1280]{1,0:T(8,128)(2,1)S(1)}, bf16[208,1280]{1,0:T(8,128)(2,1)S(1)}, u32[]{:S(2)}, u32[]{:S(2)}) collective-permute-start(bf16[208,1280]{1,0:T(8,128)(2,1)S(1)} %get-tuple-element.51), channel_id=1, source_target_pairs={{0,1},{1,0},{2,3},{3,2},{4,5},{5,4},{6,7},{7,6},{8,9},{9,8},{10,11... | collective-permute-start | bytes 1597448 | tf_op jit(solution)/shard_map/ppermute | solution.py:491
  4.7 7.6 %collective-permute-start.2 = (bf16[96,1280]{1,0:T(8,128)(2,1)S(1)}, bf16[96,1280]{1,0:T(8,128)(2,1)S(1)}, u32[]{:S(2)}, u32[]{:S(2)}) collective-permute-start(bf16[96,1280]{1,0:T(8,128)(2,1)S(1)} %get-tuple-element.52), channel_id=1, source_target_pairs={{0,8},{8,0},{16,24},{24,16},{1,9},{9,1},{17,25},{25,17},{2,10},{10... | collective-permute-start | bytes 737288 | tf_op jit(solution)/shard_map/ppermute | solution.py:491
  5.7 15.5 %collective-permute-start = (bf16[192,1280]{1,0:T(8,128)(2,1)S(1)}, bf16[192,1280]{1,0:T(8,128)(2,1)S(1)}, u32[]{:S(2)}, u32[]{:S(2)}) collective-permute-start(bf16[192,1280]{1,0:T(8,128)(2,1)S(1)} %get-tuple-element.50), channel_id=1, source_target_pairs={{1,2},{2,1},{3,4},{4,3},{5,6},{6,5},{7,0},{0,7},{9,10},{10,9},{11,... | collective-permute-start | bytes 1474568 | tf_op jit(solution)/shard_map/ppermute | solution.py:491
  8.9 7.8 %collective-permute-start.3 = (bf16[96,1280]{1,0:T(8,128)(2,1)S(1)}, bf16[96,1280]{1,0:T(8,128)(2,1)S(1)}, u32[]{:S(2)}, u32[]{:S(2)}) collective-permute-start(bf16[96,1280]{1,0:T(8,128)(2,1)S(1)} %get-tuple-element.53), channel_id=1, source_target_pairs={{8,16},{16,8},{9,17},{17,9},{10,18},{18,10},{11,19},{19,11},{12,20... | collective-permute-start | bytes 737288 | tf_op jit(solution)/shard_map/ppermute | solution.py:491
  12.2 4.5 %collective-permute-start.4 = (bf16[96,1280]{1,0:T(8,128)(2,1)S(1)}, bf16[96,1280]{1,0:T(8,128)(2,1)S(1)}, u32[]{:S(2)}, u32[]{:S(2)}) collective-permute-start(bf16[96,1280]{1,0:T(8,128)(2,1)S(1)} %get-tuple-element.54), channel_id=1, source_target_pairs={{0,8},{8,0},{16,24},{24,16},{1,9},{9,1},{17,25},{25,17},{2,10},{10... | collective-permute-start | bytes 737288 | tf_op jit(solution)/shard_map/ppermute | solution.py:491
  12.3 7.8 %collective-permute-start.5 = (bf16[96,1280]{1,0:T(8,128)(2,1)S(1)}, bf16[96,1280]{1,0:T(8,128)(2,1)S(1)}, u32[]{:S(2)}, u32[]{:S(2)}) collective-permute-start(bf16[96,1280]{1,0:T(8,128)(2,1)S(1)} %get-tuple-element.55), channel_id=1, source_target_pairs={{8,16},{16,8},{9,17},{17,9},{10,18},{18,10},{11,19},{19,11},{12,20... | collective-permute-start | bytes 737288 | tf_op jit(solution)/shard_map/ppermute | solution.py:491
  22.0 7.5 %collective-permute-start.6 = (f32[24,256]{1,0:T(8,128)S(1)}, f32[24,256]{1,0:T(8,128)S(1)}, u32[]{:S(2)}, u32[]{:S(2)}) collective-permute-start(f32[24,256]{1,0:T(8,128)S(1)} %get-tuple-element.63.m), channel_id=1, source_target_pairs={{1,2},{2,1},{3,4},{4,3},{5,6},{6,5},{7,0},{0,7},{9,10},{10,9},{11,... | collective-permute-start | bytes 73736 | tf_op jit(solution)/shard_map/ppermute | solution.py:491
  25.4 4.7 %collective-permute-start.8 = (f32[24,128]{1,0:T(8,128)S(1)}, f32[24,128]{1,0:T(8,128)S(1)}, u32[]{:S(2)}, u32[]{:S(2)}) collective-permute-start(f32[24,128]{1,0:T(8,128)S(1)} %get-tuple-element.70.m), channel_id=1, source_target_pairs={{0,1},{1,0},{2,3},{3,2},{4,5},{5,4},{6,7},{7,6},{8,9},{9,8},{10,11... | collective-permute-start | bytes 36872 | tf_op jit(solution)/shard_map/ppermute | solution.py:491
  27.8 2.9 %collective-permute-start.7 = (f32[24,128]{1,0:T(8,128)S(1)}, f32[24,128]{1,0:T(8,128)S(1)}, u32[]{:S(2)}, u32[]{:S(2)}) collective-permute-start(f32[24,128]{1,0:T(8,128)S(1)} %get-tuple-element.66.refs_1_.m), channel_id=1, source_target_pairs={{0,1},{1,0},{2,3},{3,2},{4,5},{5,4},{6,7},{7,6},{8,9},{9,8},{10,11... | collective-permute-start | bytes 36872 | tf_op jit(solution)/shard_map/ppermute | solution.py:491
  30.7 14.9 %collective-permute-start.10 = (bf16[96,1280]{1,0:T(8,128)(2,1)S(1)}, bf16[96,1280]{1,0:T(8,128)(2,1)S(1)}, u32[]{:S(2)}, u32[]{:S(2)}) collective-permute-start(bf16[96,1280]{1,0:T(8,128)(2,1)S(1)} %get-tuple-element.86), channel_id=1, source_target_pairs={{0,1},{1,0},{2,3},{3,2},{4,5},{5,4},{6,7},{7,6},{8,9},{9,8},{10,11... | collective-permute-start | bytes 737288 | tf_op jit(solution)/shard_map/ppermute | solution.py:491
  32.1 14.5 %collective-permute-start.11 = (bf16[192,1280]{1,0:T(8,128)(2,1)S(1)}, bf16[192,1280]{1,0:T(8,128)(2,1)S(1)}, u32[]{:S(2)}, u32[]{:S(2)}) collective-permute-start(bf16[192,1280]{1,0:T(8,128)(2,1)S(1)} %get-tuple-element.85.refs_1_), channel_id=1, source_target_pairs={{8,16},{16,8},{9,17},{17,9},{10,18},{18,10},{11,19},{19,11},{12,20... | collective-permute-start | bytes 1474568 | tf_op jit(solution)/shard_map/ppermute | solution.py:491
  37.8 8.8 %collective-permute-start.9 = (bf16[96,1280]{1,0:T(8,128)(2,1)S(1)}, bf16[96,1280]{1,0:T(8,128)(2,1)S(1)}, u32[]{:S(2)}, u32[]{:S(2)}) collective-permute-start(bf16[96,1280]{1,0:T(8,128)(2,1)S(1)} %held.8), channel_id=1, source_target_pairs={{1,2},{2,1},{3,4},{4,3},{5,6},{6,5},{7,0},{0,7},{9,10},{10,9},{11,... | collective-permute-start | bytes 737288 | tf_op jit(solution)/shard_map/ppermute | solution.py:491
  42.5 4.1 %collective-permute-start.12 = (bf16[192,1280]{1,0:T(8,128)(2,1)S(1)}, bf16[192,1280]{1,0:T(8,128)(2,1)S(1)}, u32[]{:S(2)}, u32[]{:S(2)}) collective-permute-start(bf16[192,1280]{1,0:T(8,128)(2,1)S(1)} %get-tuple-element.89), channel_id=1, source_target_pairs={{0,8},{8,0},{16,24},{24,16},{1,9},{9,1},{17,25},{25,17},{2,10},{10... | collective-permute-start | bytes 1474568 | tf_op jit(solution)/shard_map/ppermute | solution.py:491

commit v10 on v9

--- a/solution.py
+++ b/solution.py
@@ -404,7 +404,7 @@
 
     def kernel(
         q_ref, g_ref, h_0, h_1, stat_0, stat_1, lat_ref, s_ref, d_ref, p_0, l_0, p_1, l_1, k_ref, k_0, k_1,
-        dq_ref, dk_ref, dv_ref, sums,
+        dq_ref, dk_ref, dv_ref, spread, sums,
     ):
         for head in range(count):
             lanes = lanes_of(head)
@@ -423,6 +423,10 @@
                     near = inside[at : at + edge] + dot(x[head, :edge, :], halo_head(h, edge, part, head), (1, 0))
                     sums[1 + part, at : at + edge, lanes] = near * scale
                     sums[1 + part, at + edge : at + LANES, lanes] = inside[at + edge : at + LANES] * scale
+        position = across(2 * edge)
+        place = jnp.where(position < edge, position, position - edge + LANES)
+        row, col = own_query_cell(place, rows, cols)
+        spread[...] = jnp.where(down(own) == row * cols + col, 1.0, 0.0).astype(jnp.bfloat16)
         order = restore(rows, cols)
         twice = jnp.concatenate([order, order], axis=1)
         for place, result in enumerate((dq_ref, dk_ref, dv_ref)):
@@ -435,7 +439,7 @@
     return call(
         kernel, "own_grads",
         (qp, gp, *halo, *stats, lat_low, scores, weight_grad, *lows[0], *lows[1], kp, *lat),
-        [full(own, width)] * 3, [pltpu.VMEM((3, own, width), jnp.float32)],
+        [full(own, width)] * 3 + [low(own, 2 * edge)], [pltpu.VMEM((3, own, width), jnp.float32)],
     )
 
 
@@ -445,10 +449,10 @@
     return jnp.where(down(own) == row * cols + col, 1.0, 0.0).astype(jnp.bfloat16)
 
 
-def finish(query_grad, back, key_grad, value_grad, lat_back, rows, cols, count):
+def finish(query_grad, spread, back, key_grad, value_grad, lat_back, rows, cols, count):
     own, width, edge, lat_edge = rows * cols, count * HEAD_DIM, RADIUS * rows, RADIUS * cols
 
-    def kernel(dq_ref, b_0, b_1, dk_ref, dv_ref, a_1, a_0, out_q, out_k, out_v, done_q, done_k, done_v, sems):
+    def kernel(dq_ref, spread, b_0, b_1, dk_ref, dv_ref, a_1, a_0, out_q, out_k, out_v, done_q, done_k, done_v, sems):
         copies = []
 
         def write(done, out):
@@ -463,20 +467,16 @@
                 added = arrived[part * lat_edge : (part + 1) * lat_edge, :].astype(jnp.float32)
                 done[pl.ds(start, lat_edge), :] = (grad[pl.ds(start, lat_edge), :] + added).astype(jnp.bfloat16)
             write(done, out)
-        position = across(2 * edge)
-        place = jnp.where(position < edge, position, position - edge + LANES)
-        row, col = own_query_cell(place, rows, cols)
-        spread = jnp.where(down(own) == row * cols + col, 1.0, 0.0).astype(jnp.bfloat16)
         for at in range(0, width, BLOCK):
             lanes = slice(at, at + BLOCK)
             arrived = jnp.concatenate([b_0[:, lanes], b_1[:, lanes]], axis=0)
-            done_q[:, lanes] = (dq_ref[:, lanes] + dot(spread, arrived, (1, 0))).astype(jnp.bfloat16)
+            done_q[:, lanes] = (dq_ref[:, lanes] + dot(spread[...], arrived, (1, 0))).astype(jnp.bfloat16)
         write(done_q, out_q)
         for copy in copies:
             copy.wait()
 
     return call(
-        kernel, "finish", (query_grad, *back, key_grad, value_grad, *lat_back), [low(own, width)] * 3,
+        kernel, "finish", (query_grad, spread, *back, key_grad, value_grad, *lat_back), [low(own, width)] * 3,
         [pltpu.VMEM((own, width), jnp.bfloat16)] * 3 + [pltpu.SemaphoreType.DMA((3,))],
         outs=[HBM_SPEC] * 3,
     )
@@ -538,12 +538,12 @@
     *lat_back, stats_1, lat_low = lat_grads(
         qp, gp, halo, stats_0, own_stat[1], other_1, lat_s, lat_d, (lows_0, lows_1), *size
     )
-    dq, dk, dv = own_grads(
+    dq, dk, dv, spread = own_grads(
         qp, gp, halo, (stats_0, stats_1), lat_low, own_s, own_d, (lows_0, lows_1), kp, lat[:2], *size
     )
     back = [swap_lon(0, held(result_0, lat_back[1], flops=1 << 29)), back_1]
     lat_back = [swap_lat(slot, lat_back[slot]) for slot in (1, 0)]
-    outs = finish(dq, back, held(dk), dv, lat_back, *size)
+    outs = finish(dq, spread, back, held(dk), dv, lat_back, *size)
     shape = (rows, cols, width)
     return tuple(x.reshape(shape) for x in outs)
 

time: 48.5 us -> 48.5 us (level)
  no operation moved by 1% of the time
where the time goes in v10:
time: 48.5 us; the launch traced here: 48.3 us
  starting transfers between devices  27.5 us (57%)
  Pallas kernels  13.3 us (27%)
  waiting for transfers between devices  6.78 us (14%)
  between operations  0.77 us (2%)
    ppermute x13, starting transfers between devices, swap(): return lax.ppermute(array, axis, pairs)  27.5 us
    pallas_call x15, Pallas kernels, call(): pl.pallas_call(kernel, name=name, in_specs=ins or [VMEM_SPEC] * len(opera...  13.3 us
    ppermute x13, waiting for transfers between devices, swap(): return lax.ppermute(array, axis, pairs)  6.78 us
  transfers between devices with their start and end apart: 13, of which 5 were waited for; matrix products, arithmetic and copies ran while one was open for 0% of the time, Pallas kernels for 20%

profile of v10, /device:TPU:1, one launch (start us, length us, event | category | flops | bytes accessed | tf_op | source)
XLA Modules:
  0.0 48.3 jit_solution(11516985615147521593)
XLA Ops:
  0.6 1.9 %pack_queries.1 = (bf16[256,1280]{1,0:T(8,128)(2,1)S(1)}, bf16[256,1280]{1,0:T(8,128)(2,1)S(1)}, bf16[192,1280]{1,0:T(8,128)(2,1)S(1)}, bf16[208,1280]{1,0:T(8,1...) custom-call(bf16[256,1280]{1,0:T(8,128)(2,1)} %bitcast.7, ...), custom_call_target="tpu_custom_call" | custom-call | tf_op jit(solution)/shard_map/pack_queries/pallas_call | solution.py:91
  2.6 2.1 %collective-permute-start.1 = (bf16[208,1280]{1,0:T(8,128)(2,1)S(1)}, bf16[208,1280]{1,0:T(8,128)(2,1)S(1)}, u32[]{:S(2)}, u32[]{:S(2)}) collective-permute-start(bf16[208,1280]{1,0:T(8,128)(2,1)S(1)} %get-tuple-element.52), channel_id=1, source_target_pairs={{0,1},{1,0},{2,3},{3,2},{4,5},{5,4},{6,7},{7,6},{8,9},{9,8},{10,11... | collective-permute-start | bytes 1597448 | tf_op jit(solution)/shard_map/ppermute | solution.py:491
  4.7 1.0 %collective-permute-start.2 = (bf16[96,1280]{1,0:T(8,128)(2,1)S(1)}, bf16[96,1280]{1,0:T(8,128)(2,1)S(1)}, u32[]{:S(2)}, u32[]{:S(2)}) collective-permute-start(bf16[96,1280]{1,0:T(8,128)(2,1)S(1)} %get-tuple-element.53), channel_id=1, source_target_pairs={{0,8},{8,0},{16,24},{24,16},{1,9},{9,1},{17,25},{25,17},{2,10},{10... | collective-permute-start | bytes 737288 | tf_op jit(solution)/shard_map/ppermute | solution.py:491
  5.7 3.3 %collective-permute-start = (bf16[192,1280]{1,0:T(8,128)(2,1)S(1)}, bf16[192,1280]{1,0:T(8,128)(2,1)S(1)}, u32[]{:S(2)}, u32[]{:S(2)}) collective-permute-start(bf16[192,1280]{1,0:T(8,128)(2,1)S(1)} %get-tuple-element.51), channel_id=1, source_target_pairs={{1,2},{2,1},{3,4},{4,3},{5,6},{6,5},{7,0},{0,7},{9,10},{10,9},{11,... | collective-permute-start | bytes 1474568 | tf_op jit(solution)/shard_map/ppermute | solution.py:491
  8.9 3.3 %collective-permute-start.3 = (bf16[96,1280]{1,0:T(8,128)(2,1)S(1)}, bf16[96,1280]{1,0:T(8,128)(2,1)S(1)}, u32[]{:S(2)}, u32[]{:S(2)}) collective-permute-start(bf16[96,1280]{1,0:T(8,128)(2,1)S(1)} %get-tuple-element.54), channel_id=1, source_target_pairs={{8,16},{16,8},{9,17},{17,9},{10,18},{18,10},{11,19},{19,11},{12,20... | collective-permute-start | bytes 737288 | tf_op jit(solution)/shard_map/ppermute | solution.py:491
  12.2 0.1 collective-permute-start.4
  12.3 0.0 collective-permute-done.2.k_0
  12.3 2.3 %collective-permute-start.5 = (bf16[96,1280]{1,0:T(8,128)(2,1)S(1)}, bf16[96,1280]{1,0:T(8,128)(2,1)S(1)}, u32[]{:S(2)}, u32[]{:S(2)}) collective-permute-start(bf16[96,1280]{1,0:T(8,128)(2,1)S(1)} %get-tuple-element.56), channel_id=1, source_target_pairs={{8,16},{16,8},{9,17},{17,9},{10,18},{18,10},{11,19},{19,11},{12,20... | collective-permute-start | bytes 737288 | tf_op jit(solution)/shard_map/ppermute | solution.py:491
  14.6 1.6 %own_scores.1 = (bf16[256,1280]{1,0:T(8,128)(2,1)S(1)}, bf16[256,1280]{1,0:T(8,128)(2,1)S(1)}, f32[24,128]{1,0:T(8,128)S(1)}, f32[24,128]{1,0:T(8,128)S(1)}, f32...) custom-call(bf16[256,1280]{1,0:T(8,128)(2,1)S(1)} %get-tuple-element.49.q_ref, ...), custom_call_target="tpu_custom_call" | custom-call | tf_op jit(solution)/shard_map/own_scores/pallas_call | solution.py:91
  16.2 0.5 %collective-permute-done.3.k_1 = bf16[96,1280]{1,0:T(8,128)(2,1)S(1)} collective-permute-done((bf16[96,1280]{1,0:T(8,128)(2,1)S(1)}, bf16[96,1280]{1,0:T(8,128)(2,1)S(1)}, u32[]{:S(2)}, u32[]{:S(2)}) %collective-permute-start.3) | collective-permute-done | bytes 245792 | tf_op jit(solution)/shard_map/ppermute | solution.py:491
  16.7 0.0 collective-permute-done.4.v_0
  16.7 3.4 %collective-permute-done.5.v_1 = bf16[96,1280]{1,0:T(8,128)(2,1)S(1)} collective-permute-done((bf16[96,1280]{1,0:T(8,128)(2,1)S(1)}, bf16[96,1280]{1,0:T(8,128)(2,1)S(1)}, u32[]{:S(2)}, u32[]{:S(2)}) %collective-permute-start.5) | collective-permute-done | bytes 245792 | tf_op jit(solution)/shard_map/ppermute | solution.py:491
  20.1 1.0 %lat_scores.1 = (f32[24,128]{1,0:T(8,128)S(1)}, f32[24,128]{1,0:T(8,128)S(1)}, f32[10,192,256]{2,1,0:T(8,128)S(1)}, f32[10,192,256]{2,1,0:T(8,128)S(1)}) custom-call(bf16[256,1280]{1,0:T(8,128)(2,1)S(1)} %get-tuple-element.49.q_ref, bf16[256,1280]{1,0:T(8,128)(2,1)S(1)} %get-tuple-element.50.g_ref, bf16[96,1280]{1,0:T(8,128)(2,1)S(1)} %collective-permute-done.2.k_0, ...), custom_call_target="tpu_custom_call" | custom-call | tf_op jit(solution)/shard_map/lat_scores/pallas_call | solution.py:91
  21.1 0.1 collective-permute-done.halo_ref.h_0
  21.2 0.8 %halo_scores_0.1 = (f32[24,256]{1,0:T(8,128)S(1)}, f32[10,288,128]{2,1,0:T(8,128)S(1)}, f32[10,288,128]{2,1,0:T(8,128)S(1)}, f32[288,128]{1,0:T(8,128)S(1)}) custom-call(bf16[192,1280]{1,0:T(8,128)(2,1)S(1)} %collective-permute-done.halo_ref.h_0, f32[24,128]{1,0:T(8,128)S(1)} %get-tuple-element.61.stat, bf16[256,1280]{1,0:T(8,128)(2,1)S(1)} %get-tuple-element.62.k_ref, ...), custom_call_target="tpu_custom_call" | custom-call | tf_op jit(solution)/shard_map/halo_scores_0/pallas_call | solution.py:91
  22.1 3.3 %collective-permute-start.6 = (f32[24,256]{1,0:T(8,128)S(1)}, f32[24,256]{1,0:T(8,128)S(1)}, u32[]{:S(2)}, u32[]{:S(2)}) collective-permute-start(f32[24,256]{1,0:T(8,128)S(1)} %get-tuple-element.64.m), channel_id=1, source_target_pairs={{1,2},{2,1},{3,4},{4,3},{5,6},{6,5},{7,0},{0,7},{9,10},{10,9},{11,... | collective-permute-start | bytes 73736 | tf_op jit(solution)/shard_map/ppermute | solution.py:491
  25.4 0.0 collective-permute-start.8
  25.4 1.7 %collective-permute-done.1.halo_ref.h_1 = bf16[208,1280]{1,0:T(8,128)(2,1)S(1)} collective-permute-done((bf16[208,1280]{1,0:T(8,128)(2,1)S(1)}, bf16[208,1280]{1,0:T(8,128)(2,1)S(1)}, u32[]{:S(2)}, u32[]{:S(2)}) %collective-permute-start.1) | collective-permute-done | bytes 532512 | tf_op jit(solution)/shard_map/ppermute | solution.py:491
  27.1 0.8 %halo_part_1.1 = (f32[24,128]{1,0:T(8,128)S(1)}, f32[10,288,128]{2,1,0:T(8,128)S(1)}, f32[10,288,128]{2,1,0:T(8,128)S(1)}) custom-call(bf16[208,1280]{1,0:T(8,128)(2,1)S(1)} %collective-permute-done.1.halo_ref.h_1, f32[288,128]{1,0:T(8,128)S(1)} %get-tuple-element.66.bias, bf16[256,1280]{1,0:T(8,128)(2,1)S(1)} %get-tuple-element.62.k_ref, ...), custom_call_target="tpu_custom_call" | custom-call | tf_op jit(solution)/shard_map/halo_part_1/pallas_call | solution.py:91
  27.8 1.7 %collective-permute-start.7 = (f32[24,128]{1,0:T(8,128)S(1)}, f32[24,128]{1,0:T(8,128)S(1)}, u32[]{:S(2)}, u32[]{:S(2)}) collective-permute-start(f32[24,128]{1,0:T(8,128)S(1)} %get-tuple-element.67.refs_1_.m), channel_id=1, source_target_pairs={{0,1},{1,0},{2,3},{3,2},{4,5},{5,4},{6,7},{7,6},{8,9},{9,8},{10,11... | collective-permute-start | bytes 36872 | tf_op jit(solution)/shard_map/ppermute | solution.py:491
  29.6 0.0 collective-permute-done.6.refs_0_
  29.6 0.6 %halo_finish_0.1 = (bf16[96,1280]{1,0:T(8,128)(2,1)S(1)}, f32[24,128]{1,0:T(8,128)S(1)}, bf16[10,288,128]{2,1,0:T(8,128)(2,1)S(1)}, bf16[10,288,128]{2,1,0:T(8,128)(2,1)S(1)}) custom-call(f32[24,256]{1,0:T(8,128)S(1)} %get-tuple-element.64.m, f32[24,256]{1,0:T(8,128)S(1)} %held.5.t, f32[10,288,128]{2,1,0:T(8,128)S(1)} %get-tuple-element.68.s_ref, ...), custom_call_target="tpu_custom_call" | custom-call | tf_op jit(solution)/shard_map/halo_finish_0/pallas_call | solution.py:91
  30.1 0.0 collective-permute-done.8.refs_0_
  30.2 0.5 %halo_rest_1.1 = (bf16[96,1280]{1,0:T(8,128)(2,1)S(1)}, bf16[10,288,128]{2,1,0:T(8,128)(2,1)S(1)}, bf16[10,288,128]{2,1,0:T(8,128)(2,1)S(1)}) custom-call(f32[24,128]{1,0:T(8,128)S(1)} %get-tuple-element.67.refs_1_.m, f32[24,128]{1,0:T(8,128)S(1)} %held.7.t, f32[10,288,128]{2,1,0:T(8,128)S(1)} %get-tuple-element.77.s_ref, ...), custom_call_target="tpu_custom_call" | custom-call | tf_op jit(solution)/shard_map/halo_rest_1/pallas_call | solution.py:91
  30.7 0.1 collective-permute-start.10
  30.8 0.0 collective-permute-done.7.refs_0_
  30.8 1.3 %lat_grads.1 = (bf16[192,1280]{1,0:T(8,128)(2,1)S(1)}, bf16[192,1280]{1,0:T(8,128)(2,1)S(1)}, f32[24,128]{1,0:T(8,128)S(1)}, bf16[10,192,256]{2,1,0:T(8,128)(2,1)S(1)}) custom-call(bf16[256,1280]{1,0:T(8,128)(2,1)S(1)} %get-tuple-element.49.q_ref, bf16[256,1280]{1,0:T(8,128)(2,1)S(1)} %get-tuple-element.50.g_ref, ...), custom_call_target="tpu_custom_call" | custom-call | tf_op jit(solution)/shard_map/lat_grads/pallas_call | solution.py:91
  32.1 5.6 %collective-permute-start.11 = (bf16[192,1280]{1,0:T(8,128)(2,1)S(1)}, bf16[192,1280]{1,0:T(8,128)(2,1)S(1)}, u32[]{:S(2)}, u32[]{:S(2)}) collective-permute-start(bf16[192,1280]{1,0:T(8,128)(2,1)S(1)} %get-tuple-element.87.refs_1_), channel_id=1, source_target_pairs={{8,16},{16,8},{9,17},{17,9},{10,18},{18,10},{11,19},{19,11},{12,20... | collective-permute-start | bytes 1474568 | tf_op jit(solution)/shard_map/ppermute | solution.py:491
  37.8 4.7 %collective-permute-start.9 = (bf16[96,1280]{1,0:T(8,128)(2,1)S(1)}, bf16[96,1280]{1,0:T(8,128)(2,1)S(1)}, u32[]{:S(2)}, u32[]{:S(2)}) collective-permute-start(bf16[96,1280]{1,0:T(8,128)(2,1)S(1)} %held.8), channel_id=1, source_target_pairs={{1,2},{2,1},{3,4},{4,3},{5,6},{6,5},{7,0},{0,7},{9,10},{10,9},{11,... | collective-permute-start | bytes 737288 | tf_op jit(solution)/shard_map/ppermute | solution.py:491
  42.5 0.0 collective-permute-start.12
  42.5 3.0 %own_grads.1 = (f32[256,1280]{1,0:T(8,128)S(1)}, f32[256,1280]{1,0:T(8,128)S(1)}, f32[256,1280]{1,0:T(8,128)S(1)}, bf16[256,192]{1,0:T(8,128)(2,1)S(1)}) custom-call(bf16[256,1280]{1,0:T(8,128)(2,1)S(1)} %get-tuple-element.49.q_ref, bf16[256,1280]{1,0:T(8,128)(2,1)S(1)} %get-tuple-element.50.g_ref, bf16[192,1280]{1,0:T(8,128)(2,1)S(1)} %collective-permute-done.halo_ref.h_0, ...), custom_call_target="tpu_custom_call" | custom-call | tf_op jit(solution)/shard_map/own_grads/pallas_call | solution.py:91
  45.6 0.0 collective-permute-done.10.b_1
  45.6 1.0 %collective-permute-done.9.b_0 = bf16[96,1280]{1,0:T(8,128)(2,1)S(1)} collective-permute-done((bf16[96,1280]{1,0:T(8,128)(2,1)S(1)}, bf16[96,1280]{1,0:T(8,128)(2,1)S(1)}, u32[]{:S(2)}, u32[]{:S(2)}) %collective-permute-start.9) | collective-permute-done | bytes 245792 | tf_op jit(solution)/shard_map/ppermute | solution.py:491
  46.6 0.0 collective-permute-done.11.a_1
  46.6 0.0 collective-permute-done.12.a_0
  46.6 1.7 %finish.1 = (bf16[256,1280]{1,0:T(8,128)(2,1)}, bf16[256,1280]{1,0:T(8,128)(2,1)}, bf16[256,1280]{1,0:T(8,128)(2,1)}) custom-call(f32[256,1280]{1,0:T(8,128)S(1)} %get-tuple-element.85.dq_ref, bf16[256,192]{1,0:T(8,128)(2,1)S(1)} %get-tuple-element.86.spread, bf16[96,1280]{1,0:T(8,128)(2,1)S(1)} %collective-permute-done.9.b_0, ...), custom_call_target="tpu_custom_call" | custom-call | tf_op jit(solution)/shard_map/finish/pallas_call | solution.py:91
  (5 shorter events, 0.0 us)
Async XLA Ops:
  2.6 24.5 %collective-permute-start.1 = (bf16[208,1280]{1,0:T(8,128)(2,1)S(1)}, bf16[208,1280]{1,0:T(8,128)(2,1)S(1)}, u32[]{:S(2)}, u32[]{:S(2)}) collective-permute-start(bf16[208,1280]{1,0:T(8,128)(2,1)S(1)} %get-tuple-element.52), channel_id=1, source_target_pairs={{0,1},{1,0},{2,3},{3,2},{4,5},{5,4},{6,7},{7,6},{8,9},{9,8},{10,11... | collective-permute-start | bytes 1597448 | tf_op jit(solution)/shard_map/ppermute | solution.py:491
  4.7 7.6 %collective-permute-start.2 = (bf16[96,1280]{1,0:T(8,128)(2,1)S(1)}, bf16[96,1280]{1,0:T(8,128)(2,1)S(1)}, u32[]{:S(2)}, u32[]{:S(2)}) collective-permute-start(bf16[96,1280]{1,0:T(8,128)(2,1)S(1)} %get-tuple-element.53), channel_id=1, source_target_pairs={{0,8},{8,0},{16,24},{24,16},{1,9},{9,1},{17,25},{25,17},{2,10},{10... | collective-permute-start | bytes 737288 | tf_op jit(solution)/shard_map/ppermute | solution.py:491
  5.7 15.5 %collective-permute-start = (bf16[192,1280]{1,0:T(8,128)(2,1)S(1)}, bf16[192,1280]{1,0:T(8,128)(2,1)S(1)}, u32[]{:S(2)}, u32[]{:S(2)}) collective-permute-start(bf16[192,1280]{1,0:T(8,128)(2,1)S(1)} %get-tuple-element.51), channel_id=1, source_target_pairs={{1,2},{2,1},{3,4},{4,3},{5,6},{6,5},{7,0},{0,7},{9,10},{10,9},{11,... | collective-permute-start | bytes 1474568 | tf_op jit(solution)/shard_map/ppermute | solution.py:491
  8.9 7.8 %collective-permute-start.3 = (bf16[96,1280]{1,0:T(8,128)(2,1)S(1)}, bf16[96,1280]{1,0:T(8,128)(2,1)S(1)}, u32[]{:S(2)}, u32[]{:S(2)}) collective-permute-start(bf16[96,1280]{1,0:T(8,128)(2,1)S(1)} %get-tuple-element.54), channel_id=1, source_target_pairs={{8,16},{16,8},{9,17},{17,9},{10,18},{18,10},{11,19},{19,11},{12,20... | collective-permute-start | bytes 737288 | tf_op jit(solution)/shard_map/ppermute | solution.py:491
  12.2 4.5 %collective-permute-start.4 = (bf16[96,1280]{1,0:T(8,128)(2,1)S(1)}, bf16[96,1280]{1,0:T(8,128)(2,1)S(1)}, u32[]{:S(2)}, u32[]{:S(2)}) collective-permute-start(bf16[96,1280]{1,0:T(8,128)(2,1)S(1)} %get-tuple-element.55), channel_id=1, source_target_pairs={{0,8},{8,0},{16,24},{24,16},{1,9},{9,1},{17,25},{25,17},{2,10},{10... | collective-permute-start | bytes 737288 | tf_op jit(solution)/shard_map/ppermute | solution.py:491
  12.3 7.8 %collective-permute-start.5 = (bf16[96,1280]{1,0:T(8,128)(2,1)S(1)}, bf16[96,1280]{1,0:T(8,128)(2,1)S(1)}, u32[]{:S(2)}, u32[]{:S(2)}) collective-permute-start(bf16[96,1280]{1,0:T(8,128)(2,1)S(1)} %get-tuple-element.56), channel_id=1, source_target_pairs={{8,16},{16,8},{9,17},{17,9},{10,18},{18,10},{11,19},{19,11},{12,20... | collective-permute-start | bytes 737288 | tf_op jit(solution)/shard_map/ppermute | solution.py:491
  22.1 7.5 %collective-permute-start.6 = (f32[24,256]{1,0:T(8,128)S(1)}, f32[24,256]{1,0:T(8,128)S(1)}, u32[]{:S(2)}, u32[]{:S(2)}) collective-permute-start(f32[24,256]{1,0:T(8,128)S(1)} %get-tuple-element.64.m), channel_id=1, source_target_pairs={{1,2},{2,1},{3,4},{4,3},{5,6},{6,5},{7,0},{0,7},{9,10},{10,9},{11,... | collective-permute-start | bytes 73736 | tf_op jit(solution)/shard_map/ppermute | solution.py:491
  25.4 4.8 %collective-permute-start.8 = (f32[24,128]{1,0:T(8,128)S(1)}, f32[24,128]{1,0:T(8,128)S(1)}, u32[]{:S(2)}, u32[]{:S(2)}) collective-permute-start(f32[24,128]{1,0:T(8,128)S(1)} %get-tuple-element.71.m), channel_id=1, source_target_pairs={{0,1},{1,0},{2,3},{3,2},{4,5},{5,4},{6,7},{7,6},{8,9},{9,8},{10,11... | collective-permute-start | bytes 36872 | tf_op jit(solution)/shard_map/ppermute | solution.py:491
  27.8 3.0 %collective-permute-start.7 = (f32[24,128]{1,0:T(8,128)S(1)}, f32[24,128]{1,0:T(8,128)S(1)}, u32[]{:S(2)}, u32[]{:S(2)}) collective-permute-start(f32[24,128]{1,0:T(8,128)S(1)} %get-tuple-element.67.refs_1_.m), channel_id=1, source_target_pairs={{0,1},{1,0},{2,3},{3,2},{4,5},{5,4},{6,7},{7,6},{8,9},{9,8},{10,11... | collective-permute-start | bytes 36872 | tf_op jit(solution)/shard_map/ppermute | solution.py:491
  30.7 14.9 %collective-permute-start.10 = (bf16[96,1280]{1,0:T(8,128)(2,1)S(1)}, bf16[96,1280]{1,0:T(8,128)(2,1)S(1)}, u32[]{:S(2)}, u32[]{:S(2)}) collective-permute-start(bf16[96,1280]{1,0:T(8,128)(2,1)S(1)} %get-tuple-element.88), channel_id=1, source_target_pairs={{0,1},{1,0},{2,3},{3,2},{4,5},{5,4},{6,7},{7,6},{8,9},{9,8},{10,11... | collective-permute-start | bytes 737288 | tf_op jit(solution)/shard_map/ppermute | solution.py:491
  32.1 14.4 %collective-permute-start.11 = (bf16[192,1280]{1,0:T(8,128)(2,1)S(1)}, bf16[192,1280]{1,0:T(8,128)(2,1)S(1)}, u32[]{:S(2)}, u32[]{:S(2)}) collective-permute-start(bf16[192,1280]{1,0:T(8,128)(2,1)S(1)} %get-tuple-element.87.refs_1_), channel_id=1, source_target_pairs={{8,16},{16,8},{9,17},{17,9},{10,18},{18,10},{11,19},{19,11},{12,20... | collective-permute-start | bytes 1474568 | tf_op jit(solution)/shard_map/ppermute | solution.py:491
  37.8 8.8 %collective-permute-start.9 = (bf16[96,1280]{1,0:T(8,128)(2,1)S(1)}, bf16[96,1280]{1,0:T(8,128)(2,1)S(1)}, u32[]{:S(2)}, u32[]{:S(2)}) collective-permute-start(bf16[96,1280]{1,0:T(8,128)(2,1)S(1)} %held.8), channel_id=1, source_target_pairs={{1,2},{2,1},{3,4},{4,3},{5,6},{6,5},{7,0},{0,7},{9,10},{10,9},{11,... | collective-permute-start | bytes 737288 | tf_op jit(solution)/shard_map/ppermute | solution.py:491
  42.5 4.1 %collective-permute-start.12 = (bf16[192,1280]{1,0:T(8,128)(2,1)S(1)}, bf16[192,1280]{1,0:T(8,128)(2,1)S(1)}, u32[]{:S(2)}, u32[]{:S(2)}) collective-permute-start(bf16[192,1280]{1,0:T(8,128)(2,1)S(1)} %get-tuple-element.91), channel_id=1, source_target_pairs={{0,8},{8,0},{16,24},{24,16},{1,9},{9,1},{17,25},{25,17},{2,10},{10... | collective-permute-start | bytes 1474568 | tf_op jit(solution)/shard_map/ppermute | solution.py:491
